TPU v7x, 512 devices: a whole 4x8x8 slice. The times are simulated.
512 devices in a mesh: dp: 4 (over x_hi, core), lat: 16 (over y, x_lo), lon: 8 (over z).
Axes of the slice: x: 4 (x_hi: 2, x_lo: 2; x = x_hi * 2 + x_lo), y: 8, z: 8, core: 2. Of those that a mesh axis runs over, the one named last changes fastest.
Arguments:
- state: bfloat16 [4, 32, 1440, 384], P('dp', 'lat', 'lon'), may hold values from -6 to 6
- cotangent: bfloat16 [4, 32, 1440, 384], P('dp', 'lat', 'lon'), may hold values from -6 to 6
- weights: bfloat16 [4, 384, 384], replicated, may hold values from -0.15625 to 0.15625
- lat_off: int32 [32, 16], replicated, may hold values from -2 to 2
- lon_off: int32 [32, 16], replicated, may hold values from -24 to 24
- basis: int32 [32, 16], replicated, may hold values from 0 to 3
- tap_val: float32 [32, 16], replicated, may hold values from -1.5 to 1.5
- tap_count: int32 [32], replicated, may hold values from 2 to 16
Outputs:
- new_state: bfloat16 [4, 32, 1440, 384], P('dp', 'lat', 'lon')
- state_grad: bfloat16 [4, 32, 1440, 384], P('dp', 'lat', 'lon')
- weight_grad: bfloat16 [4, 384, 384], replicated
All inputs are finite; a program needn't handle non-finite values.
Results may differ from a plain program's by a relative error of at most 0.0048.
The roundings to bfloat16 on the way count: a program that leaves them out, or rounds other values in their place, can miss the bound.
Values may be sent and summed in bfloat16 or wider, within the bound.
No kernel may reach another device: no remote copies, remote signals or barrier semaphores. Data moves between devices by JAX's collectives and lax.ppermute only.
A program may use at most 64 MiB of HBM per device.

v0:
```python
import math

import jax
import jax.numpy as jnp
from jax import lax
from jax.sharding import PartitionSpec as P

H = 2
LONREACH = 24


def with_halo(cells, sides, width):
    for axis, dim in sides:
        count = lax.axis_size(axis)
        ends = count - 1
        head = lax.slice_in_dim(cells, 0, width, axis=dim)
        tail = lax.slice_in_dim(cells, cells.shape[dim] - width, cells.shape[dim], axis=dim)
        cells = jnp.concatenate(
            [
                lax.ppermute(tail, axis, [(i, (i + 1) % count) for i in range(ends)]),
                cells,
                lax.ppermute(head, axis, [((i + 1) % count, i) for i in range(ends)]),
            ],
            axis=dim,
        )
    return cells


def to_columns(field):
    return lax.all_to_all(field, "lon", split_axis=3, concat_axis=2, tiled=True)


def to_rows(field):
    return lax.all_to_all(field, "lon", split_axis=2, concat_axis=3, tiled=True)


def band_rim(field):
    return with_halo(field, (("lat", 1),), H)


def wrap_lon(field, reach):
    return jnp.concatenate([field[:, :, -reach:], field, field[:, :, :reach]], axis=2)


def table_rows(tables, row_first, row_total):
    return [lax.dynamic_slice_in_dim(table, row_first, row_total, 0) for table in tables]


def pull_basis(source, tables, row_first, row_count, width, kcount):
    lat_tab, lon_tab, kind_tab, value_tab, count_tab = table_rows(tables, row_first + H, row_count)
    channels = source.shape[2]
    tap_total = lat_tab.shape[1]
    local_ids = jnp.arange(row_count, dtype=jnp.int32)
    tap_ids = jnp.arange(tap_total, dtype=jnp.int32)
    kind_ids = jnp.arange(kcount, dtype=jnp.int32)
    live = tap_ids[None, :] < count_tab[:, None]
    coeff = jnp.where(
        live[None] & (kind_tab[None] == kind_ids[:, None, None]), value_tab[None], 0.0
    )
    rows_src = local_ids[None, :] + H + lat_tab.T
    cols_src = LONREACH + lon_tab.T

    def pull_one_row(row_start, col_start):
        return lax.dynamic_slice(source, (row_start, col_start, 0), (1, width, channels))[0]

    gather_rows = jax.vmap(jax.vmap(pull_one_row))
    total = jnp.zeros((kcount, row_count, width, channels), jnp.float32)
    for first in range(0, tap_total, 4):
        last = min(first + 4, tap_total)
        pieces = gather_rows(rows_src[first:last], cols_src[first:last])
        total = total + jnp.einsum(
            "trjc,krt->krjc",
            pieces,
            coeff[:, :, first:last],
            preferred_element_type=jnp.float32,
            precision=lax.Precision.HIGHEST,
        )
    return total


def push_basis(source, tables, row_first, row_count, width):
    extended = row_count + 2 * H
    lat_tab, lon_tab, kind_tab, value_tab, count_tab = table_rows(tables, row_first, extended)
    channels = source.shape[3]
    source_ids = jnp.arange(extended, dtype=jnp.int32)

    def push_one_row(kind_sel, row_sel, col_sel):
        return lax.dynamic_slice(source, (kind_sel, row_sel, col_sel, 0), (1, 1, width, channels))[
            0, 0
        ]

    def add_tap(tap_index, total):
        lat_step = lax.dynamic_index_in_dim(lat_tab, tap_index, 1, keepdims=False)
        lon_step = lax.dynamic_index_in_dim(lon_tab, tap_index, 1, keepdims=False)
        kind = lax.dynamic_index_in_dim(kind_tab, tap_index, 1, keepdims=False)
        value = lax.dynamic_index_in_dim(value_tab, tap_index, 1, keepdims=False)
        weight = jnp.where(tap_index < count_tab, value, 0.0)
        piece = jax.vmap(push_one_row)(kind, source_ids, LONREACH - lon_step)
        target = source_ids - H + lat_step
        target = jnp.where((target >= 0) & (target < row_count), target, row_count)
        return total.at[target].add(weight[:, None, None] * piece, mode="drop")

    start = jnp.zeros((row_count, width, channels), jnp.float32)
    return lax.fori_loop(0, jnp.max(count_tab), add_tap, start)


def shards(state, cotangent, weights, lat_off, lon_off, basis, tap_val, tap_count):
    field = state[0]
    upstream = cotangent[0]
    row_count = field.shape[0]
    lon_local = field.shape[1]
    kcount = weights.shape[0]
    row_first = lax.axis_index("lat") * row_count
    widths = ((H, H), (0, 0))
    tables = [
        jnp.pad(lat_off, widths),
        jnp.pad(lon_off, widths),
        jnp.pad(basis, widths),
        jnp.pad(tap_val, widths),
        jnp.pad(tap_count, ((H, H),))[:, None],
    ]
    tables[4] = tables[4][:, 0]
    columns = band_rim(to_columns(field[None]))
    source = wrap_lon(columns, LONREACH)[0]
    z_part = pull_basis(source, tables, row_first, row_count, columns.shape[2], kcount)
    z_basis = to_rows(z_part.astype(jnp.bfloat16))
    mixed = jnp.einsum("krjc,kcd->rjd", z_basis, weights, preferred_element_type=jnp.float32)
    activated, gelu_back = jax.vjp(jax.nn.gelu, mixed)
    new_field = (field.astype(jnp.float32) + activated).astype(jnp.bfloat16)
    dmixed = gelu_back(upstream.astype(jnp.float32))[0].astype(jnp.bfloat16)
    local_grad = jnp.einsum("krjc,rjd->kcd", z_basis, dmixed, preferred_element_type=jnp.float32)
    summed = lax.psum(local_grad, ("dp", "lat", "lon"))
    cell_total = (
        lax.axis_size("dp") * lax.axis_size("lat") * row_count * lax.axis_size("lon") * lon_local
    )
    weight_grad = (summed / math.sqrt(cell_total)).astype(jnp.bfloat16)
    dz_basis = jnp.einsum(
        "rjd,kcd->krjc", dmixed, weights, preferred_element_type=jnp.float32
    ).astype(jnp.bfloat16)
    dz_cols = band_rim(to_columns(dz_basis))
    dz_source = wrap_lon(dz_cols, LONREACH)
    adjoint_part = push_basis(dz_source, tables, row_first, row_count, dz_cols.shape[2]).astype(
        jnp.bfloat16
    )
    adjoint = to_rows(adjoint_part[None])[0]
    field_grad = (upstream.astype(jnp.float32) + adjoint.astype(jnp.float32)).astype(jnp.bfloat16)
    return (new_field[None], field_grad[None], weight_grad)


def solution(mesh):
    return jax.shard_map(
        shards,
        mesh=mesh,
        in_specs=(
            P("dp", "lat", "lon", None),
            P("dp", "lat", "lon", None),
            P(),
            P(),
            P(),
            P(),
            P(),
            P(),
        ),
        out_specs=(P("dp", "lat", "lon", None), P("dp", "lat", "lon", None), P()),
        check_vma=False,
    )
```

profile of v0, /device:TPU:56, one launch (start us, length us, event | category | flops | bytes accessed | tf_op | source)
XLA Modules:
  0.0 894.5 jit_solution(9331970586372149648)
XLA Ops:
  58.3 21.3 %while.24 = (s32[]{:T(128)}, bf16[6,1488,48]{2,1,0:T(8,128)(2,1)S(1)}, s32[8,3]{1,0:T(8,128)S(1)}, bf16[8,1,1440,48]{3,2,1,0:T(8,128)(2,1)}, s32[]{:T(128)}) while((s32[]{:T(128)}, bf16[6,1488,48]{2,1,0:T(8,128)(2,1)S(1)}, s32[8,3]{1,0:T(8,128)S(1)}, bf16[8,1,1440,48]{3,2,1,0:T(8,128)(2,1)}, s32[]{:T(128)}) %tuple.182), condition=%wide.while_cond.3, body=%wide.while_body.3.sunk | while | flops 2 | bytes 508021 | solution.py:64
  85.9 21.1 %while.23 = (s32[]{:T(128)}, bf16[6,1488,48]{2,1,0:T(8,128)(2,1)S(1)}, s32[8,3]{1,0:T(8,128)S(1)}, bf16[8,1,1440,48]{3,2,1,0:T(8,128)(2,1)}, s32[]{:T(128)}) while((s32[]{:T(128)}, bf16[6,1488,48]{2,1,0:T(8,128)(2,1)S(1)}, s32[8,3]{1,0:T(8,128)S(1)}, bf16[8,1,1440,48]{3,2,1,0:T(8,128)(2,1)}, s32[]{:T(128)}) %tuple.181), condition=%wide.while_cond.2, body=%wide.while_body.2.sunk | while | flops 2 | bytes 508021 | solution.py:64
  113.3 21.9 %while.22 = (s32[]{:T(128)}, bf16[6,1488,48]{2,1,0:T(8,128)(2,1)S(1)}, s32[8,3]{1,0:T(8,128)S(1)}, bf16[8,1,1440,48]{3,2,1,0:T(8,128)(2,1)}, s32[]{:T(128)}) while((s32[]{:T(128)}, bf16[6,1488,48]{2,1,0:T(8,128)(2,1)S(1)}, s32[8,3]{1,0:T(8,128)S(1)}, bf16[8,1,1440,48]{3,2,1,0:T(8,128)(2,1)}, s32[]{:T(128)}) %tuple.180), condition=%wide.while_cond.1, body=%wide.while_body.1.sunk | while | flops 2 | bytes 508021 | solution.py:64
  141.5 21.9 %while.25 = (s32[]{:T(128)}, bf16[6,1488,48]{2,1,0:T(8,128)(2,1)S(1)}, s32[8,3]{1,0:T(8,128)S(1)}, bf16[8,1,1440,48]{3,2,1,0:T(8,128)(2,1)}, s32[]{:T(128)}) while((s32[]{:T(128)}, bf16[6,1488,48]{2,1,0:T(8,128)(2,1)S(1)}, s32[8,3]{1,0:T(8,128)S(1)}, bf16[8,1,1440,48]{3,2,1,0:T(8,128)(2,1)}, s32[]{:T(128)}) %tuple.179), condition=%wide.while_cond.4, body=%wide.while_body.4.sunk | while | flops 2 | bytes 508021 | solution.py:64
  185.0 32.8 %all_to_all.63 = bf16[8,2,34560]{2,1,0:T(2,128)(2,1)S(1)} all-to-all(bf16[8,2,34560]{2,1,0:T(2,128)(2,1)S(1)} %reshape.246), channel_id=1, replica_groups=mesh['dp'=4,'lat'=16,'lon'=8] {'lon'}, dimensions={0} | all-to-all | bytes 2211840 | tf_op jit(solution)/shard_map/all_to_all | solution.py:34
  233.4 42.5 %all_to_all.64 = bf16[4,2,180,384]{2,0,1,3:T(4,128)(2,1)S(1)} all-to-all(bf16[4,2,180,384]{2,0,1,3:T(4,128)(2,1)S(1)} %copy.164), channel_id=1, replica_groups=mesh['dp'=4,'lat'=16,'lon'=8] {'lon'}, dimensions={3} | all-to-all | bytes 2211840 | tf_op jit(solution)/shard_map/all_to_all | solution.py:30
  308.1 26.7 %collective-permute-done.3 = bf16[4,2,1440,48]{2,3,1,0:T(8,128)(2,1)S(1)} collective-permute-done((bf16[4,2,1440,48]{2,3,1,0:T(8,128)(2,1)S(1)}, bf16[4,2,1440,48]{2,3,1,0:T(8,128)(2,1)S(1)}, u32[]{:S(2)}, u32[]{:S(2)}) %collective-permute-start.3) | collective-permute-done | bytes 1105952 | tf_op jit(solution)/shard_map/ppermute | solution.py:22
  353.3 511.5 %while.27 = (s32[]{:T(128)}, f32[2,1440,48]{1,2,0:T(8,128)S(1)}, s32[]{:T(128)}, s32[6,16]{0,1:T(8,128)}, s32[6]{0:T(128)S(1)}, /*index=5*/f32[6,16]{0,1:T(8,128...) while((s32[]{:T(128)}, f32[2,1440,48]{1,2,0:T(8,128)S(1)}, ...), condition=%wide.region_3.4_spmd.clone.clone, body=%wide.region_1.3_spmd.clone.clone.sunk | while | flops 1244347 | bytes 11290484 | solution.py:104
  356.0 22.1 %while.28 = (s32[]{:T(128)}, bf16[4,6,1488,48]{3,2,1,0:T(8,128)(2,1)}, s32[6,4]{0,1:T(4,128)S(1)}, bf16[6,1,1,1440,48]{4,3,2,1,0:T(8,128)(2,1)S(1)}, s32[]{:T(128)}) while((s32[]{:T(128)}, bf16[4,6,1488,48]{3,2,1,0:T(8,128)(2,1)}, s32[6,4]{0,1:T(4,128)S(1)}, bf16[6,1,1,1440,48]{4,3,2,1,0:T(8,128)(2,1)S(1)}, s32[]{:T(128)}) %tuple.156), condition=%wide.while_cond, body=%wide.while_body.sunk | while | flops 2 | bytes 507025 | solution.py:88
  388.0 22.1 %while.28 = (s32[]{:T(128)}, bf16[4,6,1488,48]{3,2,1,0:T(8,128)(2,1)}, s32[6,4]{0,1:T(4,128)S(1)}, bf16[6,1,1,1440,48]{4,3,2,1,0:T(8,128)(2,1)S(1)}, s32[]{:T(128)}) while((s32[]{:T(128)}, bf16[4,6,1488,48]{3,2,1,0:T(8,128)(2,1)}, s32[6,4]{0,1:T(4,128)S(1)}, bf16[6,1,1,1440,48]{4,3,2,1,0:T(8,128)(2,1)S(1)}, s32[]{:T(128)}) %tuple.156), condition=%wide.while_cond, body=%wide.while_body.sunk | while | flops 2 | bytes 507025 | solution.py:88
  419.9 22.1 %while.28 = (s32[]{:T(128)}, bf16[4,6,1488,48]{3,2,1,0:T(8,128)(2,1)}, s32[6,4]{0,1:T(4,128)S(1)}, bf16[6,1,1,1440,48]{4,3,2,1,0:T(8,128)(2,1)S(1)}, s32[]{:T(128)}) while((s32[]{:T(128)}, bf16[4,6,1488,48]{3,2,1,0:T(8,128)(2,1)}, s32[6,4]{0,1:T(4,128)S(1)}, bf16[6,1,1,1440,48]{4,3,2,1,0:T(8,128)(2,1)S(1)}, s32[]{:T(128)}) %tuple.156), condition=%wide.while_cond, body=%wide.while_body.sunk | while | flops 2 | bytes 507025 | solution.py:88
  451.8 22.1 %while.28 = (s32[]{:T(128)}, bf16[4,6,1488,48]{3,2,1,0:T(8,128)(2,1)}, s32[6,4]{0,1:T(4,128)S(1)}, bf16[6,1,1,1440,48]{4,3,2,1,0:T(8,128)(2,1)S(1)}, s32[]{:T(128)}) while((s32[]{:T(128)}, bf16[4,6,1488,48]{3,2,1,0:T(8,128)(2,1)}, s32[6,4]{0,1:T(4,128)S(1)}, bf16[6,1,1,1440,48]{4,3,2,1,0:T(8,128)(2,1)S(1)}, s32[]{:T(128)}) %tuple.156), condition=%wide.while_cond, body=%wide.while_body.sunk | while | flops 2 | bytes 507025 | solution.py:88
  483.8 22.1 %while.28 = (s32[]{:T(128)}, bf16[4,6,1488,48]{3,2,1,0:T(8,128)(2,1)}, s32[6,4]{0,1:T(4,128)S(1)}, bf16[6,1,1,1440,48]{4,3,2,1,0:T(8,128)(2,1)S(1)}, s32[]{:T(128)}) while((s32[]{:T(128)}, bf16[4,6,1488,48]{3,2,1,0:T(8,128)(2,1)}, s32[6,4]{0,1:T(4,128)S(1)}, bf16[6,1,1,1440,48]{4,3,2,1,0:T(8,128)(2,1)S(1)}, s32[]{:T(128)}) %tuple.156), condition=%wide.while_cond, body=%wide.while_body.sunk | while | flops 2 | bytes 507025 | solution.py:88
  515.7 22.2 %while.28 = (s32[]{:T(128)}, bf16[4,6,1488,48]{3,2,1,0:T(8,128)(2,1)}, s32[6,4]{0,1:T(4,128)S(1)}, bf16[6,1,1,1440,48]{4,3,2,1,0:T(8,128)(2,1)S(1)}, s32[]{:T(128)}) while((s32[]{:T(128)}, bf16[4,6,1488,48]{3,2,1,0:T(8,128)(2,1)}, s32[6,4]{0,1:T(4,128)S(1)}, bf16[6,1,1,1440,48]{4,3,2,1,0:T(8,128)(2,1)S(1)}, s32[]{:T(128)}) %tuple.156), condition=%wide.while_cond, body=%wide.while_body.sunk | while | flops 2 | bytes 507025 | solution.py:88
  547.7 22.2 %while.28 = (s32[]{:T(128)}, bf16[4,6,1488,48]{3,2,1,0:T(8,128)(2,1)}, s32[6,4]{0,1:T(4,128)S(1)}, bf16[6,1,1,1440,48]{4,3,2,1,0:T(8,128)(2,1)S(1)}, s32[]{:T(128)}) while((s32[]{:T(128)}, bf16[4,6,1488,48]{3,2,1,0:T(8,128)(2,1)}, s32[6,4]{0,1:T(4,128)S(1)}, bf16[6,1,1,1440,48]{4,3,2,1,0:T(8,128)(2,1)S(1)}, s32[]{:T(128)}) %tuple.156), condition=%wide.while_cond, body=%wide.while_body.sunk | while | flops 2 | bytes 507025 | solution.py:88
  579.6 22.1 %while.28 = (s32[]{:T(128)}, bf16[4,6,1488,48]{3,2,1,0:T(8,128)(2,1)}, s32[6,4]{0,1:T(4,128)S(1)}, bf16[6,1,1,1440,48]{4,3,2,1,0:T(8,128)(2,1)S(1)}, s32[]{:T(128)}) while((s32[]{:T(128)}, bf16[4,6,1488,48]{3,2,1,0:T(8,128)(2,1)}, s32[6,4]{0,1:T(4,128)S(1)}, bf16[6,1,1,1440,48]{4,3,2,1,0:T(8,128)(2,1)S(1)}, s32[]{:T(128)}) %tuple.156), condition=%wide.while_cond, body=%wide.while_body.sunk | while | flops 2 | bytes 507025 | solution.py:88
  611.5 22.1 %while.28 = (s32[]{:T(128)}, bf16[4,6,1488,48]{3,2,1,0:T(8,128)(2,1)}, s32[6,4]{0,1:T(4,128)S(1)}, bf16[6,1,1,1440,48]{4,3,2,1,0:T(8,128)(2,1)S(1)}, s32[]{:T(128)}) while((s32[]{:T(128)}, bf16[4,6,1488,48]{3,2,1,0:T(8,128)(2,1)}, s32[6,4]{0,1:T(4,128)S(1)}, bf16[6,1,1,1440,48]{4,3,2,1,0:T(8,128)(2,1)S(1)}, s32[]{:T(128)}) %tuple.156), condition=%wide.while_cond, body=%wide.while_body.sunk | while | flops 2 | bytes 507025 | solution.py:88
  643.5 22.1 %while.28 = (s32[]{:T(128)}, bf16[4,6,1488,48]{3,2,1,0:T(8,128)(2,1)}, s32[6,4]{0,1:T(4,128)S(1)}, bf16[6,1,1,1440,48]{4,3,2,1,0:T(8,128)(2,1)S(1)}, s32[]{:T(128)}) while((s32[]{:T(128)}, bf16[4,6,1488,48]{3,2,1,0:T(8,128)(2,1)}, s32[6,4]{0,1:T(4,128)S(1)}, bf16[6,1,1,1440,48]{4,3,2,1,0:T(8,128)(2,1)S(1)}, s32[]{:T(128)}) %tuple.156), condition=%wide.while_cond, body=%wide.while_body.sunk | while | flops 2 | bytes 507025 | solution.py:88
  675.4 22.1 %while.28 = (s32[]{:T(128)}, bf16[4,6,1488,48]{3,2,1,0:T(8,128)(2,1)}, s32[6,4]{0,1:T(4,128)S(1)}, bf16[6,1,1,1440,48]{4,3,2,1,0:T(8,128)(2,1)S(1)}, s32[]{:T(128)}) while((s32[]{:T(128)}, bf16[4,6,1488,48]{3,2,1,0:T(8,128)(2,1)}, s32[6,4]{0,1:T(4,128)S(1)}, bf16[6,1,1,1440,48]{4,3,2,1,0:T(8,128)(2,1)S(1)}, s32[]{:T(128)}) %tuple.156), condition=%wide.while_cond, body=%wide.while_body.sunk | while | flops 2 | bytes 507025 | solution.py:88
  707.3 22.1 %while.28 = (s32[]{:T(128)}, bf16[4,6,1488,48]{3,2,1,0:T(8,128)(2,1)}, s32[6,4]{0,1:T(4,128)S(1)}, bf16[6,1,1,1440,48]{4,3,2,1,0:T(8,128)(2,1)S(1)}, s32[]{:T(128)}) while((s32[]{:T(128)}, bf16[4,6,1488,48]{3,2,1,0:T(8,128)(2,1)}, s32[6,4]{0,1:T(4,128)S(1)}, bf16[6,1,1,1440,48]{4,3,2,1,0:T(8,128)(2,1)S(1)}, s32[]{:T(128)}) %tuple.156), condition=%wide.while_cond, body=%wide.while_body.sunk | while | flops 2 | bytes 507025 | solution.py:88
  739.2 22.1 %while.28 = (s32[]{:T(128)}, bf16[4,6,1488,48]{3,2,1,0:T(8,128)(2,1)}, s32[6,4]{0,1:T(4,128)S(1)}, bf16[6,1,1,1440,48]{4,3,2,1,0:T(8,128)(2,1)S(1)}, s32[]{:T(128)}) while((s32[]{:T(128)}, bf16[4,6,1488,48]{3,2,1,0:T(8,128)(2,1)}, s32[6,4]{0,1:T(4,128)S(1)}, bf16[6,1,1,1440,48]{4,3,2,1,0:T(8,128)(2,1)S(1)}, s32[]{:T(128)}) %tuple.156), condition=%wide.while_cond, body=%wide.while_body.sunk | while | flops 2 | bytes 507025 | solution.py:88
  771.2 22.1 %while.28 = (s32[]{:T(128)}, bf16[4,6,1488,48]{3,2,1,0:T(8,128)(2,1)}, s32[6,4]{0,1:T(4,128)S(1)}, bf16[6,1,1,1440,48]{4,3,2,1,0:T(8,128)(2,1)S(1)}, s32[]{:T(128)}) while((s32[]{:T(128)}, bf16[4,6,1488,48]{3,2,1,0:T(8,128)(2,1)}, s32[6,4]{0,1:T(4,128)S(1)}, bf16[6,1,1,1440,48]{4,3,2,1,0:T(8,128)(2,1)S(1)}, s32[]{:T(128)}) %tuple.156), condition=%wide.while_cond, body=%wide.while_body.sunk | while | flops 2 | bytes 507025 | solution.py:88
  803.1 22.1 %while.28 = (s32[]{:T(128)}, bf16[4,6,1488,48]{3,2,1,0:T(8,128)(2,1)}, s32[6,4]{0,1:T(4,128)S(1)}, bf16[6,1,1,1440,48]{4,3,2,1,0:T(8,128)(2,1)S(1)}, s32[]{:T(128)}) while((s32[]{:T(128)}, bf16[4,6,1488,48]{3,2,1,0:T(8,128)(2,1)}, s32[6,4]{0,1:T(4,128)S(1)}, bf16[6,1,1,1440,48]{4,3,2,1,0:T(8,128)(2,1)S(1)}, s32[]{:T(128)}) %tuple.156), condition=%wide.while_cond, body=%wide.while_body.sunk | while | flops 2 | bytes 507025 | solution.py:88
  835.0 22.1 %while.28 = (s32[]{:T(128)}, bf16[4,6,1488,48]{3,2,1,0:T(8,128)(2,1)}, s32[6,4]{0,1:T(4,128)S(1)}, bf16[6,1,1,1440,48]{4,3,2,1,0:T(8,128)(2,1)S(1)}, s32[]{:T(128)}) while((s32[]{:T(128)}, bf16[4,6,1488,48]{3,2,1,0:T(8,128)(2,1)}, s32[6,4]{0,1:T(4,128)S(1)}, bf16[6,1,1,1440,48]{4,3,2,1,0:T(8,128)(2,1)S(1)}, s32[]{:T(128)}) %tuple.156), condition=%wide.while_cond, body=%wide.while_body.sunk | while | flops 2 | bytes 507025 | solution.py:88
  (669 shorter events, 766.2 us)
Async XLA Ops:
  7.2 219.5 %copy-start = (bf16[4,384,384]{2,1,0:T(8,128)(2,1)S(1)}, bf16[4,384,384]{2,1,0:T(8,128)(2,1)}, u32[]{:S(2)}) copy-start(bf16[4,384,384]{2,1,0:T(8,128)(2,1)} %param.12) | copy-start | bytes 3538948
  7.2 31.2 %copy-start.13 = (f32[32,16]{0,1:T(8,128)S(1)}, f32[32,16]{0,1:T(8,128)}, u32[]{:S(2)}) copy-start(f32[32,16]{0,1:T(8,128)} %param.16) | copy-start | bytes 6148
  9.3 25.0 %all-to-all-start = ((bf16[1,2,180,384]{2,1,0,3:T(2,128)(2,1)}), bf16[1,2,180,384]{2,1,0,3:T(2,128)(2,1)S(1)}, u32[]{:S(2)}, u32[]{:S(2)}) async-start(bf16[1,2,180,384]{2,1,0,3:T(2,128)(2,1)} %copy.133), calls=%async_computation | async-start | bytes 786432 | tf_op jit(solution)/shard_map/all_to_all | solution.py:30
  19.7 853.3 %all-reduce.7.cloned.1.call-start = ((), (), s32[]{:S(2)}) async-start(), calls=%async_computation.4 | async-start | bytes 4718592 | tf_op jit(solution)/shard_map/psum | solution.py:132
  34.9 10.9 %collective-permute-start = (bf16[1,2,1440,48]{2,3,1,0:T(8,128)(2,1)S(1)}, bf16[1,2,1440,48]{2,3,1,0:T(8,128)(2,1)S(1)}, u32[]{:S(2)}, u32[]{:S(2)}) collective-permute-start(bf16[1,2,1440,48]{2,3,1,0:T(8,128)(2,1)S(1)} %all_to_all.49), channel_id=1, source_target_pairs={{0,8},{8,16},{16,24},{24,32},{32,40},{40,48},{48,56},{56,64},{64,7... | collective-permute-start | bytes 829448 | tf_op jit(solution)/shard_map/ppermute | solution.py:20
  39.0 13.0 %collective-permute-start.1 = (bf16[1,2,1440,48]{2,3,1,0:T(8,128)(2,1)S(1)}, bf16[1,2,1440,48]{2,3,1,0:T(8,128)(2,1)S(1)}, u32[]{:S(2)}, u32[]{:S(2)}) collective-permute-start(bf16[1,2,1440,48]{2,3,1,0:T(8,128)(2,1)S(1)} %all_to_all.49), channel_id=1, source_target_pairs={{8,0},{16,8},{24,16},{32,24},{40,32},{48,40},{56,48},{64,56},{72,6... | collective-permute-start | bytes 829448 | tf_op jit(solution)/shard_map/ppermute | solution.py:22
  163.4 3.6 copy-start.5
  166.9 2.0 copy-start.4
  169.0 2.4 copy-start.3
  226.6 1.2 copy-start.6
  226.6 2.0 copy-start.10
  227.8 0.8 copy-start.8
  276.2 4.5 copy-start.12
  276.2 10.0 %copy-start.14 = (s32[32]{0:T(128)S(1)}, s32[32]{0:T(128)}, u32[]{:S(2)}) copy-start(s32[32]{0:T(128)} %param.17) | copy-start | bytes 388
  278.8 29.0 %collective-permute-start.2 = (bf16[4,2,1440,48]{2,3,1,0:T(8,128)(2,1)S(1)}, bf16[4,2,1440,48]{2,3,1,0:T(8,128)(2,1)S(1)}, u32[]{:S(2)}, u32[]{:S(2)}) collective-permute-start(bf16[4,2,1440,48]{2,3,1,0:T(8,128)(2,1)S(1)} %all_to_all.57), channel_id=1, source_target_pairs={{0,8},{8,16},{16,24},{24,32},{32,40},{40,48},{48,56},{56,64},{64,7... | collective-permute-start | bytes 3317768 | tf_op jit(solution)/shard_map/ppermute | solution.py:20
  281.5 53.3 %collective-permute-start.3 = (bf16[4,2,1440,48]{2,3,1,0:T(8,128)(2,1)S(1)}, bf16[4,2,1440,48]{2,3,1,0:T(8,128)(2,1)S(1)}, u32[]{:S(2)}, u32[]{:S(2)}) collective-permute-start(bf16[4,2,1440,48]{2,3,1,0:T(8,128)(2,1)S(1)} %all_to_all.57), channel_id=1, source_target_pairs={{8,0},{16,8},{24,16},{32,24},{40,32},{48,40},{56,48},{64,56},{72,6... | collective-permute-start | bytes 3317768 | tf_op jit(solution)/shard_map/ppermute | solution.py:22
  334.8 1.7 copy-start.2
  864.8 7.0 copy-start.7
  864.8 7.0 copy-start.9
  868.1 16.1 %all-to-all-start.3 = ((bf16[8,2,8640]{2,1,0:T(2,128)(2,1)}), bf16[8,2,8640]{2,1,0:T(2,128)(2,1)S(1)}, u32[]{:S(2)}, u32[]{:S(2)}) async-start(bf16[8,2,8640]{2,1,0:T(2,128)(2,1)} %reshape.248), calls=%async_computation.3 | async-start | bytes 557056 | tf_op jit(solution)/shard_map/all_to_all | solution.py:34
  875.9 10.8 %copy-start.11 = (bf16[1,2,180,384]{3,1,2,0:T(2,128)(2,1)S(1)}, bf16[1,2,180,384]{3,1,2,0:T(2,128)(2,1)}, u32[]{:S(2)}) copy-start(bf16[1,2,180,384]{3,1,2,0:T(2,128)(2,1)} %param.11) | copy-start | bytes 829444
  884.2 3.4 copy-start.1
Sparse Core Ops, SparseCore 0:
  293.4 280.9 all-reduce.6
where the time goes:
time: 905 us; the launch traced here: 895 us
  local copies, waits for them, and re-layouts  574 us (63%)
  other arithmetic  105 us (12%)
  blocking collectives  75.3 us (8%)
  waiting for transfers between devices  69.9 us (8%)
  starting transfers between devices  27.5 us (3%)
  matrix products  16.2 us (2%)
  between operations  14.5 us (2%)
  loops' own time  11.9 us (1%)
    gather x384, local copies, waits for them, and re-layouts  439 us
    mul x16, local copies, waits for them, and re-layouts, add_tap(): return total.at[target].add(weight[:, None, None] * piece, mode='drop')  47.1 us
    all_to_all x1, blocking collectives, to_columns(): return lax.all_to_all(field, 'lon', split_axis=3, concat_axis=2, tiled=True)  42.5 us
    unnamed x49, local copies, waits for them, and re-layouts  40.1 us
    mul x16, other arithmetic, add_tap(): return total.at[target].add(weight[:, None, None] * piece, mode='drop')  40 us
    ppermute x2, waiting for transfers between devices, with_halo(): lax.ppermute(head, axis, [((i + 1) % count, i) for i in range(ends)])  32.9 us
    all_to_all x1, blocking collectives, to_rows(): return lax.all_to_all(field, 'lon', split_axis=2, concat_axis=3, tiled=True)  32.8 us
    scatter-add x16, other arithmetic, add_tap(): return total.at[target].add(weight[:, None, None] * piece, mode='drop')  25.9 us
  transfers between devices with their start and end apart: 7, of which 6 were waited for; matrix products, arithmetic and copies ran while one was open for 60% of the time, Pallas kernels for 0%

commit v1 on v0

v1 whole, which is shorter than its diff:
```python
import functools
import math

import jax
import jax.numpy as jnp
from jax import lax
from jax.experimental import pallas as pl
from jax.experimental.pallas import tpu as pltpu
from jax.sharding import PartitionSpec as P

H = 2
LONREACH = 24
LANES = 128
ROW = 192
EXT = ROW + 2 * LONREACH
SLOPE = math.sqrt(2.0 / math.pi)
CUBIC = 0.044715

SMEM = pl.BlockSpec(memory_space=pltpu.SMEM)
VMEM = pl.BlockSpec(memory_space=pltpu.VMEM)


def plan_kernel(lat_off, lon_off, basis, tap_val, tap_count, f_pos, f_val, f_seg, b_pos, b_val, b_num):
    rows, kcount = f_seg.shape[0] // 8, 4
    taps = lat_off.shape[1]
    total = lat_off.shape[0]
    first = lax.axis_index("lat") * rows
    for i in range(rows):
        row = first + i
        used = tap_count[row]
        slot = jnp.int32(0)
        for k in range(kcount):
            f_seg[i * 8 + k] = slot

            def add(t, slot):
                hit = basis[row, t] == k

                @pl.when(hit)
                def _():
                    f_pos[i * taps + slot] = (i + H + lat_off[row, t]) * EXT + LONREACH + lon_off[row, t]
                    f_val[i * taps + slot] = tap_val[row, t]

                return slot + hit.astype(jnp.int32)

            slot = lax.fori_loop(0, used, add, slot)
        f_seg[i * 8 + kcount] = slot
    room = b_pos.shape[0] // rows
    counts = tuple(jnp.int32(0) for _ in range(rows))
    for e in range(rows + 2 * H):
        row = first + (e - H)
        inside = (row >= 0) & (row < total)
        row = jnp.clip(row, 0, total - 1)
        used = jnp.where(inside, tap_count[row], 0)

        def give(t, counts):
            target = e - H + lat_off[row, t]
            new = []
            for i in range(rows):
                hit = target == i

                @pl.when(hit)
                def _():
                    at = i * room + counts[i]
                    b_pos[at] = (basis[row, t] * (rows + 2 * H) + e) * EXT + LONREACH - lon_off[row, t]
                    b_val[at] = tap_val[row, t]

                new.append(counts[i] + hit.astype(jnp.int32))
            return tuple(new)

        counts = lax.fori_loop(0, used, give, counts)
    for i in range(rows):
        b_num[i] = counts[i]


def plan(tables, rows):
    taps = tables[0].shape[1]
    room = (rows + 2 * H) * taps
    shapes = [
        jax.ShapeDtypeStruct((rows * taps,), jnp.int32),
        jax.ShapeDtypeStruct((rows * taps,), jnp.float32),
        jax.ShapeDtypeStruct((rows * 8,), jnp.int32),
        jax.ShapeDtypeStruct((rows * room,), jnp.int32),
        jax.ShapeDtypeStruct((rows * room,), jnp.float32),
        jax.ShapeDtypeStruct((8,), jnp.int32),
    ]
    return pl.pallas_call(
        plan_kernel,
        out_shape=shapes,
        in_specs=[SMEM] * 5,
        out_specs=[SMEM] * 6,
    )(*tables)


def pieces(own, north, south, west, east, nw, ne, sw, se):
    rows = own.shape[0]
    out = []
    for side, w, mid, e in ((0, nw, north, ne), (rows, west, own, east), (2 * rows, sw, south, se)):
        for r in range(rows):
            out.append((side + r, w, mid, e, r))
    return out


def forward_kernel(f_pos, f_val, f_seg, own, north, south, west, east, nw, ne, sw, se, upstream, weights,
                   new_state, dmixed, d_west, d_east, grad, ext, z, dm):
    rows, width, channels = own.shape
    kcount = weights.shape[0] // channels
    taps = f_pos.shape[0] // rows
    chunks = channels // LANES
    for q, w, mid, e, r in pieces(own, north, south, west, east, nw, ne, sw, se):
        base = q * EXT
        for c in range(chunks):
            lanes = slice(c * LANES, (c + 1) * LANES)
            ext[c, base + LONREACH + width : base + EXT, :] = jnp.zeros((EXT - LONREACH - width, LANES), jnp.float32)
            ext[c, base : base + LONREACH, :] = w[r, :, lanes].astype(jnp.float32)
            ext[c, base + LONREACH : base + LONREACH + width, :] = mid[r, :, lanes].astype(jnp.float32)
            ext[c, base + LONREACH + width : base + 2 * LONREACH + width, :] = e[r, :, lanes].astype(jnp.float32)
    for i in range(rows):
        for k in range(kcount):
            for c in range(chunks):

                def add(n, acc):
                    at = i * taps + n
                    return acc + f_val[at] * ext[c, pl.ds(f_pos[at], ROW), :]

                acc = lax.fori_loop(
                    f_seg[i * 8 + k], f_seg[i * 8 + k + 1], add, jnp.zeros((ROW, LANES), jnp.float32)
                )
                col = k * channels + c * LANES
                z[i * ROW : (i + 1) * ROW, col : col + LANES] = acc.astype(jnp.bfloat16)
    mixed = jnp.dot(z[...], weights[...], preferred_element_type=jnp.float32)
    for i in range(rows):
        x = mixed[i * ROW : i * ROW + width]
        square = x * x
        t = jnp.tanh(SLOPE * (x + CUBIC * (square * x)))
        cdf = 0.5 * (1.0 + t)
        new_state[i] = (own[i].astype(jnp.float32) + x * cdf).astype(jnp.bfloat16)
        slope = cdf + x * (0.5 * (1.0 - t * t)) * (SLOPE * (1.0 + (3.0 * CUBIC) * square))
        d = (upstream[i].astype(jnp.float32) * slope).astype(jnp.bfloat16)
        dmixed[i] = d
        d_west[i] = d[:LONREACH]
        d_east[i] = d[width - LONREACH :]
        dm[i * ROW : (i + 1) * ROW, :] = jnp.concatenate(
            [d, jnp.zeros((ROW - width, channels), jnp.bfloat16)], axis=0
        )
    grad[...] = lax.dot_general(
        z[...], dm[...], (((0,), (0,)), ((), ())), preferred_element_type=jnp.float32
    )


def forward(lists, around, upstream, weights):
    rows, width, channels = upstream.shape
    wide = weights.shape[0]
    block = jax.ShapeDtypeStruct((rows, width, channels), jnp.bfloat16)
    rim = jax.ShapeDtypeStruct((rows, LONREACH, channels), jnp.bfloat16)
    return pl.pallas_call(
        forward_kernel,
        out_shape=[block, block, rim, rim, jax.ShapeDtypeStruct((wide, channels), jnp.float32)],
        in_specs=[SMEM] * 3 + [VMEM] * 11,
        out_specs=[VMEM] * 5,
        scratch_shapes=[
            pltpu.VMEM((channels // LANES, (rows + 2 * H) * EXT, LANES), jnp.float32),
            pltpu.VMEM((rows * ROW, wide), jnp.bfloat16),
            pltpu.VMEM((rows * ROW, channels), jnp.bfloat16),
        ],
        compiler_params=pltpu.CompilerParams(vmem_limit_bytes=40 << 20),
        cost_estimate=pl.CostEstimate(flops=2_000_000_000, bytes_accessed=8_000_000, transcendentals=140_000),
    )(*lists, *around, upstream, weights)


def backward_kernel(b_pos, b_val, b_num, own, north, south, west, east, nw, ne, sw, se, upstream, weights,
                    state_grad, dext, dz):
    rows, width, channels = own.shape
    kcount = weights.shape[0] // channels
    room = b_pos.shape[0] // rows
    chunks = channels // LANES
    high = rows + 2 * H
    for q, w, mid, e, r in pieces(own, north, south, west, east, nw, ne, sw, se):
        base = q * EXT
        line = jnp.concatenate(
            [w[r], mid[r], e[r], jnp.zeros((EXT - 2 * LONREACH - width, channels), jnp.bfloat16)], axis=0
        )
        dext[base : base + EXT, :] = line
    for k in range(kcount):
        part = lax.dot_general(
            dext[...],
            weights[k * channels : (k + 1) * channels, :],
            (((1,), (1,)), ((), ())),
            preferred_element_type=jnp.float32,
        )
        part = part.astype(jnp.bfloat16).astype(jnp.float32)
        for c in range(chunks):
            dz[c, k * high * EXT : (k + 1) * high * EXT, :] = part[:, c * LANES : (c + 1) * LANES]
    for i in range(rows):
        for c in range(chunks):

            def add(n, acc):
                at = i * room + n
                return acc + b_val[at] * dz[c, pl.ds(b_pos[at], ROW), :]

            acc = lax.fori_loop(0, b_num[i], add, jnp.zeros((ROW, LANES), jnp.float32))
            lanes = slice(c * LANES, (c + 1) * LANES)
            adjoint = acc[:width].astype(jnp.bfloat16).astype(jnp.float32)
            state_grad[i, :, lanes] = (upstream[i, :, lanes].astype(jnp.float32) + adjoint).astype(jnp.bfloat16)


def backward(lists, around, upstream, weights):
    rows, width, channels = upstream.shape
    high = rows + 2 * H
    kcount = weights.shape[0] // channels
    return pl.pallas_call(
        backward_kernel,
        out_shape=jax.ShapeDtypeStruct((rows, width, channels), jnp.bfloat16),
        in_specs=[SMEM] * 3 + [VMEM] * 11,
        out_specs=VMEM,
        scratch_shapes=[
            pltpu.VMEM((high * EXT, channels), jnp.bfloat16),
            pltpu.VMEM((channels // LANES, kcount * high * EXT, LANES), jnp.float32),
        ],
        compiler_params=pltpu.CompilerParams(vmem_limit_bytes=40 << 20),
        cost_estimate=pl.CostEstimate(flops=2_500_000_000, bytes_accessed=5_000_000, transcendentals=0),
    )(*lists, *around, upstream, weights)


def around(block, west, east):
    lats, lons = lax.axis_size("lat"), lax.axis_size("lon")
    from_north = [(i, i + 1) for i in range(lats - 1)]
    from_south = [(i + 1, i) for i in range(lats - 1)]
    from_west = [(j, (j + 1) % lons) for j in range(lons)]
    from_east = [((j + 1) % lons, j) for j in range(lons)]

    def corner(lat_pairs, lon_pairs):
        return [(a * lons + c, b * lons + d) for a, b in lat_pairs for c, d in lon_pairs]

    north = lax.ppermute(block, "lat", from_north)
    south = lax.ppermute(block, "lat", from_south)
    w = lax.ppermute(east, "lon", from_west)
    e = lax.ppermute(west, "lon", from_east)
    both = ("lat", "lon")
    nw = lax.ppermute(east, both, corner(from_north, from_west))
    ne = lax.ppermute(west, both, corner(from_north, from_east))
    sw = lax.ppermute(east, both, corner(from_south, from_west))
    se = lax.ppermute(west, both, corner(from_south, from_east))
    return block, north, south, w, e, nw, ne, sw, se


def shards(state, cotangent, weights, lat_off, lon_off, basis, tap_val, tap_count):
    field, upstream = state[0], cotangent[0]
    rows, width, channels = field.shape
    wide = weights.reshape(-1, channels)
    lists = plan((lat_off, lon_off, basis, tap_val, tap_count), rows)
    near = around(field, field[:, :LONREACH], field[:, width - LONREACH :])
    new_field, dmixed, d_west, d_east, local_grad = forward(lists[:3], near, upstream, wide)
    summed = lax.psum(local_grad, ("dp", "lat", "lon"))
    cells = lax.axis_size("dp") * lax.axis_size("lat") * rows * lax.axis_size("lon") * width
    weight_grad = (summed / math.sqrt(cells)).astype(jnp.bfloat16).reshape(weights.shape)
    d_near = around(dmixed, d_west, d_east)
    field_grad = backward(lists[3:], d_near, upstream, wide)
    return new_field[None], field_grad[None], weight_grad


def solution(mesh):
    cells = P("dp", "lat", "lon", None)
    return jax.shard_map(
        shards,
        mesh=mesh,
        in_specs=(cells, cells, P(), P(), P(), P(), P(), P()),
        out_specs=(cells, cells, P()),
        check_vma=False,
    )
```

time: 905 us -> 357 us (0.39)
  the two profiles are of different devices: /device:TPU:56 before, /device:TPU:1 now
where the time goes in v1:
time: 357 us; the launch traced here: 356 us
  waiting for transfers between devices  256 us (72%)
  starting transfers between devices  59.5 us (17%)
  between operations  14.3 us (4%)
  local copies, waits for them, and re-layouts  12.6 us (4%)
  Pallas kernels  11.6 us (3%)
    psum x1, waiting for transfers between devices, shards(): summed = lax.psum(local_grad, ('dp', 'lat', 'lon'))  252 us
    ppermute x2, starting transfers between devices, around(): ne = lax.ppermute(west, both, corner(from_north, from_east))  16.7 us
    unnamed x24, local copies, waits for them, and re-layouts  12.5 us
    ppermute x2, starting transfers between devices, around(): e = lax.ppermute(west, 'lon', from_east)  12.3 us
    ppermute x2, starting transfers between devices, around(): north = lax.ppermute(block, 'lat', from_north)  8.46 us
  transfers between devices with their start and end apart: 17, of which 3 were waited for; matrix products, arithmetic and copies ran while one was open for 2% of the time, Pallas kernels for 2%

profile of v1, /device:TPU:1, one launch (start us, length us, event | category | flops | bytes accessed | tf_op | source)
XLA Modules:
  0.0 356.5 jit_solution(1906372626142635703)
XLA Ops:
  8.2 4.0 %collective-permute-start = (bf16[2,180,384]{2,1,0:T(8,128)(2,1)S(1)}, bf16[2,180,384]{2,1,0:T(8,128)(2,1)S(1)}, u32[]{:S(2)}, u32[]{:S(2)}) collective-permute-start(bf16[2,180,384]{2,1,0:T(8,128)(2,1)S(1)} %bitcast.10), channel_id=1, source_target_pairs={{0,8},{8,16},{16,24},{24,32},{32,40},{40,48},{48,56},{56,64},{64,7... | collective-permute-start | bytes 829448 | tf_op jit(solution)/shard_map/ppermute | solution.py:234
  12.2 1.3 collective-permute-start.1
  13.5 4.0 %collective-permute-start.2 = (bf16[2,24,384]{2,1,0:T(8,128)(2,1)S(1)}, bf16[2,24,384]{2,1,0:T(8,128)(2,1)S(1)}, u32[]{:S(2)}, u32[]{:S(2)}) collective-permute-start(bf16[2,24,384]{2,1,0:T(8,128)(2,1)S(1)} %get-tuple-element.29), channel_id=1, source_target_pairs={{0,1},{1,2},{2,3},{3,4},{4,5},{5,6},{6,7},{7,0},{8,9},{9,10},{10,1... | collective-permute-start | bytes 110600 | tf_op jit(solution)/shard_map/ppermute | solution.py:236
  17.5 8.6 %collective-permute-start.3 = (bf16[2,24,384]{2,1,0:T(8,128)(2,1)S(1)}, bf16[2,24,384]{2,1,0:T(8,128)(2,1)S(1)}, u32[]{:S(2)}, u32[]{:S(2)}) collective-permute-start(bf16[2,24,384]{2,1,0:T(8,128)(2,1)S(1)} %get-tuple-element.28), channel_id=1, source_target_pairs={{1,0},{2,1},{3,2},{4,3},{5,4},{6,5},{7,6},{0,7},{9,8},{10,9},{11,1... | collective-permute-start | bytes 110600 | tf_op jit(solution)/shard_map/ppermute | solution.py:237
  26.1 1.3 collective-permute-start.4
  27.4 8.9 %collective-permute-start.5 = (bf16[2,24,384]{2,1,0:T(8,128)(2,1)S(1)}, bf16[2,24,384]{2,1,0:T(8,128)(2,1)S(1)}, u32[]{:S(2)}, u32[]{:S(2)}) collective-permute-start(bf16[2,24,384]{2,1,0:T(8,128)(2,1)S(1)} %get-tuple-element.28), channel_id=1, source_target_pairs={{1,8},{2,9},{3,10},{4,11},{5,12},{6,13},{7,14},{0,15},{9,16},{10,1... | collective-permute-start | bytes 110600 | tf_op jit(solution)/shard_map/ppermute | solution.py:240
  36.3 1.3 collective-permute-start.6
  37.6 1.3 collective-permute-start.7
  38.9 1.4 copy.11.lat_off
  40.3 1.4 copy.12.lon_off
  41.7 1.4 copy.13.basis
  43.0 1.4 copy.14.tap_val
  45.4 3.2 shard_map.103
  51.9 4.6 %shard_map.104 = (bf16[2,180,384]{2,1,0:T(8,128)(2,1)S(1)}, bf16[2,180,384]{2,1,0:T(8,128)(2,1)S(1)}, bf16[2,24,384]{2,1,0:T(8,128)(2,1)S(1)}, bf16[2,24,384]{2,1,0:T(8,128)(2,1)S(1)}, f32[1536,384]{1,0:T(8,128)}) custom-call(s32[32]{0:T(128)S(1)} %copy-done.5, f32[32]{0:T(128)S(1)} %copy-done.6, s32[16]{0:T(128)S(1)} %copy-done.7, ...), custom_call_target="tpu_custom_call" | custom-call | flops 2000000000 | bytes 8000000 | tf_op jit(solution)/shard_map/pallas_call | solution.py:155
  56.5 4.5 %collective-permute-start.8 = (bf16[2,180,384]{2,1,0:T(8,128)(2,1)S(1)}, bf16[2,180,384]{2,1,0:T(8,128)(2,1)S(1)}, u32[]{:S(2)}, u32[]{:S(2)}) collective-permute-start(bf16[2,180,384]{2,1,0:T(8,128)(2,1)S(1)} %get-tuple-element.21.own), channel_id=1, source_target_pairs={{0,8},{8,16},{16,24},{24,32},{32,40},{40,48},{48,56},{56,64},{64,7... | collective-permute-start | bytes 829448 | tf_op jit(solution)/shard_map/ppermute | solution.py:234
  62.3 3.1 collective-permute-start.10
  65.4 3.8 %collective-permute-start.11 = (bf16[2,24,384]{2,1,0:T(8,128)(2,1)S(1)}, bf16[2,24,384]{2,1,0:T(8,128)(2,1)S(1)}, u32[]{:S(2)}, u32[]{:S(2)}) collective-permute-start(bf16[2,24,384]{2,1,0:T(8,128)(2,1)S(1)} %get-tuple-element.23), channel_id=1, source_target_pairs={{1,0},{2,1},{3,2},{4,3},{5,4},{6,5},{7,6},{0,7},{9,8},{10,9},{11,1... | collective-permute-start | bytes 110600 | tf_op jit(solution)/shard_map/ppermute | solution.py:237
  69.2 5.7 %collective-permute-start.12 = (bf16[2,24,384]{2,1,0:T(8,128)(2,1)S(1)}, bf16[2,24,384]{2,1,0:T(8,128)(2,1)S(1)}, u32[]{:S(2)}, u32[]{:S(2)}) collective-permute-start(bf16[2,24,384]{2,1,0:T(8,128)(2,1)S(1)} %get-tuple-element.22), channel_id=1, source_target_pairs={{0,9},{1,10},{2,11},{3,12},{4,13},{5,14},{6,15},{7,8},{8,17},{9,18... | collective-permute-start | bytes 110600 | tf_op jit(solution)/shard_map/ppermute | solution.py:239
  75.0 7.9 %collective-permute-start.13 = (bf16[2,24,384]{2,1,0:T(8,128)(2,1)S(1)}, bf16[2,24,384]{2,1,0:T(8,128)(2,1)S(1)}, u32[]{:S(2)}, u32[]{:S(2)}) collective-permute-start(bf16[2,24,384]{2,1,0:T(8,128)(2,1)S(1)} %get-tuple-element.23), channel_id=1, source_target_pairs={{1,8},{2,9},{3,10},{4,11},{5,12},{6,13},{7,14},{0,15},{9,16},{10,1... | collective-permute-start | bytes 110600 | tf_op jit(solution)/shard_map/ppermute | solution.py:240
  84.2 1.3 collective-permute-start.15
  86.4 3.6 %collective-permute-done.14.sw = bf16[2,24,384]{2,1,0:T(8,128)(2,1)S(1)} collective-permute-done((bf16[2,24,384]{2,1,0:T(8,128)(2,1)S(1)}, bf16[2,24,384]{2,1,0:T(8,128)(2,1)S(1)}, u32[]{:S(2)}, u32[]{:S(2)}) %collective-permute-start.14) | collective-permute-done | bytes 36896 | tf_op jit(solution)/shard_map/ppermute | solution.py:241
  90.1 3.8 %shard_map.105 = bf16[2,180,384]{2,1,0:T(8,128)(2,1)S(1)} custom-call(s32[192]{0:T(256)S(1)} %copy-done.2, f32[192]{0:T(256)S(1)} %copy-done.3, s32[8]{0:T(128)S(1)} %copy-done.4, bf16[2,180,384]{2,1,0:T(8,128)(2,1)S(1)} %get-tuple-element.21.own, bf16[2,180,384]{2,1,0:T(8,128)(2,1)S(1)} %collective-permute-done.8.north, ...), custom_call_target="tpu_custom_call" | custom-call | flops 2500000000 | bytes 5000000 | tf_op jit(solution)/shard_map/pallas_call | solution.py:210
  94.8 251.9 %all-reduce.2.cloned.1.call-done = f32[1536,384]{1,0:T(8,128)} async-done(((f32[1536,384]{1,0:T(8,128)}), f32[1536,384]{1,0:T(8,128)}) %all-reduce.2.cloned.1.call-update) | async-done | bytes 2359312 | tf_op jit(solution)/shard_map/psum | solution.py:253
  346.7 2.9 multiply_convert_fusion
  (40 shorter events, 9.8 us)
Async XLA Ops:
  7.2 339.6 %all-reduce.2.cloned.1.call-start = ((), (), s32[]{:S(2)}) async-start(), calls=%async_computation | async-start | bytes 4718592 | tf_op jit(solution)/shard_map/psum | solution.py:253
  8.2 40.5 %collective-permute-start = (bf16[2,180,384]{2,1,0:T(8,128)(2,1)S(1)}, bf16[2,180,384]{2,1,0:T(8,128)(2,1)S(1)}, u32[]{:S(2)}, u32[]{:S(2)}) collective-permute-start(bf16[2,180,384]{2,1,0:T(8,128)(2,1)S(1)} %bitcast.10), channel_id=1, source_target_pairs={{0,8},{8,16},{16,24},{24,32},{32,40},{40,48},{48,56},{56,64},{64,7... | collective-permute-start | bytes 829448 | tf_op jit(solution)/shard_map/ppermute | solution.py:234
  12.2 36.5 %collective-permute-start.1 = (bf16[2,180,384]{2,1,0:T(8,128)(2,1)S(1)}, bf16[2,180,384]{2,1,0:T(8,128)(2,1)S(1)}, u32[]{:S(2)}, u32[]{:S(2)}) collective-permute-start(bf16[2,180,384]{2,1,0:T(8,128)(2,1)S(1)} %bitcast.11), channel_id=1, source_target_pairs={{8,0},{16,8},{24,16},{32,24},{40,32},{48,40},{56,48},{64,56},{72,6... | collective-permute-start | bytes 829448 | tf_op jit(solution)/shard_map/ppermute | solution.py:235
  13.5 13.9 %collective-permute-start.2 = (bf16[2,24,384]{2,1,0:T(8,128)(2,1)S(1)}, bf16[2,24,384]{2,1,0:T(8,128)(2,1)S(1)}, u32[]{:S(2)}, u32[]{:S(2)}) collective-permute-start(bf16[2,24,384]{2,1,0:T(8,128)(2,1)S(1)} %get-tuple-element.29), channel_id=1, source_target_pairs={{0,1},{1,2},{2,3},{3,4},{4,5},{5,6},{6,7},{7,0},{8,9},{9,10},{10,1... | collective-permute-start | bytes 110600 | tf_op jit(solution)/shard_map/ppermute | solution.py:236
  17.5 18.8 %collective-permute-start.3 = (bf16[2,24,384]{2,1,0:T(8,128)(2,1)S(1)}, bf16[2,24,384]{2,1,0:T(8,128)(2,1)S(1)}, u32[]{:S(2)}, u32[]{:S(2)}) collective-permute-start(bf16[2,24,384]{2,1,0:T(8,128)(2,1)S(1)} %get-tuple-element.28), channel_id=1, source_target_pairs={{1,0},{2,1},{3,2},{4,3},{5,4},{6,5},{7,6},{0,7},{9,8},{10,9},{11,1... | collective-permute-start | bytes 110600 | tf_op jit(solution)/shard_map/ppermute | solution.py:237
  26.1 11.5 %collective-permute-start.4 = (bf16[2,24,384]{2,1,0:T(8,128)(2,1)S(1)}, bf16[2,24,384]{2,1,0:T(8,128)(2,1)S(1)}, u32[]{:S(2)}, u32[]{:S(2)}) collective-permute-start(bf16[2,24,384]{2,1,0:T(8,128)(2,1)S(1)} %get-tuple-element.29), channel_id=1, source_target_pairs={{0,9},{1,10},{2,11},{3,12},{4,13},{5,14},{6,15},{7,8},{8,17},{9,18... | collective-permute-start | bytes 110600 | tf_op jit(solution)/shard_map/ppermute | solution.py:239
  27.4 21.2 %collective-permute-start.5 = (bf16[2,24,384]{2,1,0:T(8,128)(2,1)S(1)}, bf16[2,24,384]{2,1,0:T(8,128)(2,1)S(1)}, u32[]{:S(2)}, u32[]{:S(2)}) collective-permute-start(bf16[2,24,384]{2,1,0:T(8,128)(2,1)S(1)} %get-tuple-element.28), channel_id=1, source_target_pairs={{1,8},{2,9},{3,10},{4,11},{5,12},{6,13},{7,14},{0,15},{9,16},{10,1... | collective-permute-start | bytes 110600 | tf_op jit(solution)/shard_map/ppermute | solution.py:240
  36.3 12.4 %collective-permute-start.6 = (bf16[2,24,384]{2,1,0:T(8,128)(2,1)S(1)}, bf16[2,24,384]{2,1,0:T(8,128)(2,1)S(1)}, u32[]{:S(2)}, u32[]{:S(2)}) collective-permute-start(bf16[2,24,384]{2,1,0:T(8,128)(2,1)S(1)} %get-tuple-element.29), channel_id=1, source_target_pairs={{8,1},{9,2},{10,3},{11,4},{12,5},{13,6},{14,7},{15,0},{16,9},{17,1... | collective-permute-start | bytes 110600 | tf_op jit(solution)/shard_map/ppermute | solution.py:241
  37.6 11.1 %collective-permute-start.7 = (bf16[2,24,384]{2,1,0:T(8,128)(2,1)S(1)}, bf16[2,24,384]{2,1,0:T(8,128)(2,1)S(1)}, u32[]{:S(2)}, u32[]{:S(2)}) collective-permute-start(bf16[2,24,384]{2,1,0:T(8,128)(2,1)S(1)} %get-tuple-element.28), channel_id=1, source_target_pairs={{9,0},{10,1},{11,2},{12,3},{13,4},{14,5},{15,6},{8,7},{17,8},{18,9... | collective-permute-start | bytes 110600 | tf_op jit(solution)/shard_map/ppermute | solution.py:242
  48.7 1.3 copy-start
  50.0 0.7 copy-start.5
  51.3 0.6 copy-start.7
  56.5 33.6 %copy-start.1 = (bf16[4,384,384]{2,1,0:T(8,128)(2,1)S(1)}, bf16[4,384,384]{2,1,0:T(8,128)(2,1)}, u32[]{:S(2)}) copy-start(bf16[4,384,384]{2,1,0:T(8,128)(2,1)} %param.10) | copy-start | bytes 3538948
  56.5 33.6 %copy-start.2 = (s32[192]{0:T(256)S(1)}, s32[192]{0:T(256)}, u32[]{:S(2)}) copy-start(s32[192]{0:T(256)} %get-tuple-element.18.b_pos) | copy-start | bytes 2308
  56.5 33.6 %copy-start.3 = (f32[192]{0:T(256)S(1)}, f32[192]{0:T(256)}, u32[]{:S(2)}) copy-start(f32[192]{0:T(256)} %get-tuple-element.19.b_val) | copy-start | bytes 2308
  56.5 33.6 %copy-start.4 = (s32[8]{0:T(128)S(1)}, s32[8]{0:T(128)}, u32[]{:S(2)}) copy-start(s32[8]{0:T(128)} %get-tuple-element.20.b_num) | copy-start | bytes 100
  56.5 33.6 %collective-permute-start.8 = (bf16[2,180,384]{2,1,0:T(8,128)(2,1)S(1)}, bf16[2,180,384]{2,1,0:T(8,128)(2,1)S(1)}, u32[]{:S(2)}, u32[]{:S(2)}) collective-permute-start(bf16[2,180,384]{2,1,0:T(8,128)(2,1)S(1)} %get-tuple-element.21.own), channel_id=1, source_target_pairs={{0,8},{8,16},{16,24},{24,32},{32,40},{40,48},{48,56},{56,64},{64,7... | collective-permute-start | bytes 829448 | tf_op jit(solution)/shard_map/ppermute | solution.py:234
  61.0 29.1 %collective-permute-start.9 = (bf16[2,180,384]{2,1,0:T(8,128)(2,1)S(1)}, bf16[2,180,384]{2,1,0:T(8,128)(2,1)S(1)}, u32[]{:S(2)}, u32[]{:S(2)}) collective-permute-start(bf16[2,180,384]{2,1,0:T(8,128)(2,1)S(1)} %get-tuple-element.21.own), channel_id=1, source_target_pairs={{8,0},{16,8},{24,16},{32,24},{40,32},{48,40},{56,48},{64,56},{72,6... | collective-permute-start | bytes 829448 | tf_op jit(solution)/shard_map/ppermute | solution.py:235
  62.3 12.7 %collective-permute-start.10 = (bf16[2,24,384]{2,1,0:T(8,128)(2,1)S(1)}, bf16[2,24,384]{2,1,0:T(8,128)(2,1)S(1)}, u32[]{:S(2)}, u32[]{:S(2)}) collective-permute-start(bf16[2,24,384]{2,1,0:T(8,128)(2,1)S(1)} %get-tuple-element.22), channel_id=1, source_target_pairs={{0,1},{1,2},{2,3},{3,4},{4,5},{5,6},{6,7},{7,0},{8,9},{9,10},{10,1... | collective-permute-start | bytes 110600 | tf_op jit(solution)/shard_map/ppermute | solution.py:236
  65.4 17.4 %collective-permute-start.11 = (bf16[2,24,384]{2,1,0:T(8,128)(2,1)S(1)}, bf16[2,24,384]{2,1,0:T(8,128)(2,1)S(1)}, u32[]{:S(2)}, u32[]{:S(2)}) collective-permute-start(bf16[2,24,384]{2,1,0:T(8,128)(2,1)S(1)} %get-tuple-element.23), channel_id=1, source_target_pairs={{1,0},{2,1},{3,2},{4,3},{5,4},{6,5},{7,6},{0,7},{9,8},{10,9},{11,1... | collective-permute-start | bytes 110600 | tf_op jit(solution)/shard_map/ppermute | solution.py:237
  69.2 14.9 %collective-permute-start.12 = (bf16[2,24,384]{2,1,0:T(8,128)(2,1)S(1)}, bf16[2,24,384]{2,1,0:T(8,128)(2,1)S(1)}, u32[]{:S(2)}, u32[]{:S(2)}) collective-permute-start(bf16[2,24,384]{2,1,0:T(8,128)(2,1)S(1)} %get-tuple-element.22), channel_id=1, source_target_pairs={{0,9},{1,10},{2,11},{3,12},{4,13},{5,14},{6,15},{7,8},{8,17},{9,18... | collective-permute-start | bytes 110600 | tf_op jit(solution)/shard_map/ppermute | solution.py:239
  75.0 11.4 %collective-permute-start.13 = (bf16[2,24,384]{2,1,0:T(8,128)(2,1)S(1)}, bf16[2,24,384]{2,1,0:T(8,128)(2,1)S(1)}, u32[]{:S(2)}, u32[]{:S(2)}) collective-permute-start(bf16[2,24,384]{2,1,0:T(8,128)(2,1)S(1)} %get-tuple-element.23), channel_id=1, source_target_pairs={{1,8},{2,9},{3,10},{4,11},{5,12},{6,13},{7,14},{0,15},{9,16},{10,1... | collective-permute-start | bytes 110600 | tf_op jit(solution)/shard_map/ppermute | solution.py:240
  82.9 7.1 %collective-permute-start.14 = (bf16[2,24,384]{2,1,0:T(8,128)(2,1)S(1)}, bf16[2,24,384]{2,1,0:T(8,128)(2,1)S(1)}, u32[]{:S(2)}, u32[]{:S(2)}) collective-permute-start(bf16[2,24,384]{2,1,0:T(8,128)(2,1)S(1)} %get-tuple-element.22), channel_id=1, source_target_pairs={{8,1},{9,2},{10,3},{11,4},{12,5},{13,6},{14,7},{15,0},{16,9},{17,1... | collective-permute-start | bytes 110600 | tf_op jit(solution)/shard_map/ppermute | solution.py:241
  84.2 5.9 %collective-permute-start.15 = (bf16[2,24,384]{2,1,0:T(8,128)(2,1)S(1)}, bf16[2,24,384]{2,1,0:T(8,128)(2,1)S(1)}, u32[]{:S(2)}, u32[]{:S(2)}) collective-permute-start(bf16[2,24,384]{2,1,0:T(8,128)(2,1)S(1)} %get-tuple-element.23), channel_id=1, source_target_pairs={{9,0},{10,1},{11,2},{12,3},{13,4},{14,5},{15,6},{8,7},{17,8},{18,9... | collective-permute-start | bytes 110600 | tf_op jit(solution)/shard_map/ppermute | solution.py:242
  (1 other events, 0.6 us)
Sparse Core Ops, SparseCore 0:
  56.6 290.0 all-reduce.1

commit v2 on v1

v2 whole, which is shorter than its diff:
```python
import math

import jax
import jax.numpy as jnp
from jax import lax
from jax.experimental import pallas as pl
from jax.experimental.pallas import tpu as pltpu
from jax.sharding import PartitionSpec as P

H = 2
LONREACH = 24
RIM = 2 * LONREACH
LANES = 128
ROW = 192
EXT = ROW + RIM
SLOPE = math.sqrt(2.0 / math.pi)
CUBIC = 0.044715


SMEM = pl.BlockSpec(memory_space=pltpu.SMEM)
VMEM = pl.BlockSpec(memory_space=pltpu.VMEM)
HBM = pl.BlockSpec(memory_space=pltpu.HBM)
BF16, F32 = jnp.bfloat16, jnp.float32


def plan_kernel(lat_off, lon_off, basis, tap_val, tap_count, f_pos, f_val, b_pos, b_val, *, rows, kcount):
    taps, total = lat_off.shape
    high = rows + 2 * H
    first = lax.axis_index("lat") * rows
    for i in range(rows):
        row = first + i
        used = tap_count[row]
        slot = jnp.int32(0)
        for k in range(kcount):
            f_pos[rows * taps + i * 8 + k] = slot

            def add(t, slot):
                hit = basis[t, row] == k

                @pl.when(hit)
                def _():
                    f_pos[i * taps + slot] = (i + H + lat_off[t, row]) * EXT + LONREACH + lon_off[t, row]
                    f_val[i * taps + slot] = tap_val[t, row]

                return slot + hit.astype(jnp.int32)

            slot = lax.fori_loop(0, used, add, slot)
        f_pos[rows * taps + i * 8 + kcount] = slot
    room = high * taps
    counts = tuple(jnp.int32(0) for _ in range(rows))
    for e in range(high):
        row = first + (e - H)
        inside = (row >= 0) & (row < total)
        row = jnp.clip(row, 0, total - 1)
        used = jnp.where(inside, tap_count[row], 0)

        def give(t, counts):
            target = e - H + lat_off[t, row]
            new = []
            for i in range(rows):
                hit = target == i

                @pl.when(hit)
                def _():
                    at = i * room + counts[i]
                    b_pos[at] = (basis[t, row] * high + e) * EXT + LONREACH - lon_off[t, row]
                    b_val[at] = tap_val[t, row]

                new.append(counts[i] + hit.astype(jnp.int32))
            return tuple(new)

        counts = lax.fori_loop(0, used, give, counts)
    for i in range(rows):
        b_pos[rows * room + i] = counts[i]


def plan(tables, rows, kcount):
    taps = tables[0].shape[0]
    room = (rows + 2 * H) * taps

    def body(*refs):
        plan_kernel(*refs, rows=rows, kcount=kcount)

    return pl.pallas_call(
        body,
        out_shape=[
            jax.ShapeDtypeStruct((rows * taps + rows * 8,), jnp.int32),
            jax.ShapeDtypeStruct((rows * taps,), F32),
            jax.ShapeDtypeStruct((rows * room + 8,), jnp.int32),
            jax.ShapeDtypeStruct((rows * room,), F32),
        ],
        in_specs=[SMEM] * 5,
        out_specs=[SMEM] * 4,
    )(*tables)


def forward_kernel(pos_hbm, val_hbm, weights_hbm, own, north, south, east, ne, se, upstream,
                   new_state, dmixed, west_out, rim_out, grad, pos, val, weights, ext, up, z, dm, sems, *, scale):
    rows, width, channels = own.shape
    kcount = weights.shape[0] // channels
    taps = val.shape[0] // rows
    chunks = channels // LANES
    copies = [
        pltpu.make_async_copy(pos_hbm, pos, sems.at[0]),
        pltpu.make_async_copy(val_hbm, val, sems.at[1]),
        pltpu.make_async_copy(weights_hbm, weights, sems.at[2]),
    ]
    for copy in copies:
        copy.start()
    for side, (mid, rim) in enumerate(((north, ne), (own, east), (south, se))):
        for r in range(rows):
            base = (side * rows + r) * EXT
            for c in range(chunks):
                lanes = slice(c * LANES, (c + 1) * LANES)
                ext[c, base : base + width, :] = mid[r, :, lanes].astype(F32)
                ext[c, base + width : base + width + RIM, :] = rim[r, :RIM, lanes].astype(F32)
                ext[c, base + width + RIM : base + EXT, :] = jnp.zeros((EXT - RIM - width, LANES), F32)
    for i in range(rows):
        kept = width - LONREACH
        up[i, :kept] = upstream[i].astype(F32)[LONREACH:]
        up[i, kept:width] = east[i].astype(F32)[RIM:]
    copies[0].wait()
    copies[1].wait()
    for i in range(rows):
        for k in range(kcount):
            for c in range(chunks):

                def add(n, acc):
                    at = i * taps + n
                    return acc + val[at] * ext[c, pl.ds(pos[at], ROW), :]

                begin = pos[rows * taps + i * 8 + k]
                end = pos[rows * taps + i * 8 + k + 1]
                acc = lax.fori_loop(begin, end, add, jnp.zeros((ROW, LANES), F32))
                col = k * channels + c * LANES
                z[i * ROW : (i + 1) * ROW, col : col + LANES] = acc.astype(BF16)
    copies[2].wait()
    mixed = jnp.dot(z[...], weights[...], preferred_element_type=F32)
    for i in range(rows):
        x = mixed[i * ROW : i * ROW + width]
        square = x * x
        t = jnp.tanh(SLOPE * (x + CUBIC * (square * x)))
        cdf = 0.5 * (1.0 + t)
        base = (H + i) * EXT + LONREACH
        field = jnp.concatenate([ext[c, base : base + width, :] for c in range(chunks)], axis=1)
        made = (field + x * cdf).astype(BF16)
        slope = cdf + x * (0.5 * (1.0 - t * t)) * (SLOPE * (1.0 + (3.0 * CUBIC) * square))
        d = (up[i, :width] * slope).astype(BF16)
        new_state[i] = made
        dmixed[i] = d
        rim_out[i] = d[width - RIM :]
        west_out[i, :RIM] = d[width - RIM :]
        west_out[i, RIM:] = made[width - LONREACH :]
        dm[i * ROW : (i + 1) * ROW, :] = jnp.concatenate([d, jnp.zeros((ROW - width, channels), BF16)], axis=0)
    total = lax.dot_general(z[...], dm[...], (((0,), (0,)), ((), ())), preferred_element_type=F32)
    grad[...] = total * scale


def forward(lists, weights, fields, upstream, scale):
    rows, width, channels = upstream.shape
    wide = weights.shape[0]
    block = jax.ShapeDtypeStruct((rows, width, channels), BF16)

    def body(*refs):
        forward_kernel(*refs, scale=scale)

    return pl.pallas_call(
        body,
        out_shape=[
            block,
            block,
            jax.ShapeDtypeStruct((rows, RIM + LONREACH, channels), BF16),
            jax.ShapeDtypeStruct((rows, RIM, channels), BF16),
            jax.ShapeDtypeStruct((wide, channels), F32),
        ],
        in_specs=[HBM] * 3 + [VMEM] * 7,
        out_specs=[VMEM] * 5,
        scratch_shapes=[
            pltpu.SMEM(lists[0].shape, jnp.int32),
            pltpu.SMEM(lists[1].shape, F32),
            pltpu.VMEM(weights.shape, BF16),
            pltpu.VMEM((channels // LANES, (rows + 2 * H) * EXT, LANES), F32),
            pltpu.VMEM((rows, ROW, channels), F32),
            pltpu.VMEM((rows * ROW, wide), BF16),
            pltpu.VMEM((rows * ROW, channels), BF16),
            pltpu.SemaphoreType.DMA((3,)),
        ],
        compiler_params=pltpu.CompilerParams(vmem_limit_bytes=40 << 20),
        cost_estimate=pl.CostEstimate(flops=2_000_000_000, bytes_accessed=8_000_000, transcendentals=140_000),
    )(*lists, weights, *fields, upstream)


def backward_kernel(pos_hbm, val_hbm, weights_hbm, own, north, south, west, nw, sw, made, upstream,
                    new_state, state_grad, pos, val, weights, dext, dz, sems):
    rows, width, channels = own.shape
    kcount = weights.shape[0] // channels
    room = val.shape[0] // rows
    chunks = channels // LANES
    high = rows + 2 * H
    copies = [
        pltpu.make_async_copy(weights_hbm, weights, sems.at[2]),
        pltpu.make_async_copy(pos_hbm, pos, sems.at[0]),
        pltpu.make_async_copy(val_hbm, val, sems.at[1]),
    ]
    for copy in copies:
        copy.start()
    for side, (mid, rim) in enumerate(((north, nw), (own, west), (south, sw))):
        for r in range(rows):
            base = (side * rows + r) * EXT
            dext[base : base + RIM, :] = rim[r, :RIM]
            dext[base + RIM : base + EXT, :] = jnp.concatenate(
                [mid[r], jnp.zeros((EXT - RIM - width, channels), BF16)], axis=0
            )
    for i in range(rows):
        new_state[i] = jnp.concatenate([west[i, RIM:], made[i, : width - LONREACH]], axis=0)
    copies[0].wait()
    for k in range(kcount):
        part = lax.dot_general(
            dext[...],
            weights[k * channels : (k + 1) * channels, :],
            (((1,), (1,)), ((), ())),
            preferred_element_type=F32,
        )
        part = part.astype(BF16).astype(F32)
        for c in range(chunks):
            dz[c, k * high * EXT : (k + 1) * high * EXT, :] = part[:, c * LANES : (c + 1) * LANES]
    copies[1].wait()
    copies[2].wait()
    for i in range(rows):
        for c in range(chunks):

            def add(n, acc):
                at = i * room + n
                return acc + val[at] * dz[c, pl.ds(pos[at], ROW), :]

            acc = lax.fori_loop(0, pos[rows * room + i], add, jnp.zeros((ROW, LANES), F32))
            lanes = slice(c * LANES, (c + 1) * LANES)
            adjoint = acc[:width].astype(BF16).astype(F32)
            state_grad[i, :, lanes] = (upstream[i, :, lanes].astype(F32) + adjoint).astype(BF16)


def backward(lists, weights, fields, made, upstream):
    rows, width, channels = upstream.shape
    high = rows + 2 * H
    kcount = weights.shape[0] // channels
    block = jax.ShapeDtypeStruct((rows, width, channels), BF16)
    return pl.pallas_call(
        backward_kernel,
        out_shape=[block, block],
        in_specs=[HBM] * 3 + [VMEM] * 8,
        out_specs=[VMEM] * 2,
        scratch_shapes=[
            pltpu.SMEM(lists[0].shape, jnp.int32),
            pltpu.SMEM(lists[1].shape, F32),
            pltpu.VMEM(weights.shape, BF16),
            pltpu.VMEM((high * EXT, channels), BF16),
            pltpu.VMEM((channels // LANES, kcount * high * EXT, LANES), F32),
            pltpu.SemaphoreType.DMA((3,)),
        ],
        compiler_params=pltpu.CompilerParams(vmem_limit_bytes=40 << 20),
        cost_estimate=pl.CostEstimate(flops=2_500_000_000, bytes_accessed=5_000_000, transcendentals=0),
    )(*lists, weights, *fields, made, upstream)


def around(block, side, rim, step):
    lats, lons = lax.axis_size("lat"), lax.axis_size("lon")
    from_north = [(i, i + 1) for i in range(lats - 1)]
    from_south = [(i + 1, i) for i in range(lats - 1)]
    along = [(j, (j + step) % lons) for j in range(lons)]

    def corner(lat_pairs):
        return [(a * lons + c, b * lons + d) for a, b in lat_pairs for c, d in along]

    north = lax.ppermute(block, "lat", from_north)
    south = lax.ppermute(block, "lat", from_south)
    level = lax.ppermute(side, "lon", along)
    upper = lax.ppermute(rim, ("lat", "lon"), corner(from_north))
    lower = lax.ppermute(rim, ("lat", "lon"), corner(from_south))
    return block, north, south, level, upper, lower


def shards(state, cotangent, weights, lat_off, lon_off, basis, tap_val, tap_count):
    field, upstream = state[0], cotangent[0]
    rows, width, channels = field.shape
    kcount = weights.shape[0]
    wide = weights.reshape(-1, channels)
    side = jnp.concatenate([field[:, :RIM], upstream[:, :LONREACH]], axis=1)
    fields = around(field, side, field[:, :RIM], -1)
    lists = plan((lat_off.T, lon_off.T, basis.T, tap_val.T, tap_count), rows, kcount)
    cells = lax.axis_size("dp") * lax.axis_size("lat") * rows * lax.axis_size("lon") * width
    made, dmixed, side, rim, share = forward(lists[:2], wide, fields, upstream, 1.0 / math.sqrt(cells))
    fields = around(dmixed, side, rim, 1)
    weight_grad = lax.psum(share, ("dp", "lat", "lon")).astype(BF16).reshape(weights.shape)
    new_field, field_grad = backward(lists[2:], wide, fields, made, upstream)
    return new_field[None], field_grad[None], weight_grad


def solution(mesh):
    cells = P("dp", "lat", "lon", None)
    return jax.shard_map(
        shards,
        mesh=mesh,
        in_specs=(cells, cells, P(), P(), P(), P(), P(), P()),
        out_specs=(cells, cells, P()),
        check_vma=False,
    )
```

time: 357 us -> 183 us (0.51)
  waiting for transfers between devices: 256 us -> 0.03 us
  blocking collectives: 0 us -> 117 us
  starting transfers between devices: 59.5 us -> 38.9 us
  between operations: 14.3 us -> 0.86 us
    psum x1 -> x0, waiting for transfers between devices: 252 us -> none  [shards(): summed = lax.psum(local_grad, ('dp', 'lat', 'lon'))]
    psum x0 -> x1, blocking collectives: none -> 117 us  [shards(): lax.psum(share, ('dp', 'lat', 'lon')).astype(BF16).reshape(weights.shape)]
    ppermute x12 -> x6, starting transfers between devices: 48.4 us -> 26.5 us  [the longest x2 12.8 us: around(): level = lax.ppermute(side, 'lon', along)]
    ppermute x12 -> x6, waiting for transfers between devices: 3.71 us -> 0.02 us  [the longest x2 0.01 us: around(): lower = lax.ppermute(rim, ('lat', 'lon'), corner(from_south))]
    unnamed x24 -> x36, local copies, waits for them, and re-layouts: 12.5 us -> 15.5 us
  transfers between devices with their start and end apart: 17 -> 10, of which waited for: 3 -> 0; matrix products, arithmetic and copies ran while one was open for 2% -> 1% of each run, Pallas kernels for 2% -> 1%
where the time goes in v2:
time: 183 us; the launch traced here: 182 us
  blocking collectives  117 us (64%)
  starting transfers between devices  38.9 us (21%)
  local copies, waits for them, and re-layouts  15.5 us (8%)
  Pallas kernels  10.2 us (6%)
    psum x1, blocking collectives, shards(): lax.psum(share, ('dp', 'lat', 'lon')).astype(BF16).reshape(weights.shape)  117 us
    unnamed x36, local copies, waits for them, and re-layouts  15.5 us
    ppermute x2, starting transfers between devices, around(): level = lax.ppermute(side, 'lon', along)  12.8 us
    ppermute x2, starting transfers between devices, around(): upper = lax.ppermute(rim, ('lat', 'lon'), corner(from_north))  11.1 us
    ppermute x2, starting transfers between devices, around(): north = lax.ppermute(block, 'lat', from_north)  9.79 us
    pallas_call x1, Pallas kernels, backward(): pl.pallas_call(backward_kernel, out_shape=[block, block], in_specs=[HBM]...  4.57 us
  transfers between devices with their start and end apart: 10, of which 0 were waited for; matrix products, arithmetic and copies ran while one was open for 1% of the time, Pallas kernels for 1%

profile of v2, /device:TPU:1, one launch (start us, length us, event | category | flops | bytes accessed | tf_op | source)
XLA Modules:
  0.0 182.3 jit_solution(16438335131155418545)
XLA Ops:
  0.6 1.0 copy.18
  1.6 1.3 collective-permute-start.1
  2.9 4.6 %collective-permute-start = (bf16[2,180,384]{2,1,0:T(8,128)(2,1)S(1)}, bf16[2,180,384]{2,1,0:T(8,128)(2,1)S(1)}, u32[]{:S(2)}, u32[]{:S(2)}) collective-permute-start(bf16[2,180,384]{2,1,0:T(8,128)(2,1)S(1)} %bitcast.15), channel_id=1, source_target_pairs={{0,8},{8,16},{16,24},{24,32},{32,40},{40,48},{48,56},{56,64},{64,7... | collective-permute-start | bytes 829448 | tf_op jit(solution)/shard_map/ppermute | solution.py:274
  7.5 1.0 copy.17
  8.6 10.9 %collective-permute-start.2 = (bf16[2,72,384]{2,1,0:T(8,128)(2,1)S(1)}, bf16[2,72,384]{2,1,0:T(8,128)(2,1)S(1)}, u32[]{:S(2)}, u32[]{:S(2)}) collective-permute-start(bf16[2,72,384]{2,1,0:T(8,128)(2,1)S(1)} %pad_maximum_fusion), channel_id=1, source_target_pairs={{0,7},{1,0},{2,1},{3,2},{4,3},{5,4},{6,5},{7,6},{8,15},{9,8},{10,9... | collective-permute-start | bytes 331784 | tf_op jit(solution)/shard_map/ppermute | solution.py:276
  19.5 1.3 collective-permute-start.4
  20.8 4.6 %collective-permute-start.3 = (bf16[2,48,384]{2,1,0:T(8,128)(2,1)S(1)}, bf16[2,48,384]{2,1,0:T(8,128)(2,1)S(1)}, u32[]{:S(2)}, u32[]{:S(2)}) collective-permute-start(bf16[2,48,384]{2,1,0:T(8,128)(2,1)S(1)} %slice.9), channel_id=1, source_target_pairs={{0,15},{1,8},{2,9},{3,10},{4,11},{5,12},{6,13},{7,14},{8,23},{9,16... | collective-permute-start | bytes 221192 | tf_op jit(solution)/shard_map/ppermute | solution.py:277
  25.4 2.6 %shard_map.103 = (s32[48]{0:T(128)}, f32[32]{0:T(128)}, s32[200]{0:T(256)}, f32[192]{0:T(256)}) custom-call(s32[16,32]{1,0:T(8,128)} %bitcast.26, s32[16,32]{1,0:T(8,128)} %bitcast.27, s32[16,32]{1,0:T(8,128)} %bitcast.28, f32[16,32]{1,0:T(8,128)} %bitcast.29, s32[32]{0:T(128)} %refs_4_.1), custom_call_target="tpu_custom_call" | custom-call | tf_op jit(solution)/shard_map/pallas_call | solution.py:84
  30.6 1.3 copy-done
  31.9 1.0 copy-done.3
  32.9 0.9 copy-done.5
  33.8 0.9 copy-done.7
  36.8 3.0 %shard_map.104 = (bf16[2,180,384]{2,1,0:T(8,128)(2,1)S(1)}, bf16[2,180,384]{2,1,0:T(8,128)(2,1)S(1)}, bf16[2,72,384]{2,1,0:T(8,128)(2,1)}, bf16[2,48,384]{2,1,0:T(8,128)(2,1)}, f32[1536,384]{1,0:T(8,128)S(1)}) custom-call(s32[48]{0:T(128)S(1)} %copy-done.12, f32[32]{0:T(128)S(1)} %copy-done.13, bf16[1536,384]{1,0:T(8,128)(2,1)S(1)} %bitcast.23, ...), custom_call_target="tpu_custom_call" | custom-call | flops 2000000000 | bytes 8000000 | tf_op jit(solution)/shard_map/pallas_call | solution.py:167
  40.6 1.3 collective-permute-start.9
  41.8 6.5 %collective-permute-start.8 = (bf16[2,48,384]{2,1,0:T(8,128)(2,1)}, bf16[2,48,384]{2,1,0:T(8,128)(2,1)}, u32[]{:S(2)}, u32[]{:S(2)}) collective-permute-start(bf16[2,48,384]{2,1,0:T(8,128)(2,1)} %get-tuple-element.20), channel_id=1, source_target_pairs={{0,9},{1,10},{2,11},{3,12},{4,13},{5,14},{6,15},{7,8},{8,17},{9,18... | collective-permute-start | bytes 221192 | tf_op jit(solution)/shard_map/ppermute | solution.py:277
  48.4 1.3 collective-permute-start.6
  49.6 5.2 %collective-permute-start.5 = (bf16[2,180,384]{2,1,0:T(8,128)(2,1)S(1)}, bf16[2,180,384]{2,1,0:T(8,128)(2,1)S(1)}, u32[]{:S(2)}, u32[]{:S(2)}) collective-permute-start(bf16[2,180,384]{2,1,0:T(8,128)(2,1)S(1)} %get-tuple-element.18.own), channel_id=1, source_target_pairs={{0,8},{8,16},{16,24},{24,32},{32,40},{40,48},{48,56},{56,64},{64,7... | collective-permute-start | bytes 829448 | tf_op jit(solution)/shard_map/ppermute | solution.py:274
  54.9 1.9 %collective-permute-start.7 = (bf16[2,72,384]{2,1,0:T(8,128)(2,1)}, bf16[2,72,384]{2,1,0:T(8,128)(2,1)}, u32[]{:S(2)}, u32[]{:S(2)}) collective-permute-start(bf16[2,72,384]{2,1,0:T(8,128)(2,1)} %get-tuple-element.19), channel_id=1, source_target_pairs={{0,1},{1,2},{2,3},{3,4},{4,5},{5,6},{6,7},{7,0},{8,9},{9,10},{10,1... | collective-permute-start | bytes 331784 | tf_op jit(solution)/shard_map/ppermute | solution.py:276
  56.8 116.8 %all-reduce.1 = bf16[1536,384]{1,0:T(8,128)(2,1)} all-reduce(f32[1536,384]{1,0:T(8,128)S(1)} %get-tuple-element.24), channel_id=1, replica_groups=mesh['dp'=4,'lat'=16,'lon'=8] {'dp','lat','lon'}, use_global_device_ids=true, to_apply=%region_0.0 | all-reduce | flops 589824 | bytes 3538944 | tf_op jit(solution)/shard_map/psum | solution.py:293
  173.6 1.3 copy-done.1
  174.9 1.0 copy-done.15
  175.8 4.6 %shard_map.105 = (bf16[2,180,384]{2,1,0:T(8,128)(2,1)S(1)}, bf16[2,180,384]{2,1,0:T(8,128)(2,1)S(1)}) custom-call(s32[200]{0:T(256)S(1)} %copy-done.10, f32[192]{0:T(256)S(1)} %copy-done.11, bf16[1536,384]{1,0:T(8,128)(2,1)S(1)} %bitcast.24, bf16[2,180,384]{2,1,0:T(8,128)(2,1)S(1)} %get-tuple-element.18.own, ...), custom_call_target="tpu_custom_call" | custom-call | flops 2500000000 | bytes 5000000 | tf_op jit(solution)/shard_map/pallas_call | solution.py:247
  180.4 0.9 copy.13
  181.3 0.9 copy.14
  (39 shorter events, 5.5 us)
Async XLA Ops:
  1.6 28.3 %collective-permute-start.1 = (bf16[2,180,384]{2,1,0:T(8,128)(2,1)S(1)}, bf16[2,180,384]{2,1,0:T(8,128)(2,1)S(1)}, u32[]{:S(2)}, u32[]{:S(2)}) collective-permute-start(bf16[2,180,384]{2,1,0:T(8,128)(2,1)S(1)} %bitcast.14), channel_id=1, source_target_pairs={{8,0},{16,8},{24,16},{32,24},{40,32},{48,40},{56,48},{64,56},{72,6... | collective-permute-start | bytes 829448 | tf_op jit(solution)/shard_map/ppermute | solution.py:275
  2.9 27.0 %collective-permute-start = (bf16[2,180,384]{2,1,0:T(8,128)(2,1)S(1)}, bf16[2,180,384]{2,1,0:T(8,128)(2,1)S(1)}, u32[]{:S(2)}, u32[]{:S(2)}) collective-permute-start(bf16[2,180,384]{2,1,0:T(8,128)(2,1)S(1)} %bitcast.15), channel_id=1, source_target_pairs={{0,8},{8,16},{16,24},{24,32},{32,40},{40,48},{48,56},{56,64},{64,7... | collective-permute-start | bytes 829448 | tf_op jit(solution)/shard_map/ppermute | solution.py:274
  8.6 20.7 %collective-permute-start.2 = (bf16[2,72,384]{2,1,0:T(8,128)(2,1)S(1)}, bf16[2,72,384]{2,1,0:T(8,128)(2,1)S(1)}, u32[]{:S(2)}, u32[]{:S(2)}) collective-permute-start(bf16[2,72,384]{2,1,0:T(8,128)(2,1)S(1)} %pad_maximum_fusion), channel_id=1, source_target_pairs={{0,7},{1,0},{2,1},{3,2},{4,3},{5,4},{6,5},{7,6},{8,15},{9,8},{10,9... | collective-permute-start | bytes 331784 | tf_op jit(solution)/shard_map/ppermute | solution.py:276
  19.5 8.5 %collective-permute-start.4 = (bf16[2,48,384]{2,1,0:T(8,128)(2,1)S(1)}, bf16[2,48,384]{2,1,0:T(8,128)(2,1)S(1)}, u32[]{:S(2)}, u32[]{:S(2)}) collective-permute-start(bf16[2,48,384]{2,1,0:T(8,128)(2,1)S(1)} %slice.9), channel_id=1, source_target_pairs={{8,7},{9,0},{10,1},{11,2},{12,3},{13,4},{14,5},{15,6},{16,15},{17,... | collective-permute-start | bytes 221192 | tf_op jit(solution)/shard_map/ppermute | solution.py:278
  20.8 7.9 %collective-permute-start.3 = (bf16[2,48,384]{2,1,0:T(8,128)(2,1)S(1)}, bf16[2,48,384]{2,1,0:T(8,128)(2,1)S(1)}, u32[]{:S(2)}, u32[]{:S(2)}) collective-permute-start(bf16[2,48,384]{2,1,0:T(8,128)(2,1)S(1)} %slice.9), channel_id=1, source_target_pairs={{0,15},{1,8},{2,9},{3,10},{4,11},{5,12},{6,13},{7,14},{8,23},{9,16... | collective-permute-start | bytes 221192 | tf_op jit(solution)/shard_map/ppermute | solution.py:277
  28.6 0.6 copy-start.8
  29.3 0.6 copy-start.4
  29.9 0.7 copy-start.2
  30.6 1.3 copy-start
  31.9 1.0 copy-start.3
  32.9 0.9 copy-start.5
  33.8 0.9 copy-start.7
  34.7 0.9 copy-start.9
  35.5 0.7 copy-start.12
  39.9 0.7 copy-start.14
  40.6 133.0 %collective-permute-start.9 = (bf16[2,48,384]{2,1,0:T(8,128)(2,1)}, bf16[2,48,384]{2,1,0:T(8,128)(2,1)}, u32[]{:S(2)}, u32[]{:S(2)}) collective-permute-start(bf16[2,48,384]{2,1,0:T(8,128)(2,1)} %get-tuple-element.20), channel_id=1, source_target_pairs={{8,1},{9,2},{10,3},{11,4},{12,5},{13,6},{14,7},{15,0},{16,9},{17,1... | collective-permute-start | bytes 221192 | tf_op jit(solution)/shard_map/ppermute | solution.py:278
  41.8 131.7 %collective-permute-start.8 = (bf16[2,48,384]{2,1,0:T(8,128)(2,1)}, bf16[2,48,384]{2,1,0:T(8,128)(2,1)}, u32[]{:S(2)}, u32[]{:S(2)}) collective-permute-start(bf16[2,48,384]{2,1,0:T(8,128)(2,1)} %get-tuple-element.20), channel_id=1, source_target_pairs={{0,9},{1,10},{2,11},{3,12},{4,13},{5,14},{6,15},{7,8},{8,17},{9,18... | collective-permute-start | bytes 221192 | tf_op jit(solution)/shard_map/ppermute | solution.py:277
  48.4 125.2 %collective-permute-start.6 = (bf16[2,180,384]{2,1,0:T(8,128)(2,1)S(1)}, bf16[2,180,384]{2,1,0:T(8,128)(2,1)S(1)}, u32[]{:S(2)}, u32[]{:S(2)}) collective-permute-start(bf16[2,180,384]{2,1,0:T(8,128)(2,1)S(1)} %get-tuple-element.18.own), channel_id=1, source_target_pairs={{8,0},{16,8},{24,16},{32,24},{40,32},{48,40},{56,48},{64,56},{72,6... | collective-permute-start | bytes 829448 | tf_op jit(solution)/shard_map/ppermute | solution.py:275
  49.6 123.9 %collective-permute-start.5 = (bf16[2,180,384]{2,1,0:T(8,128)(2,1)S(1)}, bf16[2,180,384]{2,1,0:T(8,128)(2,1)S(1)}, u32[]{:S(2)}, u32[]{:S(2)}) collective-permute-start(bf16[2,180,384]{2,1,0:T(8,128)(2,1)S(1)} %get-tuple-element.18.own), channel_id=1, source_target_pairs={{0,8},{8,16},{16,24},{24,32},{32,40},{40,48},{48,56},{56,64},{64,7... | collective-permute-start | bytes 829448 | tf_op jit(solution)/shard_map/ppermute | solution.py:274
  54.9 118.7 %collective-permute-start.7 = (bf16[2,72,384]{2,1,0:T(8,128)(2,1)}, bf16[2,72,384]{2,1,0:T(8,128)(2,1)}, u32[]{:S(2)}, u32[]{:S(2)}) collective-permute-start(bf16[2,72,384]{2,1,0:T(8,128)(2,1)} %get-tuple-element.19), channel_id=1, source_target_pairs={{0,1},{1,2},{2,3},{3,4},{4,5},{5,6},{6,7},{7,0},{8,9},{9,10},{10,1... | collective-permute-start | bytes 331784 | tf_op jit(solution)/shard_map/ppermute | solution.py:276
  56.8 116.8 %copy-start.10 = (s32[200]{0:T(256)S(1)}, s32[200]{0:T(256)}, u32[]{:S(2)}) copy-start(s32[200]{0:T(256)} %get-tuple-element.14.pos_hbm) | copy-start | bytes 2404
  56.8 116.8 %copy-start.11 = (f32[192]{0:T(256)S(1)}, f32[192]{0:T(256)}, u32[]{:S(2)}) copy-start(f32[192]{0:T(256)} %get-tuple-element.15.val_hbm) | copy-start | bytes 2308
  173.6 1.3 copy-start.1
  174.9 1.0 copy-start.15
  (2 other events, 1.2 us)

commit v3 on v2

v3 whole, which is shorter than its diff:
```python
import math

import jax
import jax.numpy as jnp
from jax import lax
from jax.experimental import pallas as pl
from jax.experimental.pallas import tpu as pltpu
from jax.sharding import PartitionSpec as P

H = 2
LONREACH = 24
RIM = 2 * LONREACH
LANES = 128
ROW = 192
EXT = ROW + RIM
SLOPE = math.sqrt(2.0 / math.pi)
CUBIC = 0.044715


SMEM = pl.BlockSpec(memory_space=pltpu.SMEM)
VMEM = pl.BlockSpec(memory_space=pltpu.VMEM)
BF16, F32 = jnp.bfloat16, jnp.float32
DP, LAT = ("x_hi", "core"), ("y", "x_lo")
ALONG_X = ("x_hi", "core", "x_lo")


def forward_taps(tables, first, rows, kcount, pos, val):
    lat_off, lon_off, basis, tap_val, tap_count = tables
    taps = lat_off.shape[0]
    room = taps + 1
    for i in range(rows):
        row = first + i
        used = tap_count[row]
        counts = [jnp.int32(0) for _ in range(kcount)]
        for t in range(taps):
            where = (i + H + lat_off[t, row]) * EXT + LONREACH + lon_off[t, row]
            value = tap_val[t, row]
            kind = jnp.where(t < used, basis[t, row], kcount)
            for k in range(kcount):
                at = (i * kcount + k) * room + counts[k]
                pos[at] = where
                val[at] = value
                counts[k] = counts[k] + (kind == k).astype(jnp.int32)
        for k in range(kcount):
            pos[rows * kcount * room + i * kcount + k] = counts[k]


def backward_taps(tables, first, rows, pos, val):
    lat_off, lon_off, basis, tap_val, tap_count = tables
    taps, total = lat_off.shape
    high = rows + 2 * H
    room = high * taps + 1
    counts = [jnp.int32(0) for _ in range(rows)]
    for e in range(high):
        row = first + (e - H)
        inside = (row >= 0) & (row < total)
        row = jnp.clip(row, 0, total - 1)
        used = jnp.where(inside, tap_count[row], 0)
        for t in range(taps):
            where = (basis[t, row] * high + e) * EXT + LONREACH - lon_off[t, row]
            value = tap_val[t, row]
            target = jnp.where(t < used, e - H + lat_off[t, row], -1)
            for i in range(rows):
                at = i * room + counts[i]
                pos[at] = where
                val[at] = value
                counts[i] = counts[i] + (target == i).astype(jnp.int32)
    for i in range(rows):
        pos[rows * room + i] = counts[i]


def forward_kernel(lat_off, lon_off, basis, tap_val, tap_count, weights, own, north, south, east, ne, se, upstream,
                   new_state, dmixed, west_out, rim_out, grad, pos, val, ext, up, z, dm, *, scale):
    rows, width, channels = own.shape
    kcount = weights.shape[0] // channels
    chunks = channels // LANES
    tables = (lat_off, lon_off, basis, tap_val, tap_count)
    room = lat_off.shape[0] + 1
    forward_taps(tables, lax.axis_index(LAT) * rows, rows, kcount, pos, val)
    for side, (mid, rim) in enumerate(((north, ne), (own, east), (south, se))):
        for r in range(rows):
            base = (side * rows + r) * EXT
            for c in range(chunks):
                lanes = slice(c * LANES, (c + 1) * LANES)
                ext[c, base : base + width, :] = mid[r, :, lanes].astype(F32)
                ext[c, base + width : base + width + RIM, :] = rim[r, :RIM, lanes].astype(F32)
                ext[c, base + width + RIM : base + EXT, :] = jnp.zeros((EXT - RIM - width, LANES), F32)
    for i in range(rows):
        kept = width - LONREACH
        up[i, :kept] = upstream[i].astype(F32)[LONREACH:]
        up[i, kept:width] = east[i].astype(F32)[RIM:]
    for i in range(rows):
        for k in range(kcount):
            for c in range(chunks):

                def add(n, acc):
                    at = (i * kcount + k) * room + n
                    return acc + val[at] * ext[c, pl.ds(pos[at], ROW), :]

                count = pos[rows * kcount * room + i * kcount + k]
                acc = lax.fori_loop(0, count, add, jnp.zeros((ROW, LANES), F32))
                col = k * channels + c * LANES
                z[i * ROW : (i + 1) * ROW, col : col + LANES] = acc.astype(BF16)
    mixed = jnp.dot(z[...], weights[...], preferred_element_type=F32)
    for i in range(rows):
        x = mixed[i * ROW : i * ROW + width]
        square = x * x
        t = jnp.tanh(SLOPE * (x + CUBIC * (square * x)))
        cdf = 0.5 * (1.0 + t)
        base = (H + i) * EXT + LONREACH
        field = jnp.concatenate([ext[c, base : base + width, :] for c in range(chunks)], axis=1)
        made = (field + x * cdf).astype(BF16)
        slope = cdf + x * (0.5 * (1.0 - t * t)) * (SLOPE * (1.0 + (3.0 * CUBIC) * square))
        d = (up[i, :width] * slope).astype(BF16)
        new_state[i] = made
        dmixed[i] = d
        rim_out[i] = d[width - RIM :]
        west_out[i, :RIM] = d[width - RIM :]
        west_out[i, RIM:] = made[width - LONREACH :]
        dm[i * ROW : (i + 1) * ROW, :] = jnp.concatenate([d, jnp.zeros((ROW - width, channels), BF16)], axis=0)
    total = lax.dot_general(z[...], dm[...], (((0,), (0,)), ((), ())), preferred_element_type=F32)
    grad[...] = (total * scale).astype(BF16)


def forward(tables, weights, fields, upstream, scale):
    rows, width, channels = upstream.shape
    wide = weights.shape[0]
    lists = rows * (wide // channels) * (tables[0].shape[0] + 1)
    block = jax.ShapeDtypeStruct((rows, width, channels), BF16)

    def body(*refs):
        forward_kernel(*refs, scale=scale)

    return pl.pallas_call(
        body,
        out_shape=[
            block,
            block,
            jax.ShapeDtypeStruct((rows, RIM + LONREACH, channels), BF16),
            jax.ShapeDtypeStruct((rows, RIM, channels), BF16),
            jax.ShapeDtypeStruct((wide, channels), BF16),
        ],
        in_specs=[SMEM] * 5 + [VMEM] * 8,
        out_specs=[VMEM] * 5,
        scratch_shapes=[
            pltpu.SMEM((lists + 64,), jnp.int32),
            pltpu.SMEM((lists,), F32),
            pltpu.VMEM((channels // LANES, (rows + 2 * H) * EXT, LANES), F32),
            pltpu.VMEM((rows, ROW, channels), F32),
            pltpu.VMEM((rows * ROW, wide), BF16),
            pltpu.VMEM((rows * ROW, channels), BF16),
        ],
        compiler_params=pltpu.CompilerParams(vmem_limit_bytes=24 << 20),
        cost_estimate=pl.CostEstimate(flops=2_000_000_000, bytes_accessed=8_000_000, transcendentals=140_000),
    )(*tables, weights, *fields, upstream)


def backward_kernel(lat_off, lon_off, basis, tap_val, tap_count, weights, own, north, south, west, nw, sw, made, upstream,
                    new_state, state_grad, pos, val, dext, dz):
    rows, width, channels = own.shape
    kcount = weights.shape[0] // channels
    chunks = channels // LANES
    high = rows + 2 * H
    tables = (lat_off, lon_off, basis, tap_val, tap_count)
    room = high * lat_off.shape[0] + 1
    backward_taps(tables, lax.axis_index(LAT) * rows, rows, pos, val)
    for side, (mid, rim) in enumerate(((north, nw), (own, west), (south, sw))):
        for r in range(rows):
            base = (side * rows + r) * EXT
            dext[base : base + RIM, :] = rim[r, :RIM]
            dext[base + RIM : base + EXT, :] = jnp.concatenate(
                [mid[r], jnp.zeros((EXT - RIM - width, channels), BF16)], axis=0
            )
    for i in range(rows):
        new_state[i] = jnp.concatenate([west[i, RIM:], made[i, : width - LONREACH]], axis=0)
    for k in range(kcount):
        part = lax.dot_general(
            dext[...],
            weights[k * channels : (k + 1) * channels, :],
            (((1,), (1,)), ((), ())),
            preferred_element_type=F32,
        )
        part = part.astype(BF16).astype(F32)
        for c in range(chunks):
            dz[c, k * high * EXT : (k + 1) * high * EXT, :] = part[:, c * LANES : (c + 1) * LANES]
    for i in range(rows):
        for c in range(chunks):

            def add(n, acc):
                at = i * room + n
                return acc + val[at] * dz[c, pl.ds(pos[at], ROW), :]

            acc = lax.fori_loop(0, pos[rows * room + i], add, jnp.zeros((ROW, LANES), F32))
            lanes = slice(c * LANES, (c + 1) * LANES)
            adjoint = acc[:width].astype(BF16).astype(F32)
            state_grad[i, :, lanes] = (upstream[i, :, lanes].astype(F32) + adjoint).astype(BF16)


def backward(tables, weights, fields, made, upstream):
    rows, width, channels = upstream.shape
    high = rows + 2 * H
    kcount = weights.shape[0] // channels
    lists = rows * (high * tables[0].shape[0] + 1)
    block = jax.ShapeDtypeStruct((rows, width, channels), BF16)
    return pl.pallas_call(
        backward_kernel,
        out_shape=[block, block],
        in_specs=[SMEM] * 5 + [VMEM] * 9,
        out_specs=[VMEM] * 2,
        scratch_shapes=[
            pltpu.SMEM((lists + 8,), jnp.int32),
            pltpu.SMEM((lists,), F32),
            pltpu.VMEM((high * EXT, channels), BF16),
            pltpu.VMEM((channels // LANES, kcount * high * EXT, LANES), F32),
        ],
        compiler_params=pltpu.CompilerParams(vmem_limit_bytes=24 << 20),
        cost_estimate=pl.CostEstimate(flops=2_500_000_000, bytes_accessed=5_000_000, transcendentals=0),
    )(*tables, weights, *fields, made, upstream)


def around(block, side, rim, step):
    lats, lons = lax.axis_size(LAT), lax.axis_size("lon")
    from_north = [(i, i + 1) for i in range(lats - 1)]
    from_south = [(i + 1, i) for i in range(lats - 1)]
    along = [(j, (j + step) % lons) for j in range(lons)]

    def corner(lat_pairs):
        return [(a * lons + c, b * lons + d) for a, b in lat_pairs for c, d in along]

    north = lax.ppermute(block, LAT, from_north)
    south = lax.ppermute(block, LAT, from_south)
    level = lax.ppermute(side, "lon", along)
    upper = lax.ppermute(rim, LAT + ("lon",), corner(from_north))
    lower = lax.ppermute(rim, LAT + ("lon",), corner(from_south))
    return block, north, south, level, upper, lower


def sum_pieces(pieces, out_shape, passed=()):
    def body(*refs):
        part, out = refs[0], refs[1 + len(passed)]
        total = part[0].astype(F32)
        for n in range(1, part.shape[0]):
            total = total + part[n].astype(F32)
        total = total.astype(out.dtype)
        if len(out.shape) == len(total.shape):
            out[...] = total
        else:
            for n in range(out.shape[0]):
                out[n] = total

    anywhere = pl.BlockSpec(memory_space=pl.ANY)
    return pl.pallas_call(
        body,
        out_shape=[out_shape] + [jax.ShapeDtypeStruct(x.shape, x.dtype) for x in passed],
        in_specs=[VMEM] + [anywhere] * len(passed),
        out_specs=[VMEM] + [anywhere] * len(passed),
        input_output_aliases={1 + n: 1 + n for n in range(len(passed))},
        compiler_params=pltpu.CompilerParams(vmem_limit_bytes=8 << 20),
    )(pieces, *passed)


def spread(block, copies, passed=()):
    def body(*refs):
        source, out = refs[0], refs[1 + len(passed)]
        for n in range(copies):
            out[n] = source[...]

    anywhere = pl.BlockSpec(memory_space=pl.ANY)
    return pl.pallas_call(
        body,
        out_shape=[jax.ShapeDtypeStruct((copies, *block.shape), block.dtype)]
        + [jax.ShapeDtypeStruct(x.shape, x.dtype) for x in passed],
        in_specs=[VMEM] + [anywhere] * len(passed),
        out_specs=[VMEM] + [anywhere] * len(passed),
        input_output_aliases={1 + n: 1 + n for n in range(len(passed))},
        compiler_params=pltpu.CompilerParams(vmem_limit_bytes=8 << 20),
    )(block, *passed)


def exchange(pieces, axes):
    return lax.all_to_all(pieces, axes, 0, 0, tiled=True)


def shards(state, cotangent, weights, lat_off, lon_off, basis, tap_val, tap_count):
    field, upstream = state[0], cotangent[0]
    rows, width, channels = field.shape
    kcount = weights.shape[0]
    wide = weights.reshape(-1, channels)
    tables = (lat_off.T, lon_off.T, basis.T, tap_val.T, tap_count)
    side = jnp.concatenate([field[:, :RIM], upstream[:, :LONREACH]], axis=1)
    fields = around(field, side, field[:, :RIM], -1)
    cells = lax.axis_size(DP) * lax.axis_size(LAT) * rows * lax.axis_size("lon") * width
    made, dmixed, side, rim, share = forward(tables, wide, fields, upstream, 1.0 / math.sqrt(cells))
    nx, ny, nz = lax.axis_size(ALONG_X), lax.axis_size("y"), lax.axis_size("lon")
    shape_x = (share.shape[0] // nx, channels)
    shape_y = (shape_x[0] // ny, channels)
    got = exchange(share.reshape(nx, *shape_x), ALONG_X)
    part, dmixed, side, rim = sum_pieces(got, jax.ShapeDtypeStruct(shape_x, F32), (dmixed, side, rim))
    got = exchange(part.reshape(ny, *shape_y), "y")
    fields = around(dmixed, side, rim, 1)
    (part,) = sum_pieces(got, jax.ShapeDtypeStruct((nz, *shape_y), F32))
    got = exchange(part, "lon")
    (part,) = sum_pieces(got, jax.ShapeDtypeStruct((ny, *shape_y), BF16))
    got = exchange(part, "y")
    new_field, field_grad = backward(tables, wide, fields, made, upstream)
    part, new_field, field_grad = spread(got.reshape(shape_x), nx, (new_field, field_grad))
    weight_grad = exchange(part, ALONG_X).reshape(weights.shape)
    return new_field[None], field_grad[None], weight_grad


def solution(mesh):
    dp, lat, lon = (mesh.shape[name] for name in ("dp", "lat", "lon"))
    finer = jax.sharding.Mesh(mesh.devices.reshape(dp // 2, 2, lat // 2, 2, lon), DP + ("y", "x_lo", "lon"))
    cells = P(DP, LAT, "lon", None)
    return jax.shard_map(
        shards,
        mesh=finer,
        in_specs=(cells, cells, P(), P(), P(), P(), P(), P()),
        out_specs=(cells, cells, P()),
        check_vma=False,
    )
```

time: 183 us -> 140 us (0.77)
  blocking collectives: 117 us -> 46.7 us
  waiting for transfers between devices: 0.03 us -> 19 us
  starting transfers between devices: 38.9 us -> 56 us
  local copies, waits for them, and re-layouts: 15.5 us -> 5.92 us
    psum x1 -> x0, blocking collectives: 117 us -> none  [shards(): lax.psum(share, ('dp', 'lat', 'lon')).astype(BF16).reshape(weights.shape)]
    all_to_all x0 -> x2, blocking collectives: none -> 46.7 us  [exchange(): return lax.all_to_all(pieces, axes, 0, 0, tiled=True)]
    all_to_all x0 -> x3, starting transfers between devices: none -> 17.7 us  [exchange(): return lax.all_to_all(pieces, axes, 0, 0, tiled=True)]
    all_to_all x0 -> x3, waiting for transfers between devices: none -> 17.6 us  [exchange(): return lax.all_to_all(pieces, axes, 0, 0, tiled=True)]
    unnamed x36 -> x21, local copies, waits for them, and re-layouts: 15.5 us -> 5.91 us
    ppermute x8, starting transfers between devices: 26.1 us -> 24.2 us  [the longest x2 10.4 us: around(): upper = lax.ppermute(rim, LAT + ('lon',), corner(from_north))]
    pallas_call x2 -> x5, Pallas kernels: 7.15 us -> 6.93 us  [the longest x1 4.24 us: backward(): pl.pallas_call(backward_kernel, out_shape=[block, block], in_specs=[SMEM]...]
  transfers between devices with their start and end apart: 10 -> 13, of which waited for: 0 -> 4; matrix products, arithmetic and copies ran while one was open for 1% -> 2% of each run, Pallas kernels for 1% -> 4%
where the time goes in v3:
time: 140 us; the launch traced here: 139 us
  starting transfers between devices  56 us (40%)
  blocking collectives  46.7 us (33%)
  waiting for transfers between devices  19 us (14%)
  Pallas kernels  10.9 us (8%)
  local copies, waits for them, and re-layouts  5.92 us (4%)
    all_to_all x2, blocking collectives, exchange(): return lax.all_to_all(pieces, axes, 0, 0, tiled=True)  46.7 us
    all_to_all x3, starting transfers between devices, exchange(): return lax.all_to_all(pieces, axes, 0, 0, tiled=True)  17.7 us
    all_to_all x3, waiting for transfers between devices, exchange(): return lax.all_to_all(pieces, axes, 0, 0, tiled=True)  17.6 us
    ppermute x2, starting transfers between devices, around(): level = lax.ppermute(side, 'lon', along)  14.2 us
    ppermute x2, starting transfers between devices, around(): upper = lax.ppermute(rim, LAT + ('lon',), corner(from_north))  10.4 us
    ppermute x2, starting transfers between devices, around(): north = lax.ppermute(block, LAT, from_north)  8.59 us
    unnamed x21, local copies, waits for them, and re-layouts  5.91 us
    pallas_call x1, Pallas kernels, backward(): pl.pallas_call(backward_kernel, out_shape=[block, block], in_specs=[SMEM]...  4.24 us
  transfers between devices with their start and end apart: 13, of which 4 were waited for; matrix products, arithmetic and copies ran while one was open for 2% of the time, Pallas kernels for 4%

profile of v3, /device:TPU:1, one launch (start us, length us, event | category | flops | bytes accessed | tf_op | source)
XLA Modules:
  0.0 139.4 jit_solution(17072001605865181546)
XLA Ops:
  0.7 1.1 copy.23
  1.8 1.3 collective-permute-start.1
  3.1 4.6 %collective-permute-start = (bf16[2,180,384]{2,1,0:T(8,128)(2,1)S(1)}, bf16[2,180,384]{2,1,0:T(8,128)(2,1)S(1)}, u32[]{:S(2)}, u32[]{:S(2)}) collective-permute-start(bf16[2,180,384]{2,1,0:T(8,128)(2,1)S(1)} %bitcast.22), channel_id=1, source_target_pairs={{0,8},{8,16},{16,24},{24,32},{32,40},{40,48},{48,56},{56,64},{64,7... | collective-permute-start | bytes 829448 | tf_op jit(solution)/shard_map/ppermute | solution.py:230
  7.7 1.0 copy.22
  8.7 10.9 %collective-permute-start.2 = (bf16[2,72,384]{2,1,0:T(8,128)(2,1)S(1)}, bf16[2,72,384]{2,1,0:T(8,128)(2,1)S(1)}, u32[]{:S(2)}, u32[]{:S(2)}) collective-permute-start(bf16[2,72,384]{2,1,0:T(8,128)(2,1)S(1)} %pad_maximum_fusion), channel_id=1, source_target_pairs={{0,7},{1,0},{2,1},{3,2},{4,3},{5,4},{6,5},{7,6},{8,15},{9,8},{10,9... | collective-permute-start | bytes 331784 | tf_op jit(solution)/shard_map/ppermute | solution.py:232
  19.6 1.3 collective-permute-start.4
  20.9 4.6 %collective-permute-start.3 = (bf16[2,48,384]{2,1,0:T(8,128)(2,1)S(1)}, bf16[2,48,384]{2,1,0:T(8,128)(2,1)S(1)}, u32[]{:S(2)}, u32[]{:S(2)}) collective-permute-start(bf16[2,48,384]{2,1,0:T(8,128)(2,1)S(1)} %slice.9), channel_id=1, source_target_pairs={{0,15},{1,8},{2,9},{3,10},{4,11},{5,12},{6,13},{7,14},{8,23},{9,16... | collective-permute-start | bytes 221192 | tf_op jit(solution)/shard_map/ppermute | solution.py:233
  25.6 1.3 collective-permute-done.3.refs_10_
  27.0 3.9 %shard_map.103 = (bf16[2,180,384]{2,1,0:T(8,128)(2,1)S(1)}, bf16[2,180,384]{2,1,0:T(8,128)(2,1)S(1)}, bf16[2,72,384]{2,1,0:T(8,128)(2,1)S(1)}, bf16[2,48,384]{2,1,0:T(8,128)(2,1)S(1)}, bf16[1536,384]{1,0:T(8,128)(2,1)S(1)}) custom-call(s32[16,32]{1,0:T(8,128)S(1)} %bitcast.31, s32[16,32]{1,0:T(8,128)S(1)} %bitcast.33, s32[16,32]{1,0:T(8,128)S(1)} %bitcast.35, ...), custom_call_target="tpu_custom_call" | custom-call | flops 2000000000 | bytes 8000000 | tf_op jit(solution)/shard_map/pallas_call | solution.py:134
  31.0 24.4 %all_to_all.25.refs_0_ = bf16[8,192,384]{2,1,0:T(8,128)(2,1)S(1)} all-to-all(bf16[8,192,384]{2,1,0:T(8,128)(2,1)S(1)} %bitcast.17), channel_id=1, replica_groups=mesh['x_hi'=2,'core'=2,'y'=8,'x_lo'=2,'lon'=8] {'x_hi','core','x_lo'}, dimensions={0} | all-to-all | bytes 2359296 | tf_op jit(solution)/shard_map/all_to_all | solution.py:281
  55.5 22.3 %all_to_all.26.refs_0_ = f32[8,24,384]{2,1,0:T(8,128)S(1)} all-to-all(f32[8,24,384]{2,1,0:T(8,128)S(1)} %bitcast.28), channel_id=1, replica_groups=mesh['x_hi'=2,'core'=2,'y'=8,'x_lo'=2,'lon'=8] {'y'}, dimensions={0} | all-to-all | bytes 589824 | tf_op jit(solution)/shard_map/all_to_all | solution.py:281
  78.6 3.4 %all-to-all-start.2 = ((f32[8,24,384]{2,1,0:T(8,128)}), f32[8,24,384]{2,1,0:T(8,128)S(1)}, u32[]{:S(2)}, u32[]{:S(2)}) async-start(f32[8,24,384]{2,1,0:T(8,128)} %shard_map.105), calls=%async_computation.2 | async-start | bytes 589824 | tf_op jit(solution)/shard_map/all_to_all | solution.py:281
  82.0 1.3 collective-permute-start.6
  83.3 4.0 %collective-permute-start.5 = (bf16[2,180,384]{2,1,0:T(8,128)(2,1)S(1)}, bf16[2,180,384]{2,1,0:T(8,128)(2,1)S(1)}, u32[]{:S(2)}, u32[]{:S(2)}) collective-permute-start(bf16[2,180,384]{2,1,0:T(8,128)(2,1)S(1)} %get-tuple-element.22.own), channel_id=1, source_target_pairs={{0,8},{8,16},{16,24},{24,32},{32,40},{40,48},{48,56},{56,64},{64,7... | collective-permute-start | bytes 829448 | tf_op jit(solution)/shard_map/ppermute | solution.py:230
  87.3 3.3 %collective-permute-start.7 = (bf16[2,72,384]{2,1,0:T(8,128)(2,1)S(1)}, bf16[2,72,384]{2,1,0:T(8,128)(2,1)S(1)}, u32[]{:S(2)}, u32[]{:S(2)}) collective-permute-start(bf16[2,72,384]{2,1,0:T(8,128)(2,1)S(1)} %get-tuple-element.23), channel_id=1, source_target_pairs={{0,1},{1,2},{2,3},{3,4},{4,5},{5,6},{6,7},{7,0},{8,9},{9,10},{10,1... | collective-permute-start | bytes 331784 | tf_op jit(solution)/shard_map/ppermute | solution.py:232
  90.6 1.3 collective-permute-start.9
  91.9 5.8 %collective-permute-start.8 = (bf16[2,48,384]{2,1,0:T(8,128)(2,1)S(1)}, bf16[2,48,384]{2,1,0:T(8,128)(2,1)S(1)}, u32[]{:S(2)}, u32[]{:S(2)}) collective-permute-start(bf16[2,48,384]{2,1,0:T(8,128)(2,1)S(1)} %get-tuple-element.24), channel_id=1, source_target_pairs={{0,9},{1,10},{2,11},{3,12},{4,13},{5,14},{6,15},{7,8},{8,17},{9,18... | collective-permute-start | bytes 221192 | tf_op jit(solution)/shard_map/ppermute | solution.py:233
  98.4 4.2 %all-to-all-start.3 = ((bf16[8,24,384]{2,1,0:T(8,128)(2,1)}), bf16[8,24,384]{2,1,0:T(8,128)(2,1)S(1)}, u32[]{:S(2)}, u32[]{:S(2)}) async-start(bf16[8,24,384]{2,1,0:T(8,128)(2,1)} %shard_map.106), calls=%async_computation.3 | async-start | bytes 294912 | tf_op jit(solution)/shard_map/all_to_all | solution.py:281
  103.6 4.2 %shard_map.107 = (bf16[2,180,384]{2,1,0:T(8,128)(2,1)S(1)}, bf16[2,180,384]{2,1,0:T(8,128)(2,1)S(1)}) custom-call(s32[16,32]{1,0:T(8,128)S(1)} %bitcast.32, s32[16,32]{1,0:T(8,128)S(1)} %bitcast.34, s32[16,32]{1,0:T(8,128)S(1)} %bitcast.36, f32[16,32]{1,0:T(8,128)S(1)} %bitcast.38, s32[32]{0:T(128)S(1)} %copy-done.5, bf16[1536,384]{1,0:T(8,128)(2,1)S(1)} %bitcast.30, ...), custom_call_target="tpu_custom_call" | custom-call | flops 2500000000 | bytes 5000000 | tf_op jit(solution)/shard_map/pallas_call | solution.py:205
  107.8 2.8 %all-to-all-done.3 = bf16[8,24,384]{2,1,0:T(8,128)(2,1)S(1)} async-done(((bf16[8,24,384]{2,1,0:T(8,128)(2,1)}), bf16[8,24,384]{2,1,0:T(8,128)(2,1)S(1)}, u32[]{:S(2)}, u32[]{:S(2)}) %all-to-all-start.3) | async-done | bytes 147488 | tf_op jit(solution)/shard_map/all_to_all | solution.py:281
  110.7 1.1 shard_map.108
  111.8 10.0 %all-to-all-start.4 = ((bf16[8,192,384]{2,1,0:T(8,128)(2,1)}), bf16[8,192,384]{2,1,0:T(8,128)(2,1)S(1)}, u32[]{:S(2)}, u32[]{:S(2)}) async-start(bf16[8,192,384]{2,1,0:T(8,128)(2,1)} %get-tuple-element.30), calls=%async_computation.4 | async-start | bytes 2359296 | tf_op jit(solution)/shard_map/all_to_all | solution.py:281
  123.7 14.7 %all-to-all-done.4 = bf16[8,192,384]{2,1,0:T(8,128)(2,1)S(1)} async-done(((bf16[8,192,384]{2,1,0:T(8,128)(2,1)}), bf16[8,192,384]{2,1,0:T(8,128)(2,1)S(1)}, u32[]{:S(2)}, u32[]{:S(2)}) %all-to-all-start.4) | async-done | bytes 1179680 | tf_op jit(solution)/shard_map/all_to_all | solution.py:281
  138.4 1.0 copy.30
  (34 shorter events, 4.5 us)
Async XLA Ops:
  0.6 26.3 %copy-start.5 = (s32[32]{0:T(128)S(1)}, s32[32]{0:T(128)}, u32[]{:S(2)}) copy-start(s32[32]{0:T(128)} %tap_count.1) | copy-start | bytes 388
  0.6 26.3 %copy-start.4 = (f32[32,16]{0,1:T(8,128)S(1)}, f32[32,16]{0,1:T(8,128)}, u32[]{:S(2)}) copy-start(f32[32,16]{0,1:T(8,128)} %param.14) | copy-start | bytes 6148
  0.7 26.3 %copy-start.3 = (s32[32,16]{0,1:T(8,128)S(1)}, s32[32,16]{0,1:T(8,128)}, u32[]{:S(2)}) copy-start(s32[32,16]{0,1:T(8,128)} %param.13) | copy-start | bytes 6148
  0.7 26.3 %copy-start.2 = (s32[32,16]{0,1:T(8,128)S(1)}, s32[32,16]{0,1:T(8,128)}, u32[]{:S(2)}) copy-start(s32[32,16]{0,1:T(8,128)} %param.12) | copy-start | bytes 6148
  0.7 26.3 %copy-start.1 = (s32[32,16]{0,1:T(8,128)S(1)}, s32[32,16]{0,1:T(8,128)}, u32[]{:S(2)}) copy-start(s32[32,16]{0,1:T(8,128)} %param.11) | copy-start | bytes 6148
  0.7 26.3 %copy-start = (bf16[4,384,384]{2,1,0:T(8,128)(2,1)S(1)}, bf16[4,384,384]{2,1,0:T(8,128)(2,1)}, u32[]{:S(2)}) copy-start(bf16[4,384,384]{2,1,0:T(8,128)(2,1)} %param.10) | copy-start | bytes 3538948
  1.8 25.2 %collective-permute-start.1 = (bf16[2,180,384]{2,1,0:T(8,128)(2,1)S(1)}, bf16[2,180,384]{2,1,0:T(8,128)(2,1)S(1)}, u32[]{:S(2)}, u32[]{:S(2)}) collective-permute-start(bf16[2,180,384]{2,1,0:T(8,128)(2,1)S(1)} %bitcast.21), channel_id=1, source_target_pairs={{8,0},{16,8},{24,16},{32,24},{40,32},{48,40},{56,48},{64,56},{72,6... | collective-permute-start | bytes 829448 | tf_op jit(solution)/shard_map/ppermute | solution.py:231
  3.1 23.9 %collective-permute-start = (bf16[2,180,384]{2,1,0:T(8,128)(2,1)S(1)}, bf16[2,180,384]{2,1,0:T(8,128)(2,1)S(1)}, u32[]{:S(2)}, u32[]{:S(2)}) collective-permute-start(bf16[2,180,384]{2,1,0:T(8,128)(2,1)S(1)} %bitcast.22), channel_id=1, source_target_pairs={{0,8},{8,16},{16,24},{24,32},{32,40},{40,48},{48,56},{56,64},{64,7... | collective-permute-start | bytes 829448 | tf_op jit(solution)/shard_map/ppermute | solution.py:230
  8.7 18.2 %collective-permute-start.2 = (bf16[2,72,384]{2,1,0:T(8,128)(2,1)S(1)}, bf16[2,72,384]{2,1,0:T(8,128)(2,1)S(1)}, u32[]{:S(2)}, u32[]{:S(2)}) collective-permute-start(bf16[2,72,384]{2,1,0:T(8,128)(2,1)S(1)} %pad_maximum_fusion), channel_id=1, source_target_pairs={{0,7},{1,0},{2,1},{3,2},{4,3},{5,4},{6,5},{7,6},{8,15},{9,8},{10,9... | collective-permute-start | bytes 331784 | tf_op jit(solution)/shard_map/ppermute | solution.py:232
  19.6 6.0 %collective-permute-start.4 = (bf16[2,48,384]{2,1,0:T(8,128)(2,1)S(1)}, bf16[2,48,384]{2,1,0:T(8,128)(2,1)S(1)}, u32[]{:S(2)}, u32[]{:S(2)}) collective-permute-start(bf16[2,48,384]{2,1,0:T(8,128)(2,1)S(1)} %slice.9), channel_id=1, source_target_pairs={{8,7},{9,0},{10,1},{11,2},{12,3},{13,4},{14,5},{15,6},{16,15},{17,... | collective-permute-start | bytes 221192 | tf_op jit(solution)/shard_map/ppermute | solution.py:234
  20.9 6.0 %collective-permute-start.3 = (bf16[2,48,384]{2,1,0:T(8,128)(2,1)S(1)}, bf16[2,48,384]{2,1,0:T(8,128)(2,1)S(1)}, u32[]{:S(2)}, u32[]{:S(2)}) collective-permute-start(bf16[2,48,384]{2,1,0:T(8,128)(2,1)S(1)} %slice.9), channel_id=1, source_target_pairs={{0,15},{1,8},{2,9},{3,10},{4,11},{5,12},{6,13},{7,14},{8,23},{9,16... | collective-permute-start | bytes 221192 | tf_op jit(solution)/shard_map/ppermute | solution.py:233
  31.0 24.4 %copy-start.6 = (bf16[2,180,384]{2,1,0:T(8,128)(2,1)}, bf16[2,180,384]{2,1,0:T(8,128)(2,1)S(1)}, u32[]{:S(2)}) copy-start(bf16[2,180,384]{2,1,0:T(8,128)(2,1)S(1)} %get-tuple-element.25.made) | copy-start | bytes 829444
  78.6 19.1 %all-to-all-start.2 = ((f32[8,24,384]{2,1,0:T(8,128)}), f32[8,24,384]{2,1,0:T(8,128)S(1)}, u32[]{:S(2)}, u32[]{:S(2)}) async-start(f32[8,24,384]{2,1,0:T(8,128)} %shard_map.105), calls=%async_computation.2 | async-start | bytes 589824 | tf_op jit(solution)/shard_map/all_to_all | solution.py:281
  82.0 20.6 %collective-permute-start.6 = (bf16[2,180,384]{2,1,0:T(8,128)(2,1)S(1)}, bf16[2,180,384]{2,1,0:T(8,128)(2,1)S(1)}, u32[]{:S(2)}, u32[]{:S(2)}) collective-permute-start(bf16[2,180,384]{2,1,0:T(8,128)(2,1)S(1)} %get-tuple-element.22.own), channel_id=1, source_target_pairs={{8,0},{16,8},{24,16},{32,24},{40,32},{48,40},{56,48},{64,56},{72,6... | collective-permute-start | bytes 829448 | tf_op jit(solution)/shard_map/ppermute | solution.py:231
  83.3 19.3 %collective-permute-start.5 = (bf16[2,180,384]{2,1,0:T(8,128)(2,1)S(1)}, bf16[2,180,384]{2,1,0:T(8,128)(2,1)S(1)}, u32[]{:S(2)}, u32[]{:S(2)}) collective-permute-start(bf16[2,180,384]{2,1,0:T(8,128)(2,1)S(1)} %get-tuple-element.22.own), channel_id=1, source_target_pairs={{0,8},{8,16},{16,24},{24,32},{32,40},{40,48},{48,56},{56,64},{64,7... | collective-permute-start | bytes 829448 | tf_op jit(solution)/shard_map/ppermute | solution.py:230
  87.3 15.3 %collective-permute-start.7 = (bf16[2,72,384]{2,1,0:T(8,128)(2,1)S(1)}, bf16[2,72,384]{2,1,0:T(8,128)(2,1)S(1)}, u32[]{:S(2)}, u32[]{:S(2)}) collective-permute-start(bf16[2,72,384]{2,1,0:T(8,128)(2,1)S(1)} %get-tuple-element.23), channel_id=1, source_target_pairs={{0,1},{1,2},{2,3},{3,4},{4,5},{5,6},{6,7},{7,0},{8,9},{9,10},{10,1... | collective-permute-start | bytes 331784 | tf_op jit(solution)/shard_map/ppermute | solution.py:232
  90.6 12.0 %collective-permute-start.9 = (bf16[2,48,384]{2,1,0:T(8,128)(2,1)S(1)}, bf16[2,48,384]{2,1,0:T(8,128)(2,1)S(1)}, u32[]{:S(2)}, u32[]{:S(2)}) collective-permute-start(bf16[2,48,384]{2,1,0:T(8,128)(2,1)S(1)} %get-tuple-element.24), channel_id=1, source_target_pairs={{8,1},{9,2},{10,3},{11,4},{12,5},{13,6},{14,7},{15,0},{16,9},{17,1... | collective-permute-start | bytes 221192 | tf_op jit(solution)/shard_map/ppermute | solution.py:234
  91.9 10.7 %collective-permute-start.8 = (bf16[2,48,384]{2,1,0:T(8,128)(2,1)S(1)}, bf16[2,48,384]{2,1,0:T(8,128)(2,1)S(1)}, u32[]{:S(2)}, u32[]{:S(2)}) collective-permute-start(bf16[2,48,384]{2,1,0:T(8,128)(2,1)S(1)} %get-tuple-element.24), channel_id=1, source_target_pairs={{0,9},{1,10},{2,11},{3,12},{4,13},{5,14},{6,15},{7,8},{8,17},{9,18... | collective-permute-start | bytes 221192 | tf_op jit(solution)/shard_map/ppermute | solution.py:233
  98.4 12.3 %all-to-all-start.3 = ((bf16[8,24,384]{2,1,0:T(8,128)(2,1)}), bf16[8,24,384]{2,1,0:T(8,128)(2,1)S(1)}, u32[]{:S(2)}, u32[]{:S(2)}) async-start(bf16[8,24,384]{2,1,0:T(8,128)(2,1)} %shard_map.106), calls=%async_computation.3 | async-start | bytes 294912 | tf_op jit(solution)/shard_map/all_to_all | solution.py:281
  102.6 1.0 copy-start.7
  111.8 26.6 %all-to-all-start.4 = ((bf16[8,192,384]{2,1,0:T(8,128)(2,1)}), bf16[8,192,384]{2,1,0:T(8,128)(2,1)S(1)}, u32[]{:S(2)}, u32[]{:S(2)}) async-start(bf16[8,192,384]{2,1,0:T(8,128)(2,1)} %get-tuple-element.30), calls=%async_computation.4 | async-start | bytes 2359296 | tf_op jit(solution)/shard_map/all_to_all | solution.py:281

commit v4 on v3

--- a/solution.py
+++ b/solution.py
@@ -119,10 +119,12 @@
         west_out[i, RIM:] = made[width - LONREACH :]
         dm[i * ROW : (i + 1) * ROW, :] = jnp.concatenate([d, jnp.zeros((ROW - width, channels), BF16)], axis=0)
     total = lax.dot_general(z[...], dm[...], (((0,), (0,)), ((), ())), preferred_element_type=F32)
-    grad[...] = (total * scale).astype(BF16)
-
-
-def forward(tables, weights, fields, upstream, scale):
+    total = (total * scale).astype(BF16)
+    for n in range(grad.shape[0]):
+        grad[n] = total[n * grad.shape[1] : (n + 1) * grad.shape[1]]
+
+
+def forward(tables, weights, fields, upstream, scale, shares):
     rows, width, channels = upstream.shape
     wide = weights.shape[0]
     lists = rows * (wide // channels) * (tables[0].shape[0] + 1)
@@ -138,7 +140,7 @@
             block,
             jax.ShapeDtypeStruct((rows, RIM + LONREACH, channels), BF16),
             jax.ShapeDtypeStruct((rows, RIM, channels), BF16),
-            jax.ShapeDtypeStruct((wide, channels), BF16),
+            jax.ShapeDtypeStruct((shares, wide // shares, channels), BF16),
         ],
         in_specs=[SMEM] * 5 + [VMEM] * 8,
         out_specs=[VMEM] * 5,
@@ -242,11 +244,9 @@
         for n in range(1, part.shape[0]):
             total = total + part[n].astype(F32)
         total = total.astype(out.dtype)
-        if len(out.shape) == len(total.shape):
-            out[...] = total
-        else:
-            for n in range(out.shape[0]):
-                out[n] = total
+        rows = out.shape[1]
+        for n in range(out.shape[0]):
+            out[n] = total if rows == total.shape[0] else total[n * rows : (n + 1) * rows]
 
     anywhere = pl.BlockSpec(memory_space=pl.ANY)
     return pl.pallas_call(
@@ -290,20 +290,20 @@
     side = jnp.concatenate([field[:, :RIM], upstream[:, :LONREACH]], axis=1)
     fields = around(field, side, field[:, :RIM], -1)
     cells = lax.axis_size(DP) * lax.axis_size(LAT) * rows * lax.axis_size("lon") * width
-    made, dmixed, side, rim, share = forward(tables, wide, fields, upstream, 1.0 / math.sqrt(cells))
     nx, ny, nz = lax.axis_size(ALONG_X), lax.axis_size("y"), lax.axis_size("lon")
-    shape_x = (share.shape[0] // nx, channels)
-    shape_y = (shape_x[0] // ny, channels)
-    got = exchange(share.reshape(nx, *shape_x), ALONG_X)
-    part, dmixed, side, rim = sum_pieces(got, jax.ShapeDtypeStruct(shape_x, F32), (dmixed, side, rim))
-    got = exchange(part.reshape(ny, *shape_y), "y")
+    made, dmixed, side, rim, share = forward(tables, wide, fields, upstream, 1.0 / math.sqrt(cells), nx)
+    piece = (wide.shape[0] // (nx * ny), channels)
+    got = exchange(share, ALONG_X)
     fields = around(dmixed, side, rim, 1)
-    (part,) = sum_pieces(got, jax.ShapeDtypeStruct((nz, *shape_y), F32))
+    part, *near = sum_pieces(got, jax.ShapeDtypeStruct((ny, *piece), F32), fields[1:])
+    fields = (dmixed, *near)
+    got = exchange(part, "y")
+    (part,) = sum_pieces(got, jax.ShapeDtypeStruct((nz, *piece), F32))
     got = exchange(part, "lon")
-    (part,) = sum_pieces(got, jax.ShapeDtypeStruct((ny, *shape_y), BF16))
+    (part,) = sum_pieces(got, jax.ShapeDtypeStruct((ny, *piece), BF16))
     got = exchange(part, "y")
     new_field, field_grad = backward(tables, wide, fields, made, upstream)
-    part, new_field, field_grad = spread(got.reshape(shape_x), nx, (new_field, field_grad))
+    part, new_field, field_grad = spread(got.reshape(-1, channels), nx, (new_field, field_grad))
     weight_grad = exchange(part, ALONG_X).reshape(weights.shape)
     return new_field[None], field_grad[None], weight_grad
 

time: 140 us -> 147 us (1.050)
  waiting for transfers between devices: 19 us -> 33.2 us
  blocking collectives: 46.7 us -> 36.6 us
  starting transfers between devices: 56 us -> 58.9 us
    all_to_all x2, blocking collectives: 46.7 us -> 36.6 us  [exchange(): return lax.all_to_all(pieces, axes, 0, 0, tiled=True)]
    ppermute x2, waiting for transfers between devices: 0.01 us -> 5.92 us  [around(): north = lax.ppermute(block, LAT, from_north)]
    ppermute x2, waiting for transfers between devices: 0.01 us -> 4.91 us  [around(): south = lax.ppermute(block, LAT, from_south)]
    all_to_all x3, starting transfers between devices: 17.7 us -> 20.8 us  [exchange(): return lax.all_to_all(pieces, axes, 0, 0, tiled=True)]
    ppermute x2, waiting for transfers between devices: 0.07 us -> 2.42 us  [around(): lower = lax.ppermute(rim, LAT + ('lon',), corner(from_south))]
    unnamed x21 -> x27, local copies, waits for them, and re-layouts: 5.91 us -> 5.69 us
  transfers between devices with their start and end apart: 13 -> 13, of which waited for: 4 -> 7; matrix products, arithmetic and copies ran while one was open for 2% -> 2% of each run, Pallas kernels for 4% -> 3%
where the time goes in v4:
time: 147 us
  starting transfers between devices  58.9 us (40%)
  blocking collectives  36.6 us (25%)
  waiting for transfers between devices  33.2 us (23%)
  Pallas kernels  11.1 us (8%)
  local copies, waits for them, and re-layouts  5.71 us (4%)
    all_to_all x2, blocking collectives, exchange(): return lax.all_to_all(pieces, axes, 0, 0, tiled=True)  36.6 us
    all_to_all x3, starting transfers between devices, exchange(): return lax.all_to_all(pieces, axes, 0, 0, tiled=True)  20.8 us
    all_to_all x3, waiting for transfers between devices, exchange(): return lax.all_to_all(pieces, axes, 0, 0, tiled=True)  18.7 us
    ppermute x2, starting transfers between devices, around(): level = lax.ppermute(side, 'lon', along)  13.9 us
    ppermute x2, starting transfers between devices, around(): upper = lax.ppermute(rim, LAT + ('lon',), corner(from_north))  10.4 us
    ppermute x2, starting transfers between devices, around(): north = lax.ppermute(block, LAT, from_north)  8.59 us
    ppermute x2, waiting for transfers between devices, around(): north = lax.ppermute(block, LAT, from_north)  5.92 us
    unnamed x27, local copies, waits for them, and re-layouts  5.69 us
  transfers between devices with their start and end apart: 13, of which 7 were waited for; matrix products, arithmetic and copies ran while one was open for 2% of the time, Pallas kernels for 3%

profile of v4, /device:TPU:1, one launch (start us, length us, event | category | flops | bytes accessed | tf_op | source)
XLA Modules:
  0.0 146.5 jit_solution(18287680159474118155)
XLA Ops:
  1.8 1.3 collective-permute-start.1
  3.1 4.6 %collective-permute-start = (bf16[2,180,384]{2,1,0:T(8,128)(2,1)S(1)}, bf16[2,180,384]{2,1,0:T(8,128)(2,1)S(1)}, u32[]{:S(2)}, u32[]{:S(2)}) collective-permute-start(bf16[2,180,384]{2,1,0:T(8,128)(2,1)S(1)} %bitcast.19), channel_id=1, source_target_pairs={{0,8},{8,16},{16,24},{24,32},{32,40},{40,48},{48,56},{56,64},{64,7... | collective-permute-start | bytes 829448 | tf_op jit(solution)/shard_map/ppermute | solution.py:232
  8.7 10.9 %collective-permute-start.2 = (bf16[2,72,384]{2,1,0:T(8,128)(2,1)S(1)}, bf16[2,72,384]{2,1,0:T(8,128)(2,1)S(1)}, u32[]{:S(2)}, u32[]{:S(2)}) collective-permute-start(bf16[2,72,384]{2,1,0:T(8,128)(2,1)S(1)} %pad_maximum_fusion), channel_id=1, source_target_pairs={{0,7},{1,0},{2,1},{3,2},{4,3},{5,4},{6,5},{7,6},{8,15},{9,8},{10,9... | collective-permute-start | bytes 331784 | tf_op jit(solution)/shard_map/ppermute | solution.py:234
  19.6 1.3 collective-permute-start.4
  20.9 4.6 %collective-permute-start.3 = (bf16[2,48,384]{2,1,0:T(8,128)(2,1)S(1)}, bf16[2,48,384]{2,1,0:T(8,128)(2,1)S(1)}, u32[]{:S(2)}, u32[]{:S(2)}) collective-permute-start(bf16[2,48,384]{2,1,0:T(8,128)(2,1)S(1)} %slice.9), channel_id=1, source_target_pairs={{0,15},{1,8},{2,9},{3,10},{4,11},{5,12},{6,13},{7,14},{8,23},{9,16... | collective-permute-start | bytes 221192 | tf_op jit(solution)/shard_map/ppermute | solution.py:235
  25.6 1.3 collective-permute-done.3.refs_10_
  27.0 4.9 %shard_map.103 = (bf16[2,180,384]{2,1,0:T(8,128)(2,1)S(1)}, bf16[2,180,384]{2,1,0:T(8,128)(2,1)}, bf16[2,72,384]{2,1,0:T(8,128)(2,1)}, bf16[2,48,384]{2,1,0:T(8,128)(2,1)S(1)}, bf16[8,192,384]{2,1,0:T(8,128)(2,1)}) custom-call(s32[16,32]{1,0:T(8,128)S(1)} %bitcast.27, s32[16,32]{1,0:T(8,128)S(1)} %bitcast.29, s32[16,32]{1,0:T(8,128)S(1)} %bitcast.31, ...), custom_call_target="tpu_custom_call" | custom-call | flops 2000000000 | bytes 8000000 | tf_op jit(solution)/shard_map/pallas_call | solution.py:136
  32.7 8.2 %all-to-all-start = ((bf16[8,192,384]{2,1,0:T(8,128)(2,1)}), bf16[8,192,384]{2,1,0:T(8,128)(2,1)S(1)}, u32[]{:S(2)}, u32[]{:S(2)}) async-start(bf16[8,192,384]{2,1,0:T(8,128)(2,1)} %get-tuple-element.19), calls=%async_computation | async-start | bytes 2359296 | tf_op jit(solution)/shard_map/all_to_all | solution.py:281
  40.9 1.3 collective-permute-start.6
  42.2 4.0 %collective-permute-start.5 = (bf16[2,180,384]{2,1,0:T(8,128)(2,1)}, bf16[2,180,384]{2,1,0:T(8,128)(2,1)S(1)}, u32[]{:S(2)}, u32[]{:S(2)}) collective-permute-start(bf16[2,180,384]{2,1,0:T(8,128)(2,1)} %get-tuple-element.20.own), channel_id=1, source_target_pairs={{0,8},{8,16},{16,24},{24,32},{32,40},{40,48},{48,56},{56,64},{64,7... | collective-permute-start | bytes 829448 | tf_op jit(solution)/shard_map/ppermute | solution.py:232
  46.2 3.0 %collective-permute-start.7 = (bf16[2,72,384]{2,1,0:T(8,128)(2,1)}, bf16[2,72,384]{2,1,0:T(8,128)(2,1)S(1)}, u32[]{:S(2)}, u32[]{:S(2)}) collective-permute-start(bf16[2,72,384]{2,1,0:T(8,128)(2,1)} %get-tuple-element.21), channel_id=1, source_target_pairs={{0,1},{1,2},{2,3},{3,4},{4,5},{5,6},{6,7},{7,0},{8,9},{9,10},{10,1... | collective-permute-start | bytes 331784 | tf_op jit(solution)/shard_map/ppermute | solution.py:234
  49.2 1.3 collective-permute-start.9
  50.5 5.8 %collective-permute-start.8 = (bf16[2,48,384]{2,1,0:T(8,128)(2,1)S(1)}, bf16[2,48,384]{2,1,0:T(8,128)(2,1)S(1)}, u32[]{:S(2)}, u32[]{:S(2)}) collective-permute-start(bf16[2,48,384]{2,1,0:T(8,128)(2,1)S(1)} %get-tuple-element.22), channel_id=1, source_target_pairs={{0,9},{1,10},{2,11},{3,12},{4,13},{5,14},{6,15},{7,8},{8,17},{9,18... | collective-permute-start | bytes 221192 | tf_op jit(solution)/shard_map/ppermute | solution.py:235
  56.3 2.4 %collective-permute-done.9.refs_5_ = bf16[2,48,384]{2,1,0:T(8,128)(2,1)S(1)} collective-permute-done((bf16[2,48,384]{2,1,0:T(8,128)(2,1)S(1)}, bf16[2,48,384]{2,1,0:T(8,128)(2,1)S(1)}, u32[]{:S(2)}, u32[]{:S(2)}) %collective-permute-start.9) | collective-permute-done | bytes 73760 | tf_op jit(solution)/shard_map/ppermute | solution.py:236
  58.7 4.9 %collective-permute-done.6.refs_2_ = bf16[2,180,384]{2,1,0:T(8,128)(2,1)S(1)} collective-permute-done((bf16[2,180,384]{2,1,0:T(8,128)(2,1)}, bf16[2,180,384]{2,1,0:T(8,128)(2,1)S(1)}, u32[]{:S(2)}, u32[]{:S(2)}) %collective-permute-start.6) | collective-permute-done | bytes 276512 | tf_op jit(solution)/shard_map/ppermute | solution.py:233
  63.6 5.9 %collective-permute-done.5.refs_1_ = bf16[2,180,384]{2,1,0:T(8,128)(2,1)S(1)} collective-permute-done((bf16[2,180,384]{2,1,0:T(8,128)(2,1)}, bf16[2,180,384]{2,1,0:T(8,128)(2,1)S(1)}, u32[]{:S(2)}, u32[]{:S(2)}) %collective-permute-start.5) | collective-permute-done | bytes 276512 | tf_op jit(solution)/shard_map/ppermute | solution.py:232
  69.7 24.3 %all_to_all.25.refs_0_ = f32[8,24,384]{2,1,0:T(8,128)S(1)} all-to-all(f32[8,24,384]{2,1,0:T(8,128)S(1)} %get-tuple-element.23), channel_id=1, replica_groups=mesh['x_hi'=2,'core'=2,'y'=8,'x_lo'=2,'lon'=8] {'y'}, dimensions={0} | all-to-all | bytes 589824 | tf_op jit(solution)/shard_map/all_to_all | solution.py:281
  94.1 12.3 %all_to_all.26.refs_0_ = f32[8,24,384]{2,1,0:T(8,128)S(1)} all-to-all(f32[8,24,384]{2,1,0:T(8,128)S(1)} %shard_map.105), channel_id=1, replica_groups=mesh['x_hi'=2,'core'=2,'y'=8,'x_lo'=2,'lon'=8] {'lon'}, dimensions={0} | all-to-all | bytes 589824 | tf_op jit(solution)/shard_map/all_to_all | solution.py:281
  107.0 4.3 %all-to-all-start.3 = ((bf16[8,24,384]{2,1,0:T(8,128)(2,1)}), bf16[8,24,384]{2,1,0:T(8,128)(2,1)S(1)}, u32[]{:S(2)}, u32[]{:S(2)}) async-start(bf16[8,24,384]{2,1,0:T(8,128)(2,1)} %shard_map.106), calls=%async_computation.3 | async-start | bytes 294912 | tf_op jit(solution)/shard_map/all_to_all | solution.py:281
  111.3 4.2 %shard_map.107 = (bf16[2,180,384]{2,1,0:T(8,128)(2,1)S(1)}, bf16[2,180,384]{2,1,0:T(8,128)(2,1)S(1)}) custom-call(s32[16,32]{1,0:T(8,128)S(1)} %bitcast.28, s32[16,32]{1,0:T(8,128)S(1)} %bitcast.30, s32[16,32]{1,0:T(8,128)S(1)} %bitcast.32, f32[16,32]{1,0:T(8,128)S(1)} %bitcast.34, s32[32]{0:T(128)S(1)} %copy-done.8, bf16[1536,384]{1,0:T(8,128)(2,1)S(1)} %bitcast.26, ...), custom_call_target="tpu_custom_call" | custom-call | flops 2500000000 | bytes 5000000 | tf_op jit(solution)/shard_map/pallas_call | solution.py:207
  115.6 3.9 %all-to-all-done.3 = bf16[8,24,384]{2,1,0:T(8,128)(2,1)S(1)} async-done(((bf16[8,24,384]{2,1,0:T(8,128)(2,1)}), bf16[8,24,384]{2,1,0:T(8,128)(2,1)S(1)}, u32[]{:S(2)}, u32[]{:S(2)}) %all-to-all-start.3) | async-done | bytes 147488 | tf_op jit(solution)/shard_map/all_to_all | solution.py:281
  119.5 1.1 shard_map.108
  120.6 8.3 %all-to-all-start.4 = ((bf16[8,192,384]{2,1,0:T(8,128)(2,1)}), bf16[8,192,384]{2,1,0:T(8,128)(2,1)S(1)}, u32[]{:S(2)}, u32[]{:S(2)}) async-start(bf16[8,192,384]{2,1,0:T(8,128)(2,1)} %get-tuple-element.34), calls=%async_computation.4 | async-start | bytes 2359296 | tf_op jit(solution)/shard_map/all_to_all | solution.py:281
  130.8 14.7 %all-to-all-done.4 = bf16[8,192,384]{2,1,0:T(8,128)(2,1)S(1)} async-done(((bf16[8,192,384]{2,1,0:T(8,128)(2,1)}), bf16[8,192,384]{2,1,0:T(8,128)(2,1)S(1)}, u32[]{:S(2)}, u32[]{:S(2)}) %all-to-all-start.4) | async-done | bytes 1179680 | tf_op jit(solution)/shard_map/all_to_all | solution.py:281
  (40 shorter events, 6.7 us)
Async XLA Ops:
  0.6 26.4 %copy-start.7 = (s32[32]{0:T(128)S(1)}, s32[32]{0:T(128)}, u32[]{:S(2)}) copy-start(s32[32]{0:T(128)} %tap_count.1) | copy-start | bytes 388
  0.6 26.3 %copy-start.5 = (f32[32,16]{0,1:T(8,128)S(1)}, f32[32,16]{0,1:T(8,128)}, u32[]{:S(2)}) copy-start(f32[32,16]{0,1:T(8,128)} %param.14) | copy-start | bytes 6148
  0.7 26.3 %copy-start.3 = (s32[32,16]{0,1:T(8,128)S(1)}, s32[32,16]{0,1:T(8,128)}, u32[]{:S(2)}) copy-start(s32[32,16]{0,1:T(8,128)} %param.13) | copy-start | bytes 6148
  0.7 26.3 %copy-start.2 = (s32[32,16]{0,1:T(8,128)S(1)}, s32[32,16]{0,1:T(8,128)}, u32[]{:S(2)}) copy-start(s32[32,16]{0,1:T(8,128)} %param.12) | copy-start | bytes 6148
  0.7 26.3 %copy-start.1 = (s32[32,16]{0,1:T(8,128)S(1)}, s32[32,16]{0,1:T(8,128)}, u32[]{:S(2)}) copy-start(s32[32,16]{0,1:T(8,128)} %param.11) | copy-start | bytes 6148
  0.7 26.3 %copy-start = (bf16[4,384,384]{2,1,0:T(8,128)(2,1)S(1)}, bf16[4,384,384]{2,1,0:T(8,128)(2,1)}, u32[]{:S(2)}) copy-start(bf16[4,384,384]{2,1,0:T(8,128)(2,1)} %param.10) | copy-start | bytes 3538948
  1.8 25.2 %collective-permute-start.1 = (bf16[2,180,384]{2,1,0:T(8,128)(2,1)S(1)}, bf16[2,180,384]{2,1,0:T(8,128)(2,1)S(1)}, u32[]{:S(2)}, u32[]{:S(2)}) collective-permute-start(bf16[2,180,384]{2,1,0:T(8,128)(2,1)S(1)} %bitcast.18), channel_id=1, source_target_pairs={{8,0},{16,8},{24,16},{32,24},{40,32},{48,40},{56,48},{64,56},{72,6... | collective-permute-start | bytes 829448 | tf_op jit(solution)/shard_map/ppermute | solution.py:233
  3.1 23.9 %collective-permute-start = (bf16[2,180,384]{2,1,0:T(8,128)(2,1)S(1)}, bf16[2,180,384]{2,1,0:T(8,128)(2,1)S(1)}, u32[]{:S(2)}, u32[]{:S(2)}) collective-permute-start(bf16[2,180,384]{2,1,0:T(8,128)(2,1)S(1)} %bitcast.19), channel_id=1, source_target_pairs={{0,8},{8,16},{16,24},{24,32},{32,40},{40,48},{48,56},{56,64},{64,7... | collective-permute-start | bytes 829448 | tf_op jit(solution)/shard_map/ppermute | solution.py:232
  8.7 18.2 %collective-permute-start.2 = (bf16[2,72,384]{2,1,0:T(8,128)(2,1)S(1)}, bf16[2,72,384]{2,1,0:T(8,128)(2,1)S(1)}, u32[]{:S(2)}, u32[]{:S(2)}) collective-permute-start(bf16[2,72,384]{2,1,0:T(8,128)(2,1)S(1)} %pad_maximum_fusion), channel_id=1, source_target_pairs={{0,7},{1,0},{2,1},{3,2},{4,3},{5,4},{6,5},{7,6},{8,15},{9,8},{10,9... | collective-permute-start | bytes 331784 | tf_op jit(solution)/shard_map/ppermute | solution.py:234
  19.6 6.0 %collective-permute-start.4 = (bf16[2,48,384]{2,1,0:T(8,128)(2,1)S(1)}, bf16[2,48,384]{2,1,0:T(8,128)(2,1)S(1)}, u32[]{:S(2)}, u32[]{:S(2)}) collective-permute-start(bf16[2,48,384]{2,1,0:T(8,128)(2,1)S(1)} %slice.9), channel_id=1, source_target_pairs={{8,7},{9,0},{10,1},{11,2},{12,3},{13,4},{14,5},{15,6},{16,15},{17,... | collective-permute-start | bytes 221192 | tf_op jit(solution)/shard_map/ppermute | solution.py:236
  20.9 6.0 %collective-permute-start.3 = (bf16[2,48,384]{2,1,0:T(8,128)(2,1)S(1)}, bf16[2,48,384]{2,1,0:T(8,128)(2,1)S(1)}, u32[]{:S(2)}, u32[]{:S(2)}) collective-permute-start(bf16[2,48,384]{2,1,0:T(8,128)(2,1)S(1)} %slice.9), channel_id=1, source_target_pairs={{0,15},{1,8},{2,9},{3,10},{4,11},{5,12},{6,13},{7,14},{8,23},{9,16... | collective-permute-start | bytes 221192 | tf_op jit(solution)/shard_map/ppermute | solution.py:235
  32.0 0.7 copy-start.9
  32.7 36.8 %all-to-all-start = ((bf16[8,192,384]{2,1,0:T(8,128)(2,1)}), bf16[8,192,384]{2,1,0:T(8,128)(2,1)S(1)}, u32[]{:S(2)}, u32[]{:S(2)}) async-start(bf16[8,192,384]{2,1,0:T(8,128)(2,1)} %get-tuple-element.19), calls=%async_computation | async-start | bytes 2359296 | tf_op jit(solution)/shard_map/all_to_all | solution.py:281
  40.9 22.7 %collective-permute-start.6 = (bf16[2,180,384]{2,1,0:T(8,128)(2,1)}, bf16[2,180,384]{2,1,0:T(8,128)(2,1)S(1)}, u32[]{:S(2)}, u32[]{:S(2)}) collective-permute-start(bf16[2,180,384]{2,1,0:T(8,128)(2,1)} %get-tuple-element.20.own), channel_id=1, source_target_pairs={{8,0},{16,8},{24,16},{32,24},{40,32},{48,40},{56,48},{64,56},{72,6... | collective-permute-start | bytes 829448 | tf_op jit(solution)/shard_map/ppermute | solution.py:233
  42.2 27.3 %collective-permute-start.5 = (bf16[2,180,384]{2,1,0:T(8,128)(2,1)}, bf16[2,180,384]{2,1,0:T(8,128)(2,1)S(1)}, u32[]{:S(2)}, u32[]{:S(2)}) collective-permute-start(bf16[2,180,384]{2,1,0:T(8,128)(2,1)} %get-tuple-element.20.own), channel_id=1, source_target_pairs={{0,8},{8,16},{16,24},{24,32},{32,40},{40,48},{48,56},{56,64},{64,7... | collective-permute-start | bytes 829448 | tf_op jit(solution)/shard_map/ppermute | solution.py:232
  46.2 12.5 %collective-permute-start.7 = (bf16[2,72,384]{2,1,0:T(8,128)(2,1)}, bf16[2,72,384]{2,1,0:T(8,128)(2,1)S(1)}, u32[]{:S(2)}, u32[]{:S(2)}) collective-permute-start(bf16[2,72,384]{2,1,0:T(8,128)(2,1)} %get-tuple-element.21), channel_id=1, source_target_pairs={{0,1},{1,2},{2,3},{3,4},{4,5},{5,6},{6,7},{7,0},{8,9},{9,10},{10,1... | collective-permute-start | bytes 331784 | tf_op jit(solution)/shard_map/ppermute | solution.py:234
  49.2 9.4 %collective-permute-start.9 = (bf16[2,48,384]{2,1,0:T(8,128)(2,1)S(1)}, bf16[2,48,384]{2,1,0:T(8,128)(2,1)S(1)}, u32[]{:S(2)}, u32[]{:S(2)}) collective-permute-start(bf16[2,48,384]{2,1,0:T(8,128)(2,1)S(1)} %get-tuple-element.22), channel_id=1, source_target_pairs={{8,1},{9,2},{10,3},{11,4},{12,5},{13,6},{14,7},{15,0},{16,9},{17,1... | collective-permute-start | bytes 221192 | tf_op jit(solution)/shard_map/ppermute | solution.py:236
  50.5 8.1 %collective-permute-start.8 = (bf16[2,48,384]{2,1,0:T(8,128)(2,1)S(1)}, bf16[2,48,384]{2,1,0:T(8,128)(2,1)S(1)}, u32[]{:S(2)}, u32[]{:S(2)}) collective-permute-start(bf16[2,48,384]{2,1,0:T(8,128)(2,1)S(1)} %get-tuple-element.22), channel_id=1, source_target_pairs={{0,9},{1,10},{2,11},{3,12},{4,13},{5,14},{6,15},{7,8},{8,17},{9,18... | collective-permute-start | bytes 221192 | tf_op jit(solution)/shard_map/ppermute | solution.py:235
  69.6 41.7 %copy-start.4 = (s32[32,16]{0,1:T(8,128)S(1)}, s32[32,16]{0,1:T(8,128)}, u32[]{:S(2)}) copy-start(s32[32,16]{0,1:T(8,128)} %param.13) | copy-start | bytes 6148
  69.7 41.7 %copy-start.6 = (f32[32,16]{0,1:T(8,128)S(1)}, f32[32,16]{0,1:T(8,128)}, u32[]{:S(2)}) copy-start(f32[32,16]{0,1:T(8,128)} %param.14) | copy-start | bytes 6148
  69.7 41.7 %copy-start.8 = (s32[32]{0:T(128)S(1)}, s32[32]{0:T(128)}, u32[]{:S(2)}) copy-start(s32[32]{0:T(128)} %tap_count.1) | copy-start | bytes 388
  69.7 41.7 %copy-start.10 = (bf16[2,180,384]{2,1,0:T(8,128)(2,1)S(1)}, bf16[2,180,384]{2,1,0:T(8,128)(2,1)}, u32[]{:S(2)}) copy-start(bf16[2,180,384]{2,1,0:T(8,128)(2,1)} %copy-done.9) | copy-start | bytes 829444
  107.0 12.5 %all-to-all-start.3 = ((bf16[8,24,384]{2,1,0:T(8,128)(2,1)}), bf16[8,24,384]{2,1,0:T(8,128)(2,1)S(1)}, u32[]{:S(2)}, u32[]{:S(2)}) async-start(bf16[8,24,384]{2,1,0:T(8,128)(2,1)} %shard_map.106), calls=%async_computation.3 | async-start | bytes 294912 | tf_op jit(solution)/shard_map/all_to_all | solution.py:281
  120.6 24.9 %all-to-all-start.4 = ((bf16[8,192,384]{2,1,0:T(8,128)(2,1)}), bf16[8,192,384]{2,1,0:T(8,128)(2,1)S(1)}, u32[]{:S(2)}, u32[]{:S(2)}) async-start(bf16[8,192,384]{2,1,0:T(8,128)(2,1)} %get-tuple-element.34), calls=%async_computation.4 | async-start | bytes 2359296 | tf_op jit(solution)/shard_map/all_to_all | solution.py:281

commit v5 on v4

--- a/solution.py
+++ b/solution.py
@@ -220,21 +220,20 @@
     )(*tables, weights, *fields, made, upstream)
 
 
-def around(block, side, rim, step):
-    lats, lons = lax.axis_size(LAT), lax.axis_size("lon")
-    from_north = [(i, i + 1) for i in range(lats - 1)]
-    from_south = [(i + 1, i) for i in range(lats - 1)]
+def lat_blocks(block):
+    ends = lax.axis_size(LAT) - 1
+    north = lax.ppermute(block, LAT, [(i, i + 1) for i in range(ends)])
+    south = lax.ppermute(block, LAT, [(i + 1, i) for i in range(ends)])
+    return north, south
+
+
+def lon_strips(side, rim, step):
+    ends, lons = lax.axis_size(LAT) - 1, lax.axis_size("lon")
     along = [(j, (j + step) % lons) for j in range(lons)]
-
-    def corner(lat_pairs):
-        return [(a * lons + c, b * lons + d) for a, b in lat_pairs for c, d in along]
-
-    north = lax.ppermute(block, LAT, from_north)
-    south = lax.ppermute(block, LAT, from_south)
     level = lax.ppermute(side, "lon", along)
-    upper = lax.ppermute(rim, LAT + ("lon",), corner(from_north))
-    lower = lax.ppermute(rim, LAT + ("lon",), corner(from_south))
-    return block, north, south, level, upper, lower
+    upper = lax.ppermute(rim, LAT + ("lon",), [(i * lons + c, (i + 1) * lons + d) for i in range(ends) for c, d in along])
+    lower = lax.ppermute(rim, LAT + ("lon",), [((i + 1) * lons + c, i * lons + d) for i in range(ends) for c, d in along])
+    return level, upper, lower
 
 
 def sum_pieces(pieces, out_shape, passed=()):
@@ -288,23 +287,23 @@
     wide = weights.reshape(-1, channels)
     tables = (lat_off.T, lon_off.T, basis.T, tap_val.T, tap_count)
     side = jnp.concatenate([field[:, :RIM], upstream[:, :LONREACH]], axis=1)
-    fields = around(field, side, field[:, :RIM], -1)
+    fields = (field, *lat_blocks(field), *lon_strips(side, field[:, :RIM], -1))
     cells = lax.axis_size(DP) * lax.axis_size(LAT) * rows * lax.axis_size("lon") * width
     nx, ny, nz = lax.axis_size(ALONG_X), lax.axis_size("y"), lax.axis_size("lon")
     made, dmixed, side, rim, share = forward(tables, wide, fields, upstream, 1.0 / math.sqrt(cells), nx)
     piece = (wide.shape[0] // (nx * ny), channels)
     got = exchange(share, ALONG_X)
-    fields = around(dmixed, side, rim, 1)
-    part, *near = sum_pieces(got, jax.ShapeDtypeStruct((ny, *piece), F32), fields[1:])
-    fields = (dmixed, *near)
-    got = exchange(part, "y")
-    (part,) = sum_pieces(got, jax.ShapeDtypeStruct((nz, *piece), F32))
-    got = exchange(part, "lon")
     (part,) = sum_pieces(got, jax.ShapeDtypeStruct((ny, *piece), BF16))
     got = exchange(part, "y")
-    new_field, field_grad = backward(tables, wide, fields, made, upstream)
-    part, new_field, field_grad = spread(got.reshape(-1, channels), nx, (new_field, field_grad))
+    part, dmixed = sum_pieces(got, jax.ShapeDtypeStruct((nz, *piece), F32), (dmixed,))
+    blocks = lat_blocks(dmixed)
+    got = exchange(part, "lon")
+    part, side, rim = sum_pieces(got, jax.ShapeDtypeStruct((ny, *piece), BF16), (side, rim))
+    strips = lon_strips(side, rim, 1)
+    got = exchange(part, "y")
+    part, *near = spread(got.reshape(-1, channels), nx, (*blocks, *strips))
     weight_grad = exchange(part, ALONG_X).reshape(weights.shape)
+    new_field, field_grad = backward(tables, wide, (dmixed, *near), made, upstream)
     return new_field[None], field_grad[None], weight_grad
 
 

time: 147 us -> 137 us (0.932)
  the two profiles are of different devices: /device:TPU:1 before, /device:TPU:32 now
where the time goes in v5:
time: 137 us; the launch traced here: 136 us
  starting transfers between devices  54.6 us (40%)
  blocking collectives  32.1 us (23%)
  waiting for transfers between devices  29.8 us (22%)
  Pallas kernels  12.1 us (9%)
  local copies, waits for them, and re-layouts  6.36 us (5%)
    all_to_all x2, blocking collectives, exchange(): return lax.all_to_all(pieces, axes, 0, 0, tiled=True)  32.1 us
    all_to_all x3, starting transfers between devices, exchange(): return lax.all_to_all(pieces, axes, 0, 0, tiled=True)  16.2 us
    all_to_all x3, waiting for transfers between devices, exchange(): return lax.all_to_all(pieces, axes, 0, 0, tiled=True)  15.5 us
    ppermute x2, starting transfers between devices, lon_strips(): level = lax.ppermute(side, 'lon', along)  13.4 us
    ppermute x2, waiting for transfers between devices, lon_strips(): lax.ppermute(rim, LAT + ('lon',), [(i * lons + c, (i + 1) * lons + d) for...  11.5 us
    ppermute x2, starting transfers between devices, lat_blocks(): south = lax.ppermute(block, LAT, [(i + 1, i) for i in range(ends)])  7.68 us
    ppermute x2, starting transfers between devices, lon_strips(): lax.ppermute(rim, LAT + ('lon',), [((i + 1) * lons + c, i * lons + d) for...  7.52 us
    unnamed x17, local copies, waits for them, and re-layouts  6.34 us
  transfers between devices with their start and end apart: 13, of which 5 were waited for; matrix products, arithmetic and copies ran while one was open for 2% of the time, Pallas kernels for 4%

profile of v5, /device:TPU:32, one launch (start us, length us, event | category | flops | bytes accessed | tf_op | source)
XLA Modules:
  0.0 135.9 jit_solution(13085976722947501796)
XLA Ops:
  1.8 3.3 %collective-permute-start.1 = (bf16[2,180,384]{2,1,0:T(8,128)(2,1)S(1)}, bf16[2,180,384]{2,1,0:T(8,128)(2,1)S(1)}, u32[]{:S(2)}, u32[]{:S(2)}) collective-permute-start(bf16[2,180,384]{2,1,0:T(8,128)(2,1)S(1)} %bitcast.16), channel_id=1, source_target_pairs={{8,0},{16,8},{24,16},{32,24},{40,32},{48,40},{56,48},{64,56},{72,6... | collective-permute-start | bytes 829448 | tf_op jit(solution)/shard_map/ppermute | solution.py:226
  5.1 2.6 %collective-permute-start = (bf16[2,180,384]{2,1,0:T(8,128)(2,1)S(1)}, bf16[2,180,384]{2,1,0:T(8,128)(2,1)S(1)}, u32[]{:S(2)}, u32[]{:S(2)}) collective-permute-start(bf16[2,180,384]{2,1,0:T(8,128)(2,1)S(1)} %bitcast.17), channel_id=1, source_target_pairs={{0,8},{8,16},{16,24},{24,32},{32,40},{40,48},{48,56},{56,64},{64,7... | collective-permute-start | bytes 829448 | tf_op jit(solution)/shard_map/ppermute | solution.py:225
  8.7 10.9 %collective-permute-start.2 = (bf16[2,72,384]{2,1,0:T(8,128)(2,1)S(1)}, bf16[2,72,384]{2,1,0:T(8,128)(2,1)S(1)}, u32[]{:S(2)}, u32[]{:S(2)}) collective-permute-start(bf16[2,72,384]{2,1,0:T(8,128)(2,1)S(1)} %pad_maximum_fusion), channel_id=1, source_target_pairs={{0,7},{1,0},{2,1},{3,2},{4,3},{5,4},{6,5},{7,6},{8,15},{9,8},{10,9... | collective-permute-start | bytes 331784 | tf_op jit(solution)/shard_map/ppermute | solution.py:233
  19.6 5.4 %collective-permute-start.4 = (bf16[2,48,384]{2,1,0:T(8,128)(2,1)S(1)}, bf16[2,48,384]{2,1,0:T(8,128)(2,1)S(1)}, u32[]{:S(2)}, u32[]{:S(2)}) collective-permute-start(bf16[2,48,384]{2,1,0:T(8,128)(2,1)S(1)} %slice.9), channel_id=1, source_target_pairs={{8,7},{9,0},{10,1},{11,2},{12,3},{13,4},{14,5},{15,6},{16,15},{17,... | collective-permute-start | bytes 221192 | tf_op jit(solution)/shard_map/ppermute | solution.py:235
  25.0 1.9 %collective-permute-start.3 = (bf16[2,48,384]{2,1,0:T(8,128)(2,1)S(1)}, bf16[2,48,384]{2,1,0:T(8,128)(2,1)S(1)}, u32[]{:S(2)}, u32[]{:S(2)}) collective-permute-start(bf16[2,48,384]{2,1,0:T(8,128)(2,1)S(1)} %slice.9), channel_id=1, source_target_pairs={{0,15},{1,8},{2,9},{3,10},{4,11},{5,12},{6,13},{7,14},{8,23},{9,16... | collective-permute-start | bytes 221192 | tf_op jit(solution)/shard_map/ppermute | solution.py:234
  27.0 7.3 %collective-permute-done.3.refs_10_ = bf16[2,48,384]{2,1,0:T(8,128)(2,1)S(1)} collective-permute-done((bf16[2,48,384]{2,1,0:T(8,128)(2,1)S(1)}, bf16[2,48,384]{2,1,0:T(8,128)(2,1)S(1)}, u32[]{:S(2)}, u32[]{:S(2)}) %collective-permute-start.3) | collective-permute-done | bytes 73760 | tf_op jit(solution)/shard_map/ppermute | solution.py:234
  34.4 4.5 %shard_map.103 = (bf16[2,180,384]{2,1,0:T(8,128)(2,1)S(1)}, bf16[2,180,384]{2,1,0:T(8,128)(2,1)S(1)}, bf16[2,72,384]{2,1,0:T(8,128)(2,1)S(1)}, bf16[2,48,384]{2,1,0:T(8,128)(2,1)S(1)}, bf16[8,192,384]{2,1,0:T(8,128)(2,1)S(1)}) custom-call(s32[16,32]{1,0:T(8,128)S(1)} %bitcast.27, s32[16,32]{1,0:T(8,128)S(1)} %bitcast.29, s32[16,32]{1,0:T(8,128)S(1)} %bitcast.31, ...), custom_call_target="tpu_custom_call" | custom-call | flops 2000000000 | bytes 8000000 | tf_op jit(solution)/shard_map/pallas_call | solution.py:136
  38.9 21.2 %all_to_all.25.refs_0_ = bf16[8,192,384]{2,1,0:T(8,128)(2,1)S(1)} all-to-all(bf16[8,192,384]{2,1,0:T(8,128)(2,1)S(1)} %get-tuple-element.21), channel_id=1, replica_groups=mesh['x_hi'=2,'core'=2,'y'=8,'x_lo'=2,'lon'=8] {'x_hi','core','x_lo'}, dimensions={0} | all-to-all | bytes 2359296 | tf_op jit(solution)/shard_map/all_to_all | solution.py:280
  60.2 10.9 %all_to_all.26.refs_0_ = bf16[8,24,384]{2,1,0:T(8,128)(2,1)S(1)} all-to-all(bf16[8,24,384]{2,1,0:T(8,128)(2,1)S(1)} %shard_map.104), channel_id=1, replica_groups=mesh['x_hi'=2,'core'=2,'y'=8,'x_lo'=2,'lon'=8] {'y'}, dimensions={0} | all-to-all | bytes 294912 | tf_op jit(solution)/shard_map/all_to_all | solution.py:280
  71.8 3.4 %all-to-all-start.2 = ((f32[8,24,384]{2,1,0:T(8,128)}), f32[8,24,384]{2,1,0:T(8,128)S(1)}, u32[]{:S(2)}, u32[]{:S(2)}) async-start(f32[8,24,384]{2,1,0:T(8,128)} %get-tuple-element.24), calls=%async_computation.2 | async-start | bytes 589824 | tf_op jit(solution)/shard_map/all_to_all | solution.py:280
  75.3 4.4 %collective-permute-start.6 = (bf16[2,180,384]{2,1,0:T(8,128)(2,1)S(1)}, bf16[2,180,384]{2,1,0:T(8,128)(2,1)S(1)}, u32[]{:S(2)}, u32[]{:S(2)}) collective-permute-start(bf16[2,180,384]{2,1,0:T(8,128)(2,1)S(1)} %get-tuple-element.23.own), channel_id=1, source_target_pairs={{8,0},{16,8},{24,16},{32,24},{40,32},{48,40},{56,48},{64,56},{72,6... | collective-permute-start | bytes 829448 | tf_op jit(solution)/shard_map/ppermute | solution.py:226
  79.7 1.9 %collective-permute-start.5 = (bf16[2,180,384]{2,1,0:T(8,128)(2,1)S(1)}, bf16[2,180,384]{2,1,0:T(8,128)(2,1)S(1)}, u32[]{:S(2)}, u32[]{:S(2)}) collective-permute-start(bf16[2,180,384]{2,1,0:T(8,128)(2,1)S(1)} %get-tuple-element.23.own), channel_id=1, source_target_pairs={{0,8},{8,16},{16,24},{24,32},{32,40},{40,48},{48,56},{56,64},{64,7... | collective-permute-start | bytes 829448 | tf_op jit(solution)/shard_map/ppermute | solution.py:225
  81.6 4.8 %all-to-all-done.2.refs_0_ = f32[8,24,384]{2,1,0:T(8,128)S(1)} async-done(((f32[8,24,384]{2,1,0:T(8,128)}), f32[8,24,384]{2,1,0:T(8,128)S(1)}, u32[]{:S(2)}, u32[]{:S(2)}) %all-to-all-start.2) | async-done | bytes 294944 | tf_op jit(solution)/shard_map/all_to_all | solution.py:280
  87.1 8.5 %all-to-all-start.3 = ((bf16[8,24,384]{2,1,0:T(8,128)(2,1)}), bf16[8,24,384]{2,1,0:T(8,128)(2,1)S(1)}, u32[]{:S(2)}, u32[]{:S(2)}) async-start(bf16[8,24,384]{2,1,0:T(8,128)(2,1)} %get-tuple-element.27), calls=%async_computation.3 | async-start | bytes 294912 | tf_op jit(solution)/shard_map/all_to_all | solution.py:280
  95.6 2.5 %collective-permute-start.7 = (bf16[2,72,384]{2,1,0:T(8,128)(2,1)S(1)}, bf16[2,72,384]{2,1,0:T(8,128)(2,1)S(1)}, u32[]{:S(2)}, u32[]{:S(2)}) collective-permute-start(bf16[2,72,384]{2,1,0:T(8,128)(2,1)S(1)} %get-tuple-element.28), channel_id=1, source_target_pairs={{0,1},{1,2},{2,3},{3,4},{4,5},{5,6},{6,7},{7,0},{8,9},{9,10},{10,1... | collective-permute-start | bytes 331784 | tf_op jit(solution)/shard_map/ppermute | solution.py:233
  98.1 2.1 %collective-permute-start.9 = (bf16[2,48,384]{2,1,0:T(8,128)(2,1)S(1)}, bf16[2,48,384]{2,1,0:T(8,128)(2,1)S(1)}, u32[]{:S(2)}, u32[]{:S(2)}) collective-permute-start(bf16[2,48,384]{2,1,0:T(8,128)(2,1)S(1)} %get-tuple-element.29), channel_id=1, source_target_pairs={{8,1},{9,2},{10,3},{11,4},{12,5},{13,6},{14,7},{15,0},{16,9},{17,1... | collective-permute-start | bytes 221192 | tf_op jit(solution)/shard_map/ppermute | solution.py:235
  100.2 3.4 %collective-permute-start.8 = (bf16[2,48,384]{2,1,0:T(8,128)(2,1)S(1)}, bf16[2,48,384]{2,1,0:T(8,128)(2,1)S(1)}, u32[]{:S(2)}, u32[]{:S(2)}) collective-permute-start(bf16[2,48,384]{2,1,0:T(8,128)(2,1)S(1)} %get-tuple-element.29), channel_id=1, source_target_pairs={{0,9},{1,10},{2,11},{3,12},{4,13},{5,14},{6,15},{7,8},{8,17},{9,18... | collective-permute-start | bytes 221192 | tf_op jit(solution)/shard_map/ppermute | solution.py:234
  103.7 2.8 %collective-permute-done.9.refs_5_ = bf16[2,48,384]{2,1,0:T(8,128)(2,1)S(1)} collective-permute-done((bf16[2,48,384]{2,1,0:T(8,128)(2,1)S(1)}, bf16[2,48,384]{2,1,0:T(8,128)(2,1)S(1)}, u32[]{:S(2)}, u32[]{:S(2)}) %collective-permute-start.9) | collective-permute-done | bytes 73760 | tf_op jit(solution)/shard_map/ppermute | solution.py:235
  106.5 4.2 %collective-permute-done.8.refs_4_ = bf16[2,48,384]{2,1,0:T(8,128)(2,1)S(1)} collective-permute-done((bf16[2,48,384]{2,1,0:T(8,128)(2,1)S(1)}, bf16[2,48,384]{2,1,0:T(8,128)(2,1)S(1)}, u32[]{:S(2)}, u32[]{:S(2)}) %collective-permute-start.8) | collective-permute-done | bytes 73760 | tf_op jit(solution)/shard_map/ppermute | solution.py:234
  110.7 1.1 shard_map.107
  111.8 4.3 %all-to-all-start.4 = ((bf16[8,192,384]{2,1,0:T(8,128)(2,1)}), bf16[8,192,384]{2,1,0:T(8,128)(2,1)}, u32[]{:S(2)}, u32[]{:S(2)}) async-start(bf16[8,192,384]{2,1,0:T(8,128)(2,1)} %get-tuple-element.38), calls=%async_computation.4 | async-start | bytes 2359296 | tf_op jit(solution)/shard_map/all_to_all | solution.py:280
  116.1 4.9 %shard_map.108 = (bf16[2,180,384]{2,1,0:T(8,128)(2,1)S(1)}, bf16[2,180,384]{2,1,0:T(8,128)(2,1)S(1)}) custom-call(s32[16,32]{1,0:T(8,128)S(1)} %bitcast.28, s32[16,32]{1,0:T(8,128)S(1)} %bitcast.30, s32[16,32]{1,0:T(8,128)S(1)} %bitcast.32, f32[16,32]{1,0:T(8,128)S(1)} %bitcast.34, s32[32]{0:T(128)S(1)} %copy-done.5, bf16[1536,384]{1,0:T(8,128)(2,1)S(1)} %bitcast.26, ...), custom_call_target="tpu_custom_call" | custom-call | flops 2500000000 | bytes 5000000 | tf_op jit(solution)/shard_map/pallas_call | solution.py:207
  122.8 10.7 %all-to-all-done.4 = bf16[8,192,384]{2,1,0:T(8,128)(2,1)} async-done(((bf16[8,192,384]{2,1,0:T(8,128)(2,1)}), bf16[8,192,384]{2,1,0:T(8,128)(2,1)}, u32[]{:S(2)}, u32[]{:S(2)}) %all-to-all-start.4) | async-done | bytes 1179680 | tf_op jit(solution)/shard_map/all_to_all | solution.py:280
  133.5 2.4 %copy.36 = bf16[4,384,384]{2,1,0:T(8,128)(2,1)} copy(bf16[4,384,384]{2,1,0:T(8,128)(2,1)} %bitcast.10) | data formatting | bytes 2359296
  (30 shorter events, 5.6 us)
Async XLA Ops:
  0.6 33.7 %copy-start.5 = (s32[32]{0:T(128)S(1)}, s32[32]{0:T(128)}, u32[]{:S(2)}) copy-start(s32[32]{0:T(128)} %tap_count.1) | copy-start | bytes 388
  0.6 33.7 %copy-start.4 = (f32[32,16]{0,1:T(8,128)S(1)}, f32[32,16]{0,1:T(8,128)}, u32[]{:S(2)}) copy-start(f32[32,16]{0,1:T(8,128)} %param.14) | copy-start | bytes 6148
  0.7 33.7 %copy-start.3 = (s32[32,16]{0,1:T(8,128)S(1)}, s32[32,16]{0,1:T(8,128)}, u32[]{:S(2)}) copy-start(s32[32,16]{0,1:T(8,128)} %param.13) | copy-start | bytes 6148
  0.7 33.7 %copy-start.2 = (s32[32,16]{0,1:T(8,128)S(1)}, s32[32,16]{0,1:T(8,128)}, u32[]{:S(2)}) copy-start(s32[32,16]{0,1:T(8,128)} %param.12) | copy-start | bytes 6148
  0.7 33.7 %copy-start.1 = (s32[32,16]{0,1:T(8,128)S(1)}, s32[32,16]{0,1:T(8,128)}, u32[]{:S(2)}) copy-start(s32[32,16]{0,1:T(8,128)} %param.11) | copy-start | bytes 6148
  0.7 33.7 %copy-start = (bf16[4,384,384]{2,1,0:T(8,128)(2,1)S(1)}, bf16[4,384,384]{2,1,0:T(8,128)(2,1)}, u32[]{:S(2)}) copy-start(bf16[4,384,384]{2,1,0:T(8,128)(2,1)} %param.10) | copy-start | bytes 3538948
  1.8 32.5 %collective-permute-start.1 = (bf16[2,180,384]{2,1,0:T(8,128)(2,1)S(1)}, bf16[2,180,384]{2,1,0:T(8,128)(2,1)S(1)}, u32[]{:S(2)}, u32[]{:S(2)}) collective-permute-start(bf16[2,180,384]{2,1,0:T(8,128)(2,1)S(1)} %bitcast.16), channel_id=1, source_target_pairs={{8,0},{16,8},{24,16},{32,24},{40,32},{48,40},{56,48},{64,56},{72,6... | collective-permute-start | bytes 829448 | tf_op jit(solution)/shard_map/ppermute | solution.py:226
  5.1 29.2 %collective-permute-start = (bf16[2,180,384]{2,1,0:T(8,128)(2,1)S(1)}, bf16[2,180,384]{2,1,0:T(8,128)(2,1)S(1)}, u32[]{:S(2)}, u32[]{:S(2)}) collective-permute-start(bf16[2,180,384]{2,1,0:T(8,128)(2,1)S(1)} %bitcast.17), channel_id=1, source_target_pairs={{0,8},{8,16},{16,24},{24,32},{32,40},{40,48},{48,56},{56,64},{64,7... | collective-permute-start | bytes 829448 | tf_op jit(solution)/shard_map/ppermute | solution.py:225
  8.7 25.6 %collective-permute-start.2 = (bf16[2,72,384]{2,1,0:T(8,128)(2,1)S(1)}, bf16[2,72,384]{2,1,0:T(8,128)(2,1)S(1)}, u32[]{:S(2)}, u32[]{:S(2)}) collective-permute-start(bf16[2,72,384]{2,1,0:T(8,128)(2,1)S(1)} %pad_maximum_fusion), channel_id=1, source_target_pairs={{0,7},{1,0},{2,1},{3,2},{4,3},{5,4},{6,5},{7,6},{8,15},{9,8},{10,9... | collective-permute-start | bytes 331784 | tf_op jit(solution)/shard_map/ppermute | solution.py:233
  19.6 7.4 %collective-permute-start.4 = (bf16[2,48,384]{2,1,0:T(8,128)(2,1)S(1)}, bf16[2,48,384]{2,1,0:T(8,128)(2,1)S(1)}, u32[]{:S(2)}, u32[]{:S(2)}) collective-permute-start(bf16[2,48,384]{2,1,0:T(8,128)(2,1)S(1)} %slice.9), channel_id=1, source_target_pairs={{8,7},{9,0},{10,1},{11,2},{12,3},{13,4},{14,5},{15,6},{16,15},{17,... | collective-permute-start | bytes 221192 | tf_op jit(solution)/shard_map/ppermute | solution.py:235
  25.0 9.3 %collective-permute-start.3 = (bf16[2,48,384]{2,1,0:T(8,128)(2,1)S(1)}, bf16[2,48,384]{2,1,0:T(8,128)(2,1)S(1)}, u32[]{:S(2)}, u32[]{:S(2)}) collective-permute-start(bf16[2,48,384]{2,1,0:T(8,128)(2,1)S(1)} %slice.9), channel_id=1, source_target_pairs={{0,15},{1,8},{2,9},{3,10},{4,11},{5,12},{6,13},{7,14},{8,23},{9,16... | collective-permute-start | bytes 221192 | tf_op jit(solution)/shard_map/ppermute | solution.py:234
  71.8 14.5 %all-to-all-start.2 = ((f32[8,24,384]{2,1,0:T(8,128)}), f32[8,24,384]{2,1,0:T(8,128)S(1)}, u32[]{:S(2)}, u32[]{:S(2)}) async-start(f32[8,24,384]{2,1,0:T(8,128)} %get-tuple-element.24), calls=%async_computation.2 | async-start | bytes 589824 | tf_op jit(solution)/shard_map/all_to_all | solution.py:280
  75.3 28.4 %collective-permute-start.6 = (bf16[2,180,384]{2,1,0:T(8,128)(2,1)S(1)}, bf16[2,180,384]{2,1,0:T(8,128)(2,1)S(1)}, u32[]{:S(2)}, u32[]{:S(2)}) collective-permute-start(bf16[2,180,384]{2,1,0:T(8,128)(2,1)S(1)} %get-tuple-element.23.own), channel_id=1, source_target_pairs={{8,0},{16,8},{24,16},{32,24},{40,32},{48,40},{56,48},{64,56},{72,6... | collective-permute-start | bytes 829448 | tf_op jit(solution)/shard_map/ppermute | solution.py:226
  79.7 24.0 %collective-permute-start.5 = (bf16[2,180,384]{2,1,0:T(8,128)(2,1)S(1)}, bf16[2,180,384]{2,1,0:T(8,128)(2,1)S(1)}, u32[]{:S(2)}, u32[]{:S(2)}) collective-permute-start(bf16[2,180,384]{2,1,0:T(8,128)(2,1)S(1)} %get-tuple-element.23.own), channel_id=1, source_target_pairs={{0,8},{8,16},{16,24},{24,32},{32,40},{40,48},{48,56},{56,64},{64,7... | collective-permute-start | bytes 829448 | tf_op jit(solution)/shard_map/ppermute | solution.py:225
  87.1 23.6 %all-to-all-start.3 = ((bf16[8,24,384]{2,1,0:T(8,128)(2,1)}), bf16[8,24,384]{2,1,0:T(8,128)(2,1)S(1)}, u32[]{:S(2)}, u32[]{:S(2)}) async-start(bf16[8,24,384]{2,1,0:T(8,128)(2,1)} %get-tuple-element.27), calls=%async_computation.3 | async-start | bytes 294912 | tf_op jit(solution)/shard_map/all_to_all | solution.py:280
  95.6 15.1 %collective-permute-start.7 = (bf16[2,72,384]{2,1,0:T(8,128)(2,1)S(1)}, bf16[2,72,384]{2,1,0:T(8,128)(2,1)S(1)}, u32[]{:S(2)}, u32[]{:S(2)}) collective-permute-start(bf16[2,72,384]{2,1,0:T(8,128)(2,1)S(1)} %get-tuple-element.28), channel_id=1, source_target_pairs={{0,1},{1,2},{2,3},{3,4},{4,5},{5,6},{6,7},{7,0},{8,9},{9,10},{10,1... | collective-permute-start | bytes 331784 | tf_op jit(solution)/shard_map/ppermute | solution.py:233
  98.1 8.4 %collective-permute-start.9 = (bf16[2,48,384]{2,1,0:T(8,128)(2,1)S(1)}, bf16[2,48,384]{2,1,0:T(8,128)(2,1)S(1)}, u32[]{:S(2)}, u32[]{:S(2)}) collective-permute-start(bf16[2,48,384]{2,1,0:T(8,128)(2,1)S(1)} %get-tuple-element.29), channel_id=1, source_target_pairs={{8,1},{9,2},{10,3},{11,4},{12,5},{13,6},{14,7},{15,0},{16,9},{17,1... | collective-permute-start | bytes 221192 | tf_op jit(solution)/shard_map/ppermute | solution.py:235
  100.2 10.5 %collective-permute-start.8 = (bf16[2,48,384]{2,1,0:T(8,128)(2,1)S(1)}, bf16[2,48,384]{2,1,0:T(8,128)(2,1)S(1)}, u32[]{:S(2)}, u32[]{:S(2)}) collective-permute-start(bf16[2,48,384]{2,1,0:T(8,128)(2,1)S(1)} %get-tuple-element.29), channel_id=1, source_target_pairs={{0,9},{1,10},{2,11},{3,12},{4,13},{5,14},{6,15},{7,8},{8,17},{9,18... | collective-permute-start | bytes 221192 | tf_op jit(solution)/shard_map/ppermute | solution.py:234
  111.8 21.7 %all-to-all-start.4 = ((bf16[8,192,384]{2,1,0:T(8,128)(2,1)}), bf16[8,192,384]{2,1,0:T(8,128)(2,1)}, u32[]{:S(2)}, u32[]{:S(2)}) async-start(bf16[8,192,384]{2,1,0:T(8,128)(2,1)} %get-tuple-element.38), calls=%async_computation.4 | async-start | bytes 2359296 | tf_op jit(solution)/shard_map/all_to_all | solution.py:280

commit v6 on v5

--- a/solution.py
+++ b/solution.py
@@ -21,7 +21,7 @@
 VMEM = pl.BlockSpec(memory_space=pltpu.VMEM)
 BF16, F32 = jnp.bfloat16, jnp.float32
 DP, LAT = ("x_hi", "core"), ("y", "x_lo")
-ALONG_X = ("x_hi", "core", "x_lo")
+ALONG_X = ("x_hi", "x_lo")
 
 
 def forward_taps(tables, first, rows, kcount, pos, val):
@@ -70,7 +70,7 @@
 
 
 def forward_kernel(lat_off, lon_off, basis, tap_val, tap_count, weights, own, north, south, east, ne, se, upstream,
-                   new_state, dmixed, west_out, rim_out, grad, pos, val, ext, up, z, dm, *, scale):
+                   new_state, dmixed, keep, send, pos, val, ext, up, z, dm, *, scale):
     rows, width, channels = own.shape
     kcount = weights.shape[0] // channels
     chunks = channels // LANES
@@ -114,17 +114,16 @@
         d = (up[i, :width] * slope).astype(BF16)
         new_state[i] = made
         dmixed[i] = d
-        rim_out[i] = d[width - RIM :]
-        west_out[i, :RIM] = d[width - RIM :]
-        west_out[i, RIM:] = made[width - LONREACH :]
         dm[i * ROW : (i + 1) * ROW, :] = jnp.concatenate([d, jnp.zeros((ROW - width, channels), BF16)], axis=0)
     total = lax.dot_general(z[...], dm[...], (((0,), (0,)), ((), ())), preferred_element_type=F32)
-    total = (total * scale).astype(BF16)
-    for n in range(grad.shape[0]):
-        grad[n] = total[n * grad.shape[1] : (n + 1) * grad.shape[1]]
-
-
-def forward(tables, weights, fields, upstream, scale, shares):
+    total = total * scale
+    half = keep.shape[0]
+    first = lax.axis_index("core") == 0
+    keep[...] = jnp.where(first, total[:half], total[half:])
+    send[...] = jnp.where(first, total[half:], total[:half]).astype(BF16)
+
+
+def forward(tables, weights, fields, upstream, scale):
     rows, width, channels = upstream.shape
     wide = weights.shape[0]
     lists = rows * (wide // channels) * (tables[0].shape[0] + 1)
@@ -138,12 +137,11 @@
         out_shape=[
             block,
             block,
-            jax.ShapeDtypeStruct((rows, RIM + LONREACH, channels), BF16),
-            jax.ShapeDtypeStruct((rows, RIM, channels), BF16),
-            jax.ShapeDtypeStruct((shares, wide // shares, channels), BF16),
+            jax.ShapeDtypeStruct((wide // 2, channels), F32),
+            jax.ShapeDtypeStruct((wide // 2, channels), BF16),
         ],
         in_specs=[SMEM] * 5 + [VMEM] * 8,
-        out_specs=[VMEM] * 5,
+        out_specs=[VMEM] * 4,
         scratch_shapes=[
             pltpu.SMEM((lists + 64,), jnp.int32),
             pltpu.SMEM((lists,), F32),
@@ -157,7 +155,7 @@
     )(*tables, weights, *fields, upstream)
 
 
-def backward_kernel(lat_off, lon_off, basis, tap_val, tap_count, weights, own, north, south, west, nw, sw, made, upstream,
+def backward_kernel(lat_off, lon_off, basis, tap_val, tap_count, weights, own, north, south, strip, made, upstream,
                     new_state, state_grad, pos, val, dext, dz):
     rows, width, channels = own.shape
     kcount = weights.shape[0] // channels
@@ -166,15 +164,15 @@
     tables = (lat_off, lon_off, basis, tap_val, tap_count)
     room = high * lat_off.shape[0] + 1
     backward_taps(tables, lax.axis_index(LAT) * rows, rows, pos, val)
-    for side, (mid, rim) in enumerate(((north, nw), (own, west), (south, sw))):
+    for side, (mid, at) in enumerate(((north, 0), (own, 2 * RIM), (south, RIM))):
         for r in range(rows):
             base = (side * rows + r) * EXT
-            dext[base : base + RIM, :] = rim[r, :RIM]
+            dext[base : base + RIM, :] = strip[r, at : at + RIM]
             dext[base + RIM : base + EXT, :] = jnp.concatenate(
                 [mid[r], jnp.zeros((EXT - RIM - width, channels), BF16)], axis=0
             )
     for i in range(rows):
-        new_state[i] = jnp.concatenate([west[i, RIM:], made[i, : width - LONREACH]], axis=0)
+        new_state[i] = jnp.concatenate([strip[i, 3 * RIM :], made[i, : width - LONREACH]], axis=0)
     for k in range(kcount):
         part = lax.dot_general(
             dext[...],
@@ -207,7 +205,7 @@
     return pl.pallas_call(
         backward_kernel,
         out_shape=[block, block],
-        in_specs=[SMEM] * 5 + [VMEM] * 9,
+        in_specs=[SMEM] * 5 + [VMEM] * 7,
         out_specs=[VMEM] * 2,
         scratch_shapes=[
             pltpu.SMEM((lists + 8,), jnp.int32),
@@ -227,13 +225,81 @@
     return north, south
 
 
-def lon_strips(side, rim, step):
+def lon_shift(step):
+    lons = lax.axis_size("lon")
+    return [(j, (j + step) % lons) for j in range(lons)]
+
+
+def lon_strips(side, rim):
     ends, lons = lax.axis_size(LAT) - 1, lax.axis_size("lon")
-    along = [(j, (j + step) % lons) for j in range(lons)]
+    along = lon_shift(-1)
     level = lax.ppermute(side, "lon", along)
     upper = lax.ppermute(rim, LAT + ("lon",), [(i * lons + c, (i + 1) * lons + d) for i in range(ends) for c, d in along])
     lower = lax.ppermute(rim, LAT + ("lon",), [((i + 1) * lons + c, i * lons + d) for i in range(ends) for c, d in along])
     return level, upper, lower
+
+
+def core_swap(block):
+    return lax.ppermute(block, "core", [(0, 1), (1, 0)])
+
+
+def add_halves(keep, got, copies):
+    def body(keep, got, out):
+        rows = out.shape[1]
+        total = (keep[...] + got[...].astype(F32)).astype(BF16)
+        for n in range(copies):
+            out[n] = total[n * rows : (n + 1) * rows]
+
+    return pl.pallas_call(
+        body,
+        out_shape=jax.ShapeDtypeStruct((copies, keep.shape[0] // copies, keep.shape[1]), BF16),
+        in_specs=[VMEM] * 2,
+        out_specs=VMEM,
+        compiler_params=pltpu.CompilerParams(vmem_limit_bytes=12 << 20),
+    )(keep, got)
+
+
+def join_halves(mine, other):
+    def body(mine, other, out):
+        half = mine.shape[0]
+        first = lax.axis_index("core") == 0
+        out[:half] = jnp.where(first, mine[...], other[...])
+        out[half:] = jnp.where(first, other[...], mine[...])
+
+    return pl.pallas_call(
+        body,
+        out_shape=jax.ShapeDtypeStruct((2 * mine.shape[0], mine.shape[1]), BF16),
+        in_specs=[VMEM] * 2,
+        out_specs=VMEM,
+        compiler_params=pltpu.CompilerParams(vmem_limit_bytes=12 << 20),
+    )(mine, other)
+
+
+def sum_and_strip(pieces, copies, dmixed, north, south, made):
+    def body(part, dmixed, north, south, made, out, strip):
+        total = part[0]
+        for n in range(1, part.shape[0]):
+            total = total + part[n]
+        total = total.astype(out.dtype)
+        for n in range(copies):
+            out[n] = total
+        rows, width, _ = dmixed.shape
+        for r in range(rows):
+            for n, source in enumerate((north, south, dmixed)):
+                strip[r, n * RIM : (n + 1) * RIM] = source[r, width - RIM :]
+            strip[r, 3 * RIM :] = made[r, width - LONREACH :]
+
+    rows, _, channels = dmixed.shape
+    return pl.pallas_call(
+        body,
+        out_shape=[
+            jax.ShapeDtypeStruct((copies, *pieces.shape[1:]), BF16),
+            jax.ShapeDtypeStruct((rows, 3 * RIM + LONREACH, channels), BF16),
+        ],
+        in_specs=[VMEM] * 5,
+        out_specs=[VMEM] * 2,
+        compiler_params=pltpu.CompilerParams(vmem_limit_bytes=12 << 20),
+    )(pieces, dmixed, north, south, made)
 
 
 def sum_pieces(pieces, out_shape, passed=()):
@@ -276,6 +342,21 @@
     )(block, *passed)
 
 
+def after(*arrays):
+    def body(*refs):
+        pass
+
+    anywhere = pl.BlockSpec(memory_space=pl.ANY)
+    return pl.pallas_call(
+        body,
+        out_shape=[jax.ShapeDtypeStruct(x.shape, x.dtype) for x in arrays],
+        in_specs=[anywhere] * len(arrays),
+        out_specs=[anywhere] * len(arrays),
+        input_output_aliases={n: n for n in range(len(arrays))},
+        compiler_params=pltpu.CompilerParams(vmem_limit_bytes=1 << 20),
+    )(*arrays)
+
+
 def exchange(pieces, axes):
     return lax.all_to_all(pieces, axes, 0, 0, tiled=True)
 
@@ -287,23 +368,25 @@
     wide = weights.reshape(-1, channels)
     tables = (lat_off.T, lon_off.T, basis.T, tap_val.T, tap_count)
     side = jnp.concatenate([field[:, :RIM], upstream[:, :LONREACH]], axis=1)
-    fields = (field, *lat_blocks(field), *lon_strips(side, field[:, :RIM], -1))
+    fields = (field, *lat_blocks(field), *lon_strips(side, field[:, :RIM]))
     cells = lax.axis_size(DP) * lax.axis_size(LAT) * rows * lax.axis_size("lon") * width
     nx, ny, nz = lax.axis_size(ALONG_X), lax.axis_size("y"), lax.axis_size("lon")
-    made, dmixed, side, rim, share = forward(tables, wide, fields, upstream, 1.0 / math.sqrt(cells), nx)
-    piece = (wide.shape[0] // (nx * ny), channels)
-    got = exchange(share, ALONG_X)
-    (part,) = sum_pieces(got, jax.ShapeDtypeStruct((ny, *piece), BF16))
+    made, dmixed, keep, send = forward(tables, wide, fields, upstream, 1.0 / math.sqrt(cells))
+    piece = (keep.shape[0] // (nx * ny), channels)
+    got = exchange(add_halves(keep, core_swap(send), nx), ALONG_X)
+    part, dmixed = sum_pieces(got, jax.ShapeDtypeStruct((ny, *piece), BF16), (dmixed,))
+    north, south = lat_blocks(dmixed)
     got = exchange(part, "y")
-    part, dmixed = sum_pieces(got, jax.ShapeDtypeStruct((nz, *piece), F32), (dmixed,))
-    blocks = lat_blocks(dmixed)
+    (part,) = sum_pieces(got, jax.ShapeDtypeStruct((nz, *piece), F32))
     got = exchange(part, "lon")
-    part, side, rim = sum_pieces(got, jax.ShapeDtypeStruct((ny, *piece), BF16), (side, rim))
-    strips = lon_strips(side, rim, 1)
+    part, strip = sum_and_strip(got, ny, dmixed, north, south, made)
+    strip = lax.ppermute(strip, "lon", lon_shift(1))
     got = exchange(part, "y")
-    part, *near = spread(got.reshape(-1, channels), nx, (*blocks, *strips))
-    weight_grad = exchange(part, ALONG_X).reshape(weights.shape)
-    new_field, field_grad = backward(tables, wide, (dmixed, *near), made, upstream)
+    part, strip = spread(got.reshape(-1, channels), nx, (strip,))
+    mine = exchange(part, ALONG_X).reshape(-1, channels)
+    new_field, field_grad = backward(tables, wide, (dmixed, north, south, strip), made, upstream)
+    mine, new_field, field_grad = after(mine, new_field, field_grad)
+    weight_grad = join_halves(mine, core_swap(mine)).reshape(weights.shape)
     return new_field[None], field_grad[None], weight_grad
 
 

time: 137 us -> 127 us (0.927)
  the two profiles are of different devices: /device:TPU:32 before, /device:TPU:1 now
where the time goes in v6:
time: 127 us
  starting transfers between devices  51.5 us (41%)
  blocking collectives  35 us (28%)
  waiting for transfers between devices  22 us (17%)
  Pallas kernels  11.9 us (9%)
  local copies, waits for them, and re-layouts  5.23 us (4%)
    all_to_all x2, blocking collectives, exchange(): return lax.all_to_all(pieces, axes, 0, 0, tiled=True)  35 us
    all_to_all x3, starting transfers between devices, exchange(): return lax.all_to_all(pieces, axes, 0, 0, tiled=True)  11.1 us
    ppermute x1, starting transfers between devices, lon_strips(): level = lax.ppermute(side, 'lon', along)  10.9 us
    ppermute x2, starting transfers between devices, core_swap(): return lax.ppermute(block, 'core', [(0, 1), (1, 0)])  9.45 us
    ppermute x2, starting transfers between devices, lat_blocks(): north = lax.ppermute(block, LAT, [(i, i + 1) for i in range(ends)])  8.59 us
    ppermute x2, waiting for transfers between devices, lat_blocks(): north = lax.ppermute(block, LAT, [(i, i + 1) for i in range(ends)])  7.59 us
    all_to_all x3, waiting for transfers between devices, exchange(): return lax.all_to_all(pieces, axes, 0, 0, tiled=True)  7.22 us
    unnamed x18, local copies, waits for them, and re-layouts  5.21 us
  transfers between devices with their start and end apart: 13, of which 8 were waited for; matrix products, arithmetic and copies ran while one was open for 2% of the time, Pallas kernels for 3%

profile of v6, /device:TPU:1, one launch (start us, length us, event | category | flops | bytes accessed | tf_op | source)
XLA Modules:
  0.0 126.5 jit_solution(6514661231349763486)
XLA Ops:
  1.8 1.3 %collective-permute-start.1 = (bf16[2,180,384]{2,1,0:T(8,128)(2,1)S(1)}, bf16[2,180,384]{2,1,0:T(8,128)(2,1)S(1)}, u32[]{:S(2)}, u32[]{:S(2)}) collective-permute-start(bf16[2,180,384]{2,1,0:T(8,128)(2,1)S(1)} %bitcast.20), channel_id=1, source_target_pairs={{8,0},{16,8},{24,16},{32,24},{40,32},{48,40},{56,48},{64,56},{72,6... | collective-permute-start | bytes 829448 | tf_op jit(solution)/shard_map/ppermute | solution.py:224
  3.1 4.6 %collective-permute-start = (bf16[2,180,384]{2,1,0:T(8,128)(2,1)S(1)}, bf16[2,180,384]{2,1,0:T(8,128)(2,1)S(1)}, u32[]{:S(2)}, u32[]{:S(2)}) collective-permute-start(bf16[2,180,384]{2,1,0:T(8,128)(2,1)S(1)} %bitcast.21), channel_id=1, source_target_pairs={{0,8},{8,16},{16,24},{24,32},{32,40},{40,48},{48,56},{56,64},{64,7... | collective-permute-start | bytes 829448 | tf_op jit(solution)/shard_map/ppermute | solution.py:223
  8.7 10.9 %collective-permute-start.2 = (bf16[2,72,384]{2,1,0:T(8,128)(2,1)S(1)}, bf16[2,72,384]{2,1,0:T(8,128)(2,1)S(1)}, u32[]{:S(2)}, u32[]{:S(2)}) collective-permute-start(bf16[2,72,384]{2,1,0:T(8,128)(2,1)S(1)} %pad_maximum_fusion), channel_id=1, source_target_pairs={{0,7},{1,0},{2,1},{3,2},{4,3},{5,4},{6,5},{7,6},{8,15},{9,8},{10,9... | collective-permute-start | bytes 331784 | tf_op jit(solution)/shard_map/ppermute | solution.py:236
  19.6 1.3 %collective-permute-start.4 = (bf16[2,48,384]{2,1,0:T(8,128)(2,1)S(1)}, bf16[2,48,384]{2,1,0:T(8,128)(2,1)S(1)}, u32[]{:S(2)}, u32[]{:S(2)}) collective-permute-start(bf16[2,48,384]{2,1,0:T(8,128)(2,1)S(1)} %slice.9), channel_id=1, source_target_pairs={{8,7},{9,0},{10,1},{11,2},{12,3},{13,4},{14,5},{15,6},{16,15},{17,... | collective-permute-start | bytes 221192 | tf_op jit(solution)/shard_map/ppermute | solution.py:238
  20.9 4.6 %collective-permute-start.3 = (bf16[2,48,384]{2,1,0:T(8,128)(2,1)S(1)}, bf16[2,48,384]{2,1,0:T(8,128)(2,1)S(1)}, u32[]{:S(2)}, u32[]{:S(2)}) collective-permute-start(bf16[2,48,384]{2,1,0:T(8,128)(2,1)S(1)} %slice.9), channel_id=1, source_target_pairs={{0,15},{1,8},{2,9},{3,10},{4,11},{5,12},{6,13},{7,14},{8,23},{9,16... | collective-permute-start | bytes 221192 | tf_op jit(solution)/shard_map/ppermute | solution.py:237
  25.6 1.3 %collective-permute-done.3.refs_10_ = bf16[2,48,384]{2,1,0:T(8,128)(2,1)S(1)} collective-permute-done((bf16[2,48,384]{2,1,0:T(8,128)(2,1)S(1)}, bf16[2,48,384]{2,1,0:T(8,128)(2,1)S(1)}, u32[]{:S(2)}, u32[]{:S(2)}) %collective-permute-start.3) | collective-permute-done | bytes 73760 | tf_op jit(solution)/shard_map/ppermute | solution.py:237
  27.0 3.9 %shard_map.103 = (bf16[2,180,384]{2,1,0:T(8,128)(2,1)S(1)}, bf16[2,180,384]{2,1,0:T(8,128)(2,1)S(1)}, f32[768,384]{1,0:T(8,128)S(1)}, bf16[768,384]{1,0:T(8,128)(2,1)S(1)}) custom-call(s32[16,32]{1,0:T(8,128)S(1)} %bitcast.29, s32[16,32]{1,0:T(8,128)S(1)} %bitcast.31, s32[16,32]{1,0:T(8,128)S(1)} %bitcast.33, f32[16,32]{1,0:T(8,128)S(1)} %bitcast.35, ...), custom_call_target="tpu_custom_call" | custom-call | flops 2000000000 | bytes 8000000 | tf_op jit(solution)/shard_map/pallas_call | solution.py:135
  31.0 4.3 %collective-permute-start.5 = (bf16[768,384]{1,0:T(8,128)(2,1)S(1)}, bf16[768,384]{1,0:T(8,128)(2,1)S(1)}, u32[]{:S(2)}, u32[]{:S(2)}) collective-permute-start(bf16[768,384]{1,0:T(8,128)(2,1)S(1)} %get-tuple-element.19), channel_id=1, source_target_pairs={{0,128},{128,0},{1,129},{129,1},{2,130},{130,2},{3,131},{131,3},{4... | collective-permute-start | bytes 1769480 | tf_op jit(solution)/shard_map/ppermute | solution.py:243
  35.3 1.6 %collective-permute-done.5.got = bf16[768,384]{1,0:T(8,128)(2,1)S(1)} collective-permute-done((bf16[768,384]{1,0:T(8,128)(2,1)S(1)}, bf16[768,384]{1,0:T(8,128)(2,1)S(1)}, u32[]{:S(2)}, u32[]{:S(2)}) %collective-permute-start.5) | collective-permute-done | bytes 589856 | tf_op jit(solution)/shard_map/ppermute | solution.py:243
  37.0 15.2 %all_to_all.25.refs_0_ = bf16[4,192,384]{2,1,0:T(8,128)(2,1)S(1)} all-to-all(bf16[4,192,384]{2,1,0:T(8,128)(2,1)S(1)} %shard_map.104), channel_id=1, replica_groups=mesh['x_hi'=2,'core'=2,'y'=8,'x_lo'=2,'lon'=8] {'x_hi','x_lo'}, dimensions={0} | all-to-all | bytes 1179648 | tf_op jit(solution)/shard_map/all_to_all | solution.py:361
  52.3 19.8 %all_to_all.26.refs_0_ = bf16[8,24,384]{2,1,0:T(8,128)(2,1)S(1)} all-to-all(bf16[8,24,384]{2,1,0:T(8,128)(2,1)S(1)} %get-tuple-element.21), channel_id=1, replica_groups=mesh['x_hi'=2,'core'=2,'y'=8,'x_lo'=2,'lon'=8] {'y'}, dimensions={0} | all-to-all | bytes 294912 | tf_op jit(solution)/shard_map/all_to_all | solution.py:361
  72.8 3.4 %all-to-all-start.2 = ((f32[8,24,384]{2,1,0:T(8,128)}), f32[8,24,384]{2,1,0:T(8,128)S(1)}, u32[]{:S(2)}, u32[]{:S(2)}) async-start(f32[8,24,384]{2,1,0:T(8,128)} %shard_map.106), calls=%async_computation.2 | async-start | bytes 589824 | tf_op jit(solution)/shard_map/all_to_all | solution.py:361
  76.3 1.3 %collective-permute-start.7 = (bf16[2,180,384]{2,1,0:T(8,128)(2,1)S(1)}, bf16[2,180,384]{2,1,0:T(8,128)(2,1)S(1)}, u32[]{:S(2)}, u32[]{:S(2)}) collective-permute-start(bf16[2,180,384]{2,1,0:T(8,128)(2,1)S(1)} %get-tuple-element.22.dmixed.own), channel_id=1, source_target_pairs={{8,0},{16,8},{24,16},{32,24},{40,32},{48,40},{56,48},{64,56},{72,6... | collective-permute-start | bytes 829448 | tf_op jit(solution)/shard_map/ppermute | solution.py:224
  77.6 4.0 %collective-permute-start.6 = (bf16[2,180,384]{2,1,0:T(8,128)(2,1)S(1)}, bf16[2,180,384]{2,1,0:T(8,128)(2,1)S(1)}, u32[]{:S(2)}, u32[]{:S(2)}) collective-permute-start(bf16[2,180,384]{2,1,0:T(8,128)(2,1)S(1)} %get-tuple-element.22.dmixed.own), channel_id=1, source_target_pairs={{0,8},{8,16},{16,24},{24,32},{32,40},{40,48},{48,56},{56,64},{64,7... | collective-permute-start | bytes 829448 | tf_op jit(solution)/shard_map/ppermute | solution.py:223
  81.6 2.3 %collective-permute-done.7.south = bf16[2,180,384]{2,1,0:T(8,128)(2,1)S(1)} collective-permute-done((bf16[2,180,384]{2,1,0:T(8,128)(2,1)S(1)}, bf16[2,180,384]{2,1,0:T(8,128)(2,1)S(1)}, u32[]{:S(2)}, u32[]{:S(2)}) %collective-permute-start.7) | collective-permute-done | bytes 276512 | tf_op jit(solution)/shard_map/ppermute | solution.py:224
  83.9 7.6 %collective-permute-done.6.north = bf16[2,180,384]{2,1,0:T(8,128)(2,1)S(1)} collective-permute-done((bf16[2,180,384]{2,1,0:T(8,128)(2,1)S(1)}, bf16[2,180,384]{2,1,0:T(8,128)(2,1)S(1)}, u32[]{:S(2)}, u32[]{:S(2)}) %collective-permute-start.6) | collective-permute-done | bytes 276512 | tf_op jit(solution)/shard_map/ppermute | solution.py:223
  92.2 3.4 %all-to-all-start.3 = ((bf16[8,24,384]{2,1,0:T(8,128)(2,1)}), bf16[8,24,384]{2,1,0:T(8,128)(2,1)S(1)}, u32[]{:S(2)}, u32[]{:S(2)}) async-start(bf16[8,24,384]{2,1,0:T(8,128)(2,1)} %get-tuple-element.24), calls=%async_computation.3 | async-start | bytes 294912 | tf_op jit(solution)/shard_map/all_to_all | solution.py:361
  95.6 2.9 %collective-permute-start.8 = (bf16[2,168,384]{2,1,0:T(8,128)(2,1)S(1)}, bf16[2,168,384]{2,1,0:T(8,128)(2,1)S(1)}, u32[]{:S(2)}, u32[]{:S(2)}) collective-permute-start(bf16[2,168,384]{2,1,0:T(8,128)(2,1)S(1)} %get-tuple-element.25), channel_id=1, source_target_pairs={{0,1},{1,2},{2,3},{3,4},{4,5},{5,6},{6,7},{7,0},{8,9},{9,10},{10,1... | collective-permute-start | bytes 774152 | tf_op jit(solution)/shard_map/ppermute | solution.py:383
  98.5 4.9 %all-to-all-done.3 = bf16[8,24,384]{2,1,0:T(8,128)(2,1)S(1)} async-done(((bf16[8,24,384]{2,1,0:T(8,128)(2,1)}), bf16[8,24,384]{2,1,0:T(8,128)(2,1)S(1)}, u32[]{:S(2)}, u32[]{:S(2)}) %all-to-all-start.3) | async-done | bytes 147488 | tf_op jit(solution)/shard_map/all_to_all | solution.py:361
  103.4 1.9 %collective-permute-done.8.refs_1_ = bf16[2,168,384]{2,1,0:T(8,128)(2,1)S(1)} collective-permute-done((bf16[2,168,384]{2,1,0:T(8,128)(2,1)S(1)}, bf16[2,168,384]{2,1,0:T(8,128)(2,1)S(1)}, u32[]{:S(2)}, u32[]{:S(2)}) %collective-permute-start.8) | collective-permute-done | bytes 258080 | tf_op jit(solution)/shard_map/ppermute | solution.py:383
  106.2 4.3 %all-to-all-start.4 = ((bf16[4,192,384]{2,1,0:T(8,128)(2,1)}), bf16[4,192,384]{2,1,0:T(8,128)(2,1)S(1)}, u32[]{:S(2)}, u32[]{:S(2)}) async-start(bf16[4,192,384]{2,1,0:T(8,128)(2,1)} %get-tuple-element.26), calls=%async_computation.4 | async-start | bytes 1179648 | tf_op jit(solution)/shard_map/all_to_all | solution.py:361
  111.7 4.2 %shard_map.109 = (bf16[2,180,384]{2,1,0:T(8,128)(2,1)S(1)}, bf16[2,180,384]{2,1,0:T(8,128)(2,1)S(1)}) custom-call(s32[16,32]{1,0:T(8,128)S(1)} %bitcast.30, s32[16,32]{1,0:T(8,128)S(1)} %bitcast.32, s32[16,32]{1,0:T(8,128)S(1)} %bitcast.34, f32[16,32]{1,0:T(8,128)S(1)} %bitcast.36, s32[32]{0:T(128)S(1)} %copy-done.6, bf16[1536,384]{1,0:T(8,128)(2,1)S(1)} %bitcast.28, ...), custom_call_target="tpu_custom_call" | custom-call | flops 2500000000 | bytes 5000000 | tf_op jit(solution)/shard_map/pallas_call | solution.py:205
  116.0 2.3 %all-to-all-done.4 = bf16[4,192,384]{2,1,0:T(8,128)(2,1)S(1)} async-done(((bf16[4,192,384]{2,1,0:T(8,128)(2,1)}), bf16[4,192,384]{2,1,0:T(8,128)(2,1)S(1)}, u32[]{:S(2)}, u32[]{:S(2)}) %all-to-all-start.4) | async-done | bytes 589856 | tf_op jit(solution)/shard_map/all_to_all | solution.py:361
  118.3 5.2 %collective-permute-start.9 = (bf16[768,384]{1,0:T(8,128)(2,1)S(1)}, bf16[768,384]{1,0:T(8,128)(2,1)S(1)}, u32[]{:S(2)}, u32[]{:S(2)}) collective-permute-start(bf16[768,384]{1,0:T(8,128)(2,1)S(1)} %get-tuple-element.32.mine), channel_id=1, source_target_pairs={{0,128},{128,0},{1,129},{129,1},{2,130},{130,2},{3,131},{131,3},{4... | collective-permute-start | bytes 1769480 | tf_op jit(solution)/shard_map/ppermute | solution.py:243
  (34 shorter events, 9.0 us)
Async XLA Ops:
  0.6 26.3 %copy-start.6 = (s32[32]{0:T(128)S(1)}, s32[32]{0:T(128)}, u32[]{:S(2)}) copy-start(s32[32]{0:T(128)} %tap_count.1) | copy-start | bytes 388
  0.6 26.3 %copy-start.5 = (f32[32,16]{0,1:T(8,128)S(1)}, f32[32,16]{0,1:T(8,128)}, u32[]{:S(2)}) copy-start(f32[32,16]{0,1:T(8,128)} %param.14) | copy-start | bytes 6148
  0.7 26.3 %copy-start.4 = (s32[32,16]{0,1:T(8,128)S(1)}, s32[32,16]{0,1:T(8,128)}, u32[]{:S(2)}) copy-start(s32[32,16]{0,1:T(8,128)} %param.13) | copy-start | bytes 6148
  0.7 26.3 %copy-start.3 = (s32[32,16]{0,1:T(8,128)S(1)}, s32[32,16]{0,1:T(8,128)}, u32[]{:S(2)}) copy-start(s32[32,16]{0,1:T(8,128)} %param.12) | copy-start | bytes 6148
  0.7 26.3 %copy-start.2 = (s32[32,16]{0,1:T(8,128)S(1)}, s32[32,16]{0,1:T(8,128)}, u32[]{:S(2)}) copy-start(s32[32,16]{0,1:T(8,128)} %param.11) | copy-start | bytes 6148
  0.7 26.3 %copy-start = (bf16[4,384,384]{2,1,0:T(8,128)(2,1)S(1)}, bf16[4,384,384]{2,1,0:T(8,128)(2,1)}, u32[]{:S(2)}) copy-start(bf16[4,384,384]{2,1,0:T(8,128)(2,1)} %param.10) | copy-start | bytes 3538948
  1.8 25.2 %collective-permute-start.1 = (bf16[2,180,384]{2,1,0:T(8,128)(2,1)S(1)}, bf16[2,180,384]{2,1,0:T(8,128)(2,1)S(1)}, u32[]{:S(2)}, u32[]{:S(2)}) collective-permute-start(bf16[2,180,384]{2,1,0:T(8,128)(2,1)S(1)} %bitcast.20), channel_id=1, source_target_pairs={{8,0},{16,8},{24,16},{32,24},{40,32},{48,40},{56,48},{64,56},{72,6... | collective-permute-start | bytes 829448 | tf_op jit(solution)/shard_map/ppermute | solution.py:224
  3.1 23.9 %collective-permute-start = (bf16[2,180,384]{2,1,0:T(8,128)(2,1)S(1)}, bf16[2,180,384]{2,1,0:T(8,128)(2,1)S(1)}, u32[]{:S(2)}, u32[]{:S(2)}) collective-permute-start(bf16[2,180,384]{2,1,0:T(8,128)(2,1)S(1)} %bitcast.21), channel_id=1, source_target_pairs={{0,8},{8,16},{16,24},{24,32},{32,40},{40,48},{48,56},{56,64},{64,7... | collective-permute-start | bytes 829448 | tf_op jit(solution)/shard_map/ppermute | solution.py:223
  8.7 18.2 %collective-permute-start.2 = (bf16[2,72,384]{2,1,0:T(8,128)(2,1)S(1)}, bf16[2,72,384]{2,1,0:T(8,128)(2,1)S(1)}, u32[]{:S(2)}, u32[]{:S(2)}) collective-permute-start(bf16[2,72,384]{2,1,0:T(8,128)(2,1)S(1)} %pad_maximum_fusion), channel_id=1, source_target_pairs={{0,7},{1,0},{2,1},{3,2},{4,3},{5,4},{6,5},{7,6},{8,15},{9,8},{10,9... | collective-permute-start | bytes 331784 | tf_op jit(solution)/shard_map/ppermute | solution.py:236
  19.6 6.0 %collective-permute-start.4 = (bf16[2,48,384]{2,1,0:T(8,128)(2,1)S(1)}, bf16[2,48,384]{2,1,0:T(8,128)(2,1)S(1)}, u32[]{:S(2)}, u32[]{:S(2)}) collective-permute-start(bf16[2,48,384]{2,1,0:T(8,128)(2,1)S(1)} %slice.9), channel_id=1, source_target_pairs={{8,7},{9,0},{10,1},{11,2},{12,3},{13,4},{14,5},{15,6},{16,15},{17,... | collective-permute-start | bytes 221192 | tf_op jit(solution)/shard_map/ppermute | solution.py:238
  20.9 6.0 %collective-permute-start.3 = (bf16[2,48,384]{2,1,0:T(8,128)(2,1)S(1)}, bf16[2,48,384]{2,1,0:T(8,128)(2,1)S(1)}, u32[]{:S(2)}, u32[]{:S(2)}) collective-permute-start(bf16[2,48,384]{2,1,0:T(8,128)(2,1)S(1)} %slice.9), channel_id=1, source_target_pairs={{0,15},{1,8},{2,9},{3,10},{4,11},{5,12},{6,13},{7,14},{8,23},{9,16... | collective-permute-start | bytes 221192 | tf_op jit(solution)/shard_map/ppermute | solution.py:237
  31.0 5.9 %collective-permute-start.5 = (bf16[768,384]{1,0:T(8,128)(2,1)S(1)}, bf16[768,384]{1,0:T(8,128)(2,1)S(1)}, u32[]{:S(2)}, u32[]{:S(2)}) collective-permute-start(bf16[768,384]{1,0:T(8,128)(2,1)S(1)} %get-tuple-element.19), channel_id=1, source_target_pairs={{0,128},{128,0},{1,129},{129,1},{2,130},{130,2},{3,131},{131,3},{4... | collective-permute-start | bytes 1769480 | tf_op jit(solution)/shard_map/ppermute | solution.py:243
  72.8 18.6 %all-to-all-start.2 = ((f32[8,24,384]{2,1,0:T(8,128)}), f32[8,24,384]{2,1,0:T(8,128)S(1)}, u32[]{:S(2)}, u32[]{:S(2)}) async-start(f32[8,24,384]{2,1,0:T(8,128)} %shard_map.106), calls=%async_computation.2 | async-start | bytes 589824 | tf_op jit(solution)/shard_map/all_to_all | solution.py:361
  76.3 7.6 %collective-permute-start.7 = (bf16[2,180,384]{2,1,0:T(8,128)(2,1)S(1)}, bf16[2,180,384]{2,1,0:T(8,128)(2,1)S(1)}, u32[]{:S(2)}, u32[]{:S(2)}) collective-permute-start(bf16[2,180,384]{2,1,0:T(8,128)(2,1)S(1)} %get-tuple-element.22.dmixed.own), channel_id=1, source_target_pairs={{8,0},{16,8},{24,16},{32,24},{40,32},{48,40},{56,48},{64,56},{72,6... | collective-permute-start | bytes 829448 | tf_op jit(solution)/shard_map/ppermute | solution.py:224
  77.6 13.9 %collective-permute-start.6 = (bf16[2,180,384]{2,1,0:T(8,128)(2,1)S(1)}, bf16[2,180,384]{2,1,0:T(8,128)(2,1)S(1)}, u32[]{:S(2)}, u32[]{:S(2)}) collective-permute-start(bf16[2,180,384]{2,1,0:T(8,128)(2,1)S(1)} %get-tuple-element.22.dmixed.own), channel_id=1, source_target_pairs={{0,8},{8,16},{16,24},{24,32},{32,40},{40,48},{48,56},{56,64},{64,7... | collective-permute-start | bytes 829448 | tf_op jit(solution)/shard_map/ppermute | solution.py:223
  92.2 11.2 %all-to-all-start.3 = ((bf16[8,24,384]{2,1,0:T(8,128)(2,1)}), bf16[8,24,384]{2,1,0:T(8,128)(2,1)S(1)}, u32[]{:S(2)}, u32[]{:S(2)}) async-start(bf16[8,24,384]{2,1,0:T(8,128)(2,1)} %get-tuple-element.24), calls=%async_computation.3 | async-start | bytes 294912 | tf_op jit(solution)/shard_map/all_to_all | solution.py:361
  95.6 9.7 %collective-permute-start.8 = (bf16[2,168,384]{2,1,0:T(8,128)(2,1)S(1)}, bf16[2,168,384]{2,1,0:T(8,128)(2,1)S(1)}, u32[]{:S(2)}, u32[]{:S(2)}) collective-permute-start(bf16[2,168,384]{2,1,0:T(8,128)(2,1)S(1)} %get-tuple-element.25), channel_id=1, source_target_pairs={{0,1},{1,2},{2,3},{3,4},{4,5},{5,6},{6,7},{7,0},{8,9},{9,10},{10,1... | collective-permute-start | bytes 774152 | tf_op jit(solution)/shard_map/ppermute | solution.py:383
  106.2 12.2 %all-to-all-start.4 = ((bf16[4,192,384]{2,1,0:T(8,128)(2,1)}), bf16[4,192,384]{2,1,0:T(8,128)(2,1)S(1)}, u32[]{:S(2)}, u32[]{:S(2)}) async-start(bf16[4,192,384]{2,1,0:T(8,128)(2,1)} %get-tuple-element.26), calls=%async_computation.4 | async-start | bytes 1179648 | tf_op jit(solution)/shard_map/all_to_all | solution.py:361
  110.5 1.3 %copy-start.1 = (bf16[4,384,384]{2,1,0:T(8,128)(2,1)S(1)}, bf16[4,384,384]{2,1,0:T(8,128)(2,1)}, u32[]{:S(2)}) copy-start(bf16[4,384,384]{2,1,0:T(8,128)(2,1)} %param.10) | copy-start | bytes 3538948
  118.3 7.0 %collective-permute-start.9 = (bf16[768,384]{1,0:T(8,128)(2,1)S(1)}, bf16[768,384]{1,0:T(8,128)(2,1)S(1)}, u32[]{:S(2)}, u32[]{:S(2)}) collective-permute-start(bf16[768,384]{1,0:T(8,128)(2,1)S(1)} %get-tuple-element.32.mine), channel_id=1, source_target_pairs={{0,128},{128,0},{1,129},{129,1},{2,130},{130,2},{3,131},{131,3},{4... | collective-permute-start | bytes 1769480 | tf_op jit(solution)/shard_map/ppermute | solution.py:243

commit v7 on v6

--- a/solution.py
+++ b/solution.py
@@ -218,11 +218,12 @@
     )(*tables, weights, *fields, made, upstream)
 
 
-def lat_blocks(block):
-    ends = lax.axis_size(LAT) - 1
-    north = lax.ppermute(block, LAT, [(i, i + 1) for i in range(ends)])
-    south = lax.ppermute(block, LAT, [(i + 1, i) for i in range(ends)])
-    return north, south
+def from_north(block):
+    return lax.ppermute(block, LAT, [(i, i + 1) for i in range(lax.axis_size(LAT) - 1)])
+
+
+def from_south(block):
+    return lax.ppermute(block, LAT, [(i + 1, i) for i in range(lax.axis_size(LAT) - 1)])
 
 
 def lon_shift(step):
@@ -368,21 +369,22 @@
     wide = weights.reshape(-1, channels)
     tables = (lat_off.T, lon_off.T, basis.T, tap_val.T, tap_count)
     side = jnp.concatenate([field[:, :RIM], upstream[:, :LONREACH]], axis=1)
-    fields = (field, *lat_blocks(field), *lon_strips(side, field[:, :RIM]))
+    fields = (field, from_north(field), from_south(field), *lon_strips(side, field[:, :RIM]))
     cells = lax.axis_size(DP) * lax.axis_size(LAT) * rows * lax.axis_size("lon") * width
     nx, ny, nz = lax.axis_size(ALONG_X), lax.axis_size("y"), lax.axis_size("lon")
     made, dmixed, keep, send = forward(tables, wide, fields, upstream, 1.0 / math.sqrt(cells))
     piece = (keep.shape[0] // (nx * ny), channels)
     got = exchange(add_halves(keep, core_swap(send), nx), ALONG_X)
-    part, dmixed = sum_pieces(got, jax.ShapeDtypeStruct((ny, *piece), BF16), (dmixed,))
-    north, south = lat_blocks(dmixed)
+    part, dmixed = sum_pieces(got, jax.ShapeDtypeStruct((ny, *piece), F32), (dmixed,))
+    north = from_north(dmixed)
     got = exchange(part, "y")
-    (part,) = sum_pieces(got, jax.ShapeDtypeStruct((nz, *piece), F32))
+    part, north, dmixed = sum_pieces(got, jax.ShapeDtypeStruct((nz, *piece), F32), (north, dmixed))
+    south = from_south(dmixed)
     got = exchange(part, "lon")
     part, strip = sum_and_strip(got, ny, dmixed, north, south, made)
     strip = lax.ppermute(strip, "lon", lon_shift(1))
     got = exchange(part, "y")
-    part, strip = spread(got.reshape(-1, channels), nx, (strip,))
+    part, made = spread(got.reshape(-1, channels), nx, (made,))
     mine = exchange(part, ALONG_X).reshape(-1, channels)
     new_field, field_grad = backward(tables, wide, (dmixed, north, south, strip), made, upstream)
     mine, new_field, field_grad = after(mine, new_field, field_grad)

time: 127 us -> 131 us (1.031)
  blocking collectives: 35 us -> 15 us
  starting transfers between devices: 51.5 us -> 68.9 us
  waiting for transfers between devices: 22 us -> 27.4 us
    all_to_all x2 -> x1, blocking collectives: 35 us -> 15 us  [exchange(): return lax.all_to_all(pieces, axes, 0, 0, tiled=True)]
    all_to_all x3 -> x4, starting transfers between devices: 11.1 us -> 29.2 us  [exchange(): return lax.all_to_all(pieces, axes, 0, 0, tiled=True)]
    all_to_all x3 -> x4, waiting for transfers between devices: 7.22 us -> 11.9 us  [exchange(): return lax.all_to_all(pieces, axes, 0, 0, tiled=True)]
    ppermute x4, waiting for transfers between devices: 9.91 us -> 12.6 us  [the longest x2 8.36 us: from_south(): lax.ppermute(block, LAT, [(i + 1, i) for i in range(lax.axis_size(LAT) -...]
    ppermute x2, starting transfers between devices: 9.45 us -> 11.6 us  [core_swap(): return lax.ppermute(block, 'core', [(0, 1), (1, 0)])]
    ppermute x1, waiting for transfers between devices: 1.91 us -> 0.01 us  [shards(): strip = lax.ppermute(strip, 'lon', lon_shift(1))]
    ppermute x4, starting transfers between devices: 11.2 us -> 9.37 us  [the longest x2 6.78 us: from_north(): lax.ppermute(block, LAT, [(i, i + 1) for i in range(lax.axis_size(LAT) -...]
  transfers between devices with their start and end apart: 13 -> 14, of which waited for: 8 -> 8; matrix products, arithmetic and copies ran while one was open for 2% -> 2% of each run, Pallas kernels for 3% -> 4%
where the time goes in v7:
time: 131 us; the launch traced here: 130 us
  starting transfers between devices  68.9 us (53%)
  waiting for transfers between devices  27.4 us (21%)
  blocking collectives  15 us (11%)
  Pallas kernels  12.7 us (10%)
  local copies, waits for them, and re-layouts  5.23 us (4%)
    all_to_all x4, starting transfers between devices, exchange(): return lax.all_to_all(pieces, axes, 0, 0, tiled=True)  29.2 us
    all_to_all x1, blocking collectives, exchange(): return lax.all_to_all(pieces, axes, 0, 0, tiled=True)  15 us
    all_to_all x4, waiting for transfers between devices, exchange(): return lax.all_to_all(pieces, axes, 0, 0, tiled=True)  11.9 us
    ppermute x2, starting transfers between devices, core_swap(): return lax.ppermute(block, 'core', [(0, 1), (1, 0)])  11.6 us
    ppermute x1, starting transfers between devices, lon_strips(): level = lax.ppermute(side, 'lon', along)  10.9 us
    ppermute x2, waiting for transfers between devices, from_south(): lax.ppermute(block, LAT, [(i + 1, i) for i in range(lax.axis_size(LAT) -...  8.36 us
    ppermute x2, starting transfers between devices, from_north(): lax.ppermute(block, LAT, [(i, i + 1) for i in range(lax.axis_size(LAT) -...  6.78 us
    unnamed x18, local copies, waits for them, and re-layouts  5.21 us
  transfers between devices with their start and end apart: 14, of which 8 were waited for; matrix products, arithmetic and copies ran while one was open for 2% of the time, Pallas kernels for 4%

profile of v7, /device:TPU:1, one launch (start us, length us, event | category | flops | bytes accessed | tf_op | source)
XLA Modules:
  0.0 130.1 jit_solution(2758608755021326410)
XLA Ops:
  1.8 1.3 collective-permute-start.1
  3.1 4.6 %collective-permute-start = (bf16[2,180,384]{2,1,0:T(8,128)(2,1)S(1)}, bf16[2,180,384]{2,1,0:T(8,128)(2,1)S(1)}, u32[]{:S(2)}, u32[]{:S(2)}) collective-permute-start(bf16[2,180,384]{2,1,0:T(8,128)(2,1)S(1)} %bitcast.21), channel_id=1, source_target_pairs={{0,8},{8,16},{16,24},{24,32},{32,40},{40,48},{48,56},{56,64},{64,7... | collective-permute-start | bytes 829448 | tf_op jit(solution)/shard_map/ppermute | solution.py:222
  8.7 10.9 %collective-permute-start.2 = (bf16[2,72,384]{2,1,0:T(8,128)(2,1)S(1)}, bf16[2,72,384]{2,1,0:T(8,128)(2,1)S(1)}, u32[]{:S(2)}, u32[]{:S(2)}) collective-permute-start(bf16[2,72,384]{2,1,0:T(8,128)(2,1)S(1)} %pad_maximum_fusion), channel_id=1, source_target_pairs={{0,7},{1,0},{2,1},{3,2},{4,3},{5,4},{6,5},{7,6},{8,15},{9,8},{10,9... | collective-permute-start | bytes 331784 | tf_op jit(solution)/shard_map/ppermute | solution.py:237
  19.6 1.3 collective-permute-start.4
  20.9 4.6 %collective-permute-start.3 = (bf16[2,48,384]{2,1,0:T(8,128)(2,1)S(1)}, bf16[2,48,384]{2,1,0:T(8,128)(2,1)S(1)}, u32[]{:S(2)}, u32[]{:S(2)}) collective-permute-start(bf16[2,48,384]{2,1,0:T(8,128)(2,1)S(1)} %slice.9), channel_id=1, source_target_pairs={{0,15},{1,8},{2,9},{3,10},{4,11},{5,12},{6,13},{7,14},{8,23},{9,16... | collective-permute-start | bytes 221192 | tf_op jit(solution)/shard_map/ppermute | solution.py:238
  25.6 1.3 %collective-permute-done.3.refs_10_ = bf16[2,48,384]{2,1,0:T(8,128)(2,1)S(1)} collective-permute-done((bf16[2,48,384]{2,1,0:T(8,128)(2,1)S(1)}, bf16[2,48,384]{2,1,0:T(8,128)(2,1)S(1)}, u32[]{:S(2)}, u32[]{:S(2)}) %collective-permute-start.3) | collective-permute-done | bytes 73760 | tf_op jit(solution)/shard_map/ppermute | solution.py:238
  27.0 4.0 %shard_map.103 = (bf16[2,180,384]{2,1,0:T(8,128)(2,1)S(1)}, bf16[2,180,384]{2,1,0:T(8,128)(2,1)S(1)}, f32[768,384]{1,0:T(8,128)S(1)}, bf16[768,384]{1,0:T(8,128)(2,1)S(1)}) custom-call(s32[16,32]{1,0:T(8,128)S(1)} %bitcast.29, s32[16,32]{1,0:T(8,128)S(1)} %bitcast.31, s32[16,32]{1,0:T(8,128)S(1)} %bitcast.33, f32[16,32]{1,0:T(8,128)S(1)} %bitcast.35, ...), custom_call_target="tpu_custom_call" | custom-call | flops 2000000000 | bytes 8000000 | tf_op jit(solution)/shard_map/pallas_call | solution.py:135
  31.0 4.3 %collective-permute-start.5 = (bf16[768,384]{1,0:T(8,128)(2,1)S(1)}, bf16[768,384]{1,0:T(8,128)(2,1)S(1)}, u32[]{:S(2)}, u32[]{:S(2)}) collective-permute-start(bf16[768,384]{1,0:T(8,128)(2,1)S(1)} %get-tuple-element.22), channel_id=1, source_target_pairs={{0,128},{128,0},{1,129},{129,1},{2,130},{130,2},{3,131},{131,3},{4... | collective-permute-start | bytes 1769480 | tf_op jit(solution)/shard_map/ppermute | solution.py:244
  35.3 1.6 %collective-permute-done.5.got = bf16[768,384]{1,0:T(8,128)(2,1)S(1)} collective-permute-done((bf16[768,384]{1,0:T(8,128)(2,1)S(1)}, bf16[768,384]{1,0:T(8,128)(2,1)S(1)}, u32[]{:S(2)}, u32[]{:S(2)}) %collective-permute-start.5) | collective-permute-done | bytes 589856 | tf_op jit(solution)/shard_map/ppermute | solution.py:244
  37.0 15.0 %all_to_all.25.refs_0_ = bf16[4,192,384]{2,1,0:T(8,128)(2,1)S(1)} all-to-all(bf16[4,192,384]{2,1,0:T(8,128)(2,1)S(1)} %shard_map.104), channel_id=1, replica_groups=mesh['x_hi'=2,'core'=2,'y'=8,'x_lo'=2,'lon'=8] {'x_hi','x_lo'}, dimensions={0} | all-to-all | bytes 1179648 | tf_op jit(solution)/shard_map/all_to_all | solution.py:362
  52.8 12.1 %all-to-all-start.1 = ((f32[8,24,384]{2,1,0:T(8,128)}), f32[8,24,384]{2,1,0:T(8,128)S(1)}, u32[]{:S(2)}, u32[]{:S(2)}) async-start(f32[8,24,384]{2,1,0:T(8,128)} %get-tuple-element.24), calls=%async_computation.1 | async-start | bytes 589824 | tf_op jit(solution)/shard_map/all_to_all | solution.py:362
  64.9 2.2 %collective-permute-start.6 = (bf16[2,180,384]{2,1,0:T(8,128)(2,1)S(1)}, bf16[2,180,384]{2,1,0:T(8,128)(2,1)S(1)}, u32[]{:S(2)}, u32[]{:S(2)}) collective-permute-start(bf16[2,180,384]{2,1,0:T(8,128)(2,1)S(1)} %get-tuple-element.25.refs_2_), channel_id=1, source_target_pairs={{0,8},{8,16},{16,24},{24,32},{32,40},{40,48},{48,56},{56,64},{64,7... | collective-permute-start | bytes 829448 | tf_op jit(solution)/shard_map/ppermute | solution.py:222
  67.2 4.2 %collective-permute-done.6.refs_1_ = bf16[2,180,384]{2,1,0:T(8,128)(2,1)S(1)} collective-permute-done((bf16[2,180,384]{2,1,0:T(8,128)(2,1)S(1)}, bf16[2,180,384]{2,1,0:T(8,128)(2,1)S(1)}, u32[]{:S(2)}, u32[]{:S(2)}) %collective-permute-start.6) | collective-permute-done | bytes 276512 | tf_op jit(solution)/shard_map/ppermute | solution.py:222
  71.3 3.9 %all-to-all-done.1.refs_0_ = f32[8,24,384]{2,1,0:T(8,128)S(1)} async-done(((f32[8,24,384]{2,1,0:T(8,128)}), f32[8,24,384]{2,1,0:T(8,128)S(1)}, u32[]{:S(2)}, u32[]{:S(2)}) %all-to-all-start.1) | async-done | bytes 294944 | tf_op jit(solution)/shard_map/all_to_all | solution.py:362
  76.0 3.4 %all-to-all-start.2 = ((f32[8,24,384]{2,1,0:T(8,128)}), f32[8,24,384]{2,1,0:T(8,128)S(1)}, u32[]{:S(2)}, u32[]{:S(2)}) async-start(f32[8,24,384]{2,1,0:T(8,128)} %get-tuple-element.26), calls=%async_computation.2 | async-start | bytes 589824 | tf_op jit(solution)/shard_map/all_to_all | solution.py:362
  79.4 1.3 collective-permute-start.7
  80.7 8.4 %collective-permute-done.7.south = bf16[2,180,384]{2,1,0:T(8,128)(2,1)S(1)} collective-permute-done((bf16[2,180,384]{2,1,0:T(8,128)(2,1)S(1)}, bf16[2,180,384]{2,1,0:T(8,128)(2,1)S(1)}, u32[]{:S(2)}, u32[]{:S(2)}) %collective-permute-start.7) | collective-permute-done | bytes 276512 | tf_op jit(solution)/shard_map/ppermute | solution.py:226
  89.8 10.2 %all-to-all-start.3 = ((bf16[8,24,384]{2,1,0:T(8,128)(2,1)}), bf16[8,24,384]{2,1,0:T(8,128)(2,1)S(1)}, u32[]{:S(2)}, u32[]{:S(2)}) async-start(bf16[8,24,384]{2,1,0:T(8,128)(2,1)} %get-tuple-element.30), calls=%async_computation.3 | async-start | bytes 294912 | tf_op jit(solution)/shard_map/all_to_all | solution.py:362
  100.0 1.9 %collective-permute-start.8 = (bf16[2,168,384]{2,1,0:T(8,128)(2,1)S(1)}, bf16[2,168,384]{2,1,0:T(8,128)(2,1)S(1)}, u32[]{:S(2)}, u32[]{:S(2)}) collective-permute-start(bf16[2,168,384]{2,1,0:T(8,128)(2,1)S(1)} %get-tuple-element.32), channel_id=1, source_target_pairs={{0,1},{1,2},{2,3},{3,4},{4,5},{5,6},{6,7},{7,0},{8,9},{9,10},{10,1... | collective-permute-start | bytes 774152 | tf_op jit(solution)/shard_map/ppermute | solution.py:385
  101.9 6.3 %all-to-all-done.3 = bf16[8,24,384]{2,1,0:T(8,128)(2,1)S(1)} async-done(((bf16[8,24,384]{2,1,0:T(8,128)(2,1)}), bf16[8,24,384]{2,1,0:T(8,128)(2,1)S(1)}, u32[]{:S(2)}, u32[]{:S(2)}) %all-to-all-start.3) | async-done | bytes 147488 | tf_op jit(solution)/shard_map/all_to_all | solution.py:362
  109.1 3.5 %all-to-all-start.4 = ((bf16[4,192,384]{2,1,0:T(8,128)(2,1)}), bf16[4,192,384]{2,1,0:T(8,128)(2,1)S(1)}, u32[]{:S(2)}, u32[]{:S(2)}) async-start(bf16[4,192,384]{2,1,0:T(8,128)(2,1)} %get-tuple-element.31), calls=%async_computation.4 | async-start | bytes 1179648 | tf_op jit(solution)/shard_map/all_to_all | solution.py:362
  113.8 4.3 %shard_map.109 = (bf16[2,180,384]{2,1,0:T(8,128)(2,1)S(1)}, bf16[2,180,384]{2,1,0:T(8,128)(2,1)S(1)}) custom-call(s32[16,32]{1,0:T(8,128)S(1)} %bitcast.30, s32[16,32]{1,0:T(8,128)S(1)} %bitcast.32, s32[16,32]{1,0:T(8,128)S(1)} %bitcast.34, f32[16,32]{1,0:T(8,128)S(1)} %bitcast.36, s32[32]{0:T(128)S(1)} %copy-done.6, bf16[1536,384]{1,0:T(8,128)(2,1)S(1)} %bitcast.28, ...), custom_call_target="tpu_custom_call" | custom-call | flops 2500000000 | bytes 5000000 | tf_op jit(solution)/shard_map/pallas_call | solution.py:205
  118.1 1.7 %all-to-all-done.4 = bf16[4,192,384]{2,1,0:T(8,128)(2,1)S(1)} async-done(((bf16[4,192,384]{2,1,0:T(8,128)(2,1)}), bf16[4,192,384]{2,1,0:T(8,128)(2,1)S(1)}, u32[]{:S(2)}, u32[]{:S(2)}) %all-to-all-start.4) | async-done | bytes 589856 | tf_op jit(solution)/shard_map/all_to_all | solution.py:362
  119.8 7.3 %collective-permute-start.9 = (bf16[768,384]{1,0:T(8,128)(2,1)S(1)}, bf16[768,384]{1,0:T(8,128)(2,1)S(1)}, u32[]{:S(2)}, u32[]{:S(2)}) collective-permute-start(bf16[768,384]{1,0:T(8,128)(2,1)S(1)} %get-tuple-element.38.mine), channel_id=1, source_target_pairs={{0,128},{128,0},{1,129},{129,1},{2,130},{130,2},{3,131},{131,3},{4... | collective-permute-start | bytes 1769480 | tf_op jit(solution)/shard_map/ppermute | solution.py:244
  (35 shorter events, 9.7 us)
Async XLA Ops:
  0.6 26.3 %copy-start.6 = (s32[32]{0:T(128)S(1)}, s32[32]{0:T(128)}, u32[]{:S(2)}) copy-start(s32[32]{0:T(128)} %tap_count.1) | copy-start | bytes 388
  0.6 26.3 %copy-start.5 = (f32[32,16]{0,1:T(8,128)S(1)}, f32[32,16]{0,1:T(8,128)}, u32[]{:S(2)}) copy-start(f32[32,16]{0,1:T(8,128)} %param.14) | copy-start | bytes 6148
  0.7 26.3 %copy-start.4 = (s32[32,16]{0,1:T(8,128)S(1)}, s32[32,16]{0,1:T(8,128)}, u32[]{:S(2)}) copy-start(s32[32,16]{0,1:T(8,128)} %param.13) | copy-start | bytes 6148
  0.7 26.3 %copy-start.3 = (s32[32,16]{0,1:T(8,128)S(1)}, s32[32,16]{0,1:T(8,128)}, u32[]{:S(2)}) copy-start(s32[32,16]{0,1:T(8,128)} %param.12) | copy-start | bytes 6148
  0.7 26.3 %copy-start.2 = (s32[32,16]{0,1:T(8,128)S(1)}, s32[32,16]{0,1:T(8,128)}, u32[]{:S(2)}) copy-start(s32[32,16]{0,1:T(8,128)} %param.11) | copy-start | bytes 6148
  0.7 26.3 %copy-start = (bf16[4,384,384]{2,1,0:T(8,128)(2,1)S(1)}, bf16[4,384,384]{2,1,0:T(8,128)(2,1)}, u32[]{:S(2)}) copy-start(bf16[4,384,384]{2,1,0:T(8,128)(2,1)} %param.10) | copy-start | bytes 3538948
  1.8 25.2 %collective-permute-start.1 = (bf16[2,180,384]{2,1,0:T(8,128)(2,1)S(1)}, bf16[2,180,384]{2,1,0:T(8,128)(2,1)S(1)}, u32[]{:S(2)}, u32[]{:S(2)}) collective-permute-start(bf16[2,180,384]{2,1,0:T(8,128)(2,1)S(1)} %bitcast.20), channel_id=1, source_target_pairs={{8,0},{16,8},{24,16},{32,24},{40,32},{48,40},{56,48},{64,56},{72,6... | collective-permute-start | bytes 829448 | tf_op jit(solution)/shard_map/ppermute | solution.py:226
  3.1 23.9 %collective-permute-start = (bf16[2,180,384]{2,1,0:T(8,128)(2,1)S(1)}, bf16[2,180,384]{2,1,0:T(8,128)(2,1)S(1)}, u32[]{:S(2)}, u32[]{:S(2)}) collective-permute-start(bf16[2,180,384]{2,1,0:T(8,128)(2,1)S(1)} %bitcast.21), channel_id=1, source_target_pairs={{0,8},{8,16},{16,24},{24,32},{32,40},{40,48},{48,56},{56,64},{64,7... | collective-permute-start | bytes 829448 | tf_op jit(solution)/shard_map/ppermute | solution.py:222
  8.7 18.2 %collective-permute-start.2 = (bf16[2,72,384]{2,1,0:T(8,128)(2,1)S(1)}, bf16[2,72,384]{2,1,0:T(8,128)(2,1)S(1)}, u32[]{:S(2)}, u32[]{:S(2)}) collective-permute-start(bf16[2,72,384]{2,1,0:T(8,128)(2,1)S(1)} %pad_maximum_fusion), channel_id=1, source_target_pairs={{0,7},{1,0},{2,1},{3,2},{4,3},{5,4},{6,5},{7,6},{8,15},{9,8},{10,9... | collective-permute-start | bytes 331784 | tf_op jit(solution)/shard_map/ppermute | solution.py:237
  19.6 6.0 %collective-permute-start.4 = (bf16[2,48,384]{2,1,0:T(8,128)(2,1)S(1)}, bf16[2,48,384]{2,1,0:T(8,128)(2,1)S(1)}, u32[]{:S(2)}, u32[]{:S(2)}) collective-permute-start(bf16[2,48,384]{2,1,0:T(8,128)(2,1)S(1)} %slice.9), channel_id=1, source_target_pairs={{8,7},{9,0},{10,1},{11,2},{12,3},{13,4},{14,5},{15,6},{16,15},{17,... | collective-permute-start | bytes 221192 | tf_op jit(solution)/shard_map/ppermute | solution.py:239
  20.9 6.0 %collective-permute-start.3 = (bf16[2,48,384]{2,1,0:T(8,128)(2,1)S(1)}, bf16[2,48,384]{2,1,0:T(8,128)(2,1)S(1)}, u32[]{:S(2)}, u32[]{:S(2)}) collective-permute-start(bf16[2,48,384]{2,1,0:T(8,128)(2,1)S(1)} %slice.9), channel_id=1, source_target_pairs={{0,15},{1,8},{2,9},{3,10},{4,11},{5,12},{6,13},{7,14},{8,23},{9,16... | collective-permute-start | bytes 221192 | tf_op jit(solution)/shard_map/ppermute | solution.py:238
  31.0 5.9 %collective-permute-start.5 = (bf16[768,384]{1,0:T(8,128)(2,1)S(1)}, bf16[768,384]{1,0:T(8,128)(2,1)S(1)}, u32[]{:S(2)}, u32[]{:S(2)}) collective-permute-start(bf16[768,384]{1,0:T(8,128)(2,1)S(1)} %get-tuple-element.22), channel_id=1, source_target_pairs={{0,128},{128,0},{1,129},{129,1},{2,130},{130,2},{3,131},{131,3},{4... | collective-permute-start | bytes 1769480 | tf_op jit(solution)/shard_map/ppermute | solution.py:244
  52.8 22.4 %all-to-all-start.1 = ((f32[8,24,384]{2,1,0:T(8,128)}), f32[8,24,384]{2,1,0:T(8,128)S(1)}, u32[]{:S(2)}, u32[]{:S(2)}) async-start(f32[8,24,384]{2,1,0:T(8,128)} %get-tuple-element.24), calls=%async_computation.1 | async-start | bytes 589824 | tf_op jit(solution)/shard_map/all_to_all | solution.py:362
  64.9 6.4 %collective-permute-start.6 = (bf16[2,180,384]{2,1,0:T(8,128)(2,1)S(1)}, bf16[2,180,384]{2,1,0:T(8,128)(2,1)S(1)}, u32[]{:S(2)}, u32[]{:S(2)}) collective-permute-start(bf16[2,180,384]{2,1,0:T(8,128)(2,1)S(1)} %get-tuple-element.25.refs_2_), channel_id=1, source_target_pairs={{0,8},{8,16},{16,24},{24,32},{32,40},{40,48},{48,56},{56,64},{64,7... | collective-permute-start | bytes 829448 | tf_op jit(solution)/shard_map/ppermute | solution.py:222
  76.0 13.1 %all-to-all-start.2 = ((f32[8,24,384]{2,1,0:T(8,128)}), f32[8,24,384]{2,1,0:T(8,128)S(1)}, u32[]{:S(2)}, u32[]{:S(2)}) async-start(f32[8,24,384]{2,1,0:T(8,128)} %get-tuple-element.26), calls=%async_computation.2 | async-start | bytes 589824 | tf_op jit(solution)/shard_map/all_to_all | solution.py:362
  79.4 9.7 %collective-permute-start.7 = (bf16[2,180,384]{2,1,0:T(8,128)(2,1)S(1)}, bf16[2,180,384]{2,1,0:T(8,128)(2,1)S(1)}, u32[]{:S(2)}, u32[]{:S(2)}) collective-permute-start(bf16[2,180,384]{2,1,0:T(8,128)(2,1)S(1)} %get-tuple-element.27.dmixed.own), channel_id=1, source_target_pairs={{8,0},{16,8},{24,16},{32,24},{40,32},{48,40},{56,48},{64,56},{72,6... | collective-permute-start | bytes 829448 | tf_op jit(solution)/shard_map/ppermute | solution.py:226
  89.8 18.4 %all-to-all-start.3 = ((bf16[8,24,384]{2,1,0:T(8,128)(2,1)}), bf16[8,24,384]{2,1,0:T(8,128)(2,1)S(1)}, u32[]{:S(2)}, u32[]{:S(2)}) async-start(bf16[8,24,384]{2,1,0:T(8,128)(2,1)} %get-tuple-element.30), calls=%async_computation.3 | async-start | bytes 294912 | tf_op jit(solution)/shard_map/all_to_all | solution.py:362
  100.0 12.6 %collective-permute-start.8 = (bf16[2,168,384]{2,1,0:T(8,128)(2,1)S(1)}, bf16[2,168,384]{2,1,0:T(8,128)(2,1)S(1)}, u32[]{:S(2)}, u32[]{:S(2)}) collective-permute-start(bf16[2,168,384]{2,1,0:T(8,128)(2,1)S(1)} %get-tuple-element.32), channel_id=1, source_target_pairs={{0,1},{1,2},{2,3},{3,4},{4,5},{5,6},{6,7},{7,0},{8,9},{9,10},{10,1... | collective-permute-start | bytes 774152 | tf_op jit(solution)/shard_map/ppermute | solution.py:385
  109.1 10.7 %all-to-all-start.4 = ((bf16[4,192,384]{2,1,0:T(8,128)(2,1)}), bf16[4,192,384]{2,1,0:T(8,128)(2,1)S(1)}, u32[]{:S(2)}, u32[]{:S(2)}) async-start(bf16[4,192,384]{2,1,0:T(8,128)(2,1)} %get-tuple-element.31), calls=%async_computation.4 | async-start | bytes 1179648 | tf_op jit(solution)/shard_map/all_to_all | solution.py:362
  112.6 1.3 copy-start.1
  119.8 9.2 %collective-permute-start.9 = (bf16[768,384]{1,0:T(8,128)(2,1)S(1)}, bf16[768,384]{1,0:T(8,128)(2,1)S(1)}, u32[]{:S(2)}, u32[]{:S(2)}) collective-permute-start(bf16[768,384]{1,0:T(8,128)(2,1)S(1)} %get-tuple-element.38.mine), channel_id=1, source_target_pairs={{0,128},{128,0},{1,129},{129,1},{2,130},{130,2},{3,131},{131,3},{4... | collective-permute-start | bytes 1769480 | tf_op jit(solution)/shard_map/ppermute | solution.py:244

commit v8 on v7

--- a/solution.py
+++ b/solution.py
@@ -276,14 +276,8 @@
     )(mine, other)
 
 
-def sum_and_strip(pieces, copies, dmixed, north, south, made):
-    def body(part, dmixed, north, south, made, out, strip):
-        total = part[0]
-        for n in range(1, part.shape[0]):
-            total = total + part[n]
-        total = total.astype(out.dtype)
-        for n in range(copies):
-            out[n] = total
+def strip_for_east(dmixed, north, south, made):
+    def body(dmixed, north, south, made, strip):
         rows, width, _ = dmixed.shape
         for r in range(rows):
             for n, source in enumerate((north, south, dmixed)):
@@ -293,14 +287,11 @@
     rows, _, channels = dmixed.shape
     return pl.pallas_call(
         body,
-        out_shape=[
-            jax.ShapeDtypeStruct((copies, *pieces.shape[1:]), BF16),
-            jax.ShapeDtypeStruct((rows, 3 * RIM + LONREACH, channels), BF16),
-        ],
-        in_specs=[VMEM] * 5,
-        out_specs=[VMEM] * 2,
-        compiler_params=pltpu.CompilerParams(vmem_limit_bytes=12 << 20),
-    )(pieces, dmixed, north, south, made)
+        out_shape=jax.ShapeDtypeStruct((rows, 3 * RIM + LONREACH, channels), BF16),
+        in_specs=[VMEM] * 4,
+        out_specs=VMEM,
+        compiler_params=pltpu.CompilerParams(vmem_limit_bytes=8 << 20),
+    )(dmixed, north, south, made)
 
 
 def sum_pieces(pieces, out_shape, passed=()):
@@ -374,15 +365,12 @@
     nx, ny, nz = lax.axis_size(ALONG_X), lax.axis_size("y"), lax.axis_size("lon")
     made, dmixed, keep, send = forward(tables, wide, fields, upstream, 1.0 / math.sqrt(cells))
     piece = (keep.shape[0] // (nx * ny), channels)
-    got = exchange(add_halves(keep, core_swap(send), nx), ALONG_X)
-    part, dmixed = sum_pieces(got, jax.ShapeDtypeStruct((ny, *piece), F32), (dmixed,))
-    north = from_north(dmixed)
-    got = exchange(part, "y")
-    part, north, dmixed = sum_pieces(got, jax.ShapeDtypeStruct((nz, *piece), F32), (north, dmixed))
-    south = from_south(dmixed)
+    got = exchange(add_halves(keep, core_swap(send), nx * ny), ALONG_X + ("y",))
+    north, south = from_north(dmixed), from_south(dmixed)
+    part, north, south = sum_pieces(got, jax.ShapeDtypeStruct((nz, *piece), F32), (north, south))
     got = exchange(part, "lon")
-    part, strip = sum_and_strip(got, ny, dmixed, north, south, made)
-    strip = lax.ppermute(strip, "lon", lon_shift(1))
+    part, dmixed = sum_pieces(got, jax.ShapeDtypeStruct((ny, *piece), BF16), (dmixed,))
+    strip = lax.ppermute(strip_for_east(dmixed, north, south, made), "lon", lon_shift(1))
     got = exchange(part, "y")
     part, made = spread(got.reshape(-1, channels), nx, (made,))
     mine = exchange(part, ALONG_X).reshape(-1, channels)

time: 131 us -> 128 us (0.977)
  blocking collectives: 15 us -> 12.2 us
    ppermute x1, waiting for transfers between devices: 0.07 us -> 5.32 us  [lon_strips(): lax.ppermute(rim, LAT + ('lon',), [((i + 1) * lons + c, i * lons + d) for...]
    all_to_all x4 -> x3, waiting for transfers between devices: 11.9 us -> 7.92 us  [exchange(): return lax.all_to_all(pieces, axes, 0, 0, tiled=True)]
    ppermute x2, waiting for transfers between devices: 8.36 us -> 4.72 us  [from_south(): lax.ppermute(block, LAT, [(i + 1, i) for i in range(lax.axis_size(LAT) -...]
    ppermute x2, waiting for transfers between devices: 4.2 us -> 7.5 us  [from_north(): lax.ppermute(block, LAT, [(i, i + 1) for i in range(lax.axis_size(LAT) -...]
    all_to_all x1, blocking collectives: 15 us -> 12.2 us  [exchange(): return lax.all_to_all(pieces, axes, 0, 0, tiled=True)]
    all_to_all x4 -> x3, starting transfers between devices: 29.2 us -> 30 us  [exchange(): return lax.all_to_all(pieces, axes, 0, 0, tiled=True)]
  transfers between devices with their start and end apart: 14 -> 13, of which waited for: 8 -> 7; matrix products, arithmetic and copies ran while one was open for 2% -> 2% of each run, Pallas kernels for 4% -> 4%
where the time goes in v8:
time: 128 us
  starting transfers between devices  69.9 us (55%)
  waiting for transfers between devices  27.2 us (21%)
  blocking collectives  12.2 us (10%)
  Pallas kernels  12.1 us (9%)
  local copies, waits for them, and re-layouts  5.23 us (4%)
    all_to_all x3, starting transfers between devices, exchange(): return lax.all_to_all(pieces, axes, 0, 0, tiled=True)  30 us
    ppermute x2, starting transfers between devices, core_swap(): return lax.ppermute(block, 'core', [(0, 1), (1, 0)])  12.3 us
    all_to_all x1, blocking collectives, exchange(): return lax.all_to_all(pieces, axes, 0, 0, tiled=True)  12.2 us
    ppermute x1, starting transfers between devices, lon_strips(): level = lax.ppermute(side, 'lon', along)  10.7 us
    all_to_all x3, waiting for transfers between devices, exchange(): return lax.all_to_all(pieces, axes, 0, 0, tiled=True)  7.92 us
    ppermute x2, waiting for transfers between devices, from_north(): lax.ppermute(block, LAT, [(i, i + 1) for i in range(lax.axis_size(LAT) -...  7.5 us
    ppermute x2, starting transfers between devices, from_north(): lax.ppermute(block, LAT, [(i, i + 1) for i in range(lax.axis_size(LAT) -...  7.12 us
    ppermute x1, waiting for transfers between devices, lon_strips(): lax.ppermute(rim, LAT + ('lon',), [((i + 1) * lons + c, i * lons + d) for...  5.32 us
  transfers between devices with their start and end apart: 13, of which 7 were waited for; matrix products, arithmetic and copies ran while one was open for 2% of the time, Pallas kernels for 4%

profile of v8, /device:TPU:1, one launch (start us, length us, event | category | flops | bytes accessed | tf_op | source)
XLA Modules:
  0.0 127.6 jit_solution(1449492050452167515)
XLA Ops:
  1.8 4.0 %collective-permute-start = (bf16[2,180,384]{2,1,0:T(8,128)(2,1)S(1)}, bf16[2,180,384]{2,1,0:T(8,128)(2,1)S(1)}, u32[]{:S(2)}, u32[]{:S(2)}) collective-permute-start(bf16[2,180,384]{2,1,0:T(8,128)(2,1)S(1)} %bitcast.20), channel_id=1, source_target_pairs={{0,8},{8,16},{16,24},{24,32},{32,40},{40,48},{48,56},{56,64},{64,7... | collective-permute-start | bytes 829448 | tf_op jit(solution)/shard_map/ppermute | solution.py:222
  5.8 1.3 %collective-permute-start.1 = (bf16[2,180,384]{2,1,0:T(8,128)(2,1)S(1)}, bf16[2,180,384]{2,1,0:T(8,128)(2,1)S(1)}, u32[]{:S(2)}, u32[]{:S(2)}) collective-permute-start(bf16[2,180,384]{2,1,0:T(8,128)(2,1)S(1)} %bitcast.21), channel_id=1, source_target_pairs={{8,0},{16,8},{24,16},{32,24},{40,32},{48,40},{56,48},{64,56},{72,6... | collective-permute-start | bytes 829448 | tf_op jit(solution)/shard_map/ppermute | solution.py:226
  8.1 10.7 %collective-permute-start.2 = (bf16[2,72,384]{2,1,0:T(8,128)(2,1)S(1)}, bf16[2,72,384]{2,1,0:T(8,128)(2,1)S(1)}, u32[]{:S(2)}, u32[]{:S(2)}) collective-permute-start(bf16[2,72,384]{2,1,0:T(8,128)(2,1)S(1)} %pad_maximum_fusion), channel_id=1, source_target_pairs={{0,7},{1,0},{2,1},{3,2},{4,3},{5,4},{6,5},{7,6},{8,15},{9,8},{10,9... | collective-permute-start | bytes 331784 | tf_op jit(solution)/shard_map/ppermute | solution.py:237
  18.8 4.0 %collective-permute-start.3 = (bf16[2,48,384]{2,1,0:T(8,128)(2,1)S(1)}, bf16[2,48,384]{2,1,0:T(8,128)(2,1)S(1)}, u32[]{:S(2)}, u32[]{:S(2)}) collective-permute-start(bf16[2,48,384]{2,1,0:T(8,128)(2,1)S(1)} %slice.9), channel_id=1, source_target_pairs={{0,15},{1,8},{2,9},{3,10},{4,11},{5,12},{6,13},{7,14},{8,23},{9,16... | collective-permute-start | bytes 221192 | tf_op jit(solution)/shard_map/ppermute | solution.py:238
  22.8 1.3 %collective-permute-start.4 = (bf16[2,48,384]{2,1,0:T(8,128)(2,1)S(1)}, bf16[2,48,384]{2,1,0:T(8,128)(2,1)S(1)}, u32[]{:S(2)}, u32[]{:S(2)}) collective-permute-start(bf16[2,48,384]{2,1,0:T(8,128)(2,1)S(1)} %slice.9), channel_id=1, source_target_pairs={{8,7},{9,0},{10,1},{11,2},{12,3},{13,4},{14,5},{15,6},{16,15},{17,... | collective-permute-start | bytes 221192 | tf_op jit(solution)/shard_map/ppermute | solution.py:239
  24.1 5.3 %collective-permute-done.4.refs_11_ = bf16[2,48,384]{2,1,0:T(8,128)(2,1)S(1)} collective-permute-done((bf16[2,48,384]{2,1,0:T(8,128)(2,1)S(1)}, bf16[2,48,384]{2,1,0:T(8,128)(2,1)S(1)}, u32[]{:S(2)}, u32[]{:S(2)}) %collective-permute-start.4) | collective-permute-done | bytes 73760 | tf_op jit(solution)/shard_map/ppermute | solution.py:239
  29.5 4.0 %shard_map.103 = (bf16[2,180,384]{2,1,0:T(8,128)(2,1)S(1)}, bf16[2,180,384]{2,1,0:T(8,128)(2,1)S(1)}, f32[768,384]{1,0:T(8,128)S(1)}, bf16[768,384]{1,0:T(8,128)(2,1)S(1)}) custom-call(s32[16,32]{1,0:T(8,128)S(1)} %bitcast.29, s32[16,32]{1,0:T(8,128)S(1)} %bitcast.31, s32[16,32]{1,0:T(8,128)S(1)} %bitcast.33, f32[16,32]{1,0:T(8,128)S(1)} %bitcast.35, ...), custom_call_target="tpu_custom_call" | custom-call | flops 2000000000 | bytes 8000000 | tf_op jit(solution)/shard_map/pallas_call | solution.py:135
  33.6 4.6 %collective-permute-start.5 = (bf16[768,384]{1,0:T(8,128)(2,1)S(1)}, bf16[768,384]{1,0:T(8,128)(2,1)S(1)}, u32[]{:S(2)}, u32[]{:S(2)}) collective-permute-start(bf16[768,384]{1,0:T(8,128)(2,1)S(1)} %get-tuple-element.20), channel_id=1, source_target_pairs={{0,128},{128,0},{1,129},{129,1},{2,130},{130,2},{3,131},{131,3},{4... | collective-permute-start | bytes 1769480 | tf_op jit(solution)/shard_map/ppermute | solution.py:244
  38.1 1.6 %collective-permute-done.5.got = bf16[768,384]{1,0:T(8,128)(2,1)S(1)} collective-permute-done((bf16[768,384]{1,0:T(8,128)(2,1)S(1)}, bf16[768,384]{1,0:T(8,128)(2,1)S(1)}, u32[]{:S(2)}, u32[]{:S(2)}) %collective-permute-start.5) | collective-permute-done | bytes 589856 | tf_op jit(solution)/shard_map/ppermute | solution.py:244
  40.7 13.1 %all-to-all-start = ((bf16[32,24,384]{2,1,0:T(8,128)(2,1)}), bf16[32,24,384]{2,1,0:T(8,128)(2,1)S(1)}, u32[]{:S(2)}, u32[]{:S(2)}) async-start(bf16[32,24,384]{2,1,0:T(8,128)(2,1)} %shard_map.104), calls=%async_computation | async-start | bytes 1179648 | tf_op jit(solution)/shard_map/all_to_all | solution.py:353
  53.8 3.2 %collective-permute-start.6 = (bf16[2,180,384]{2,1,0:T(8,128)(2,1)S(1)}, bf16[2,180,384]{2,1,0:T(8,128)(2,1)S(1)}, u32[]{:S(2)}, u32[]{:S(2)}) collective-permute-start(bf16[2,180,384]{2,1,0:T(8,128)(2,1)S(1)} %get-tuple-element.21.refs_1_), channel_id=1, source_target_pairs={{0,8},{8,16},{16,24},{24,32},{32,40},{40,48},{48,56},{56,64},{64,7... | collective-permute-start | bytes 829448 | tf_op jit(solution)/shard_map/ppermute | solution.py:222
  57.0 1.3 %collective-permute-start.7 = (bf16[2,180,384]{2,1,0:T(8,128)(2,1)S(1)}, bf16[2,180,384]{2,1,0:T(8,128)(2,1)S(1)}, u32[]{:S(2)}, u32[]{:S(2)}) collective-permute-start(bf16[2,180,384]{2,1,0:T(8,128)(2,1)S(1)} %get-tuple-element.21.refs_1_), channel_id=1, source_target_pairs={{8,0},{16,8},{24,16},{32,24},{40,32},{48,40},{56,48},{64,56},{72,6... | collective-permute-start | bytes 829448 | tf_op jit(solution)/shard_map/ppermute | solution.py:226
  58.3 7.5 %collective-permute-done.6.refs_1_ = bf16[2,180,384]{2,1,0:T(8,128)(2,1)S(1)} collective-permute-done((bf16[2,180,384]{2,1,0:T(8,128)(2,1)S(1)}, bf16[2,180,384]{2,1,0:T(8,128)(2,1)S(1)}, u32[]{:S(2)}, u32[]{:S(2)}) %collective-permute-start.6) | collective-permute-done | bytes 276512 | tf_op jit(solution)/shard_map/ppermute | solution.py:222
  65.8 4.7 %collective-permute-done.7.refs_2_ = bf16[2,180,384]{2,1,0:T(8,128)(2,1)S(1)} collective-permute-done((bf16[2,180,384]{2,1,0:T(8,128)(2,1)S(1)}, bf16[2,180,384]{2,1,0:T(8,128)(2,1)S(1)}, u32[]{:S(2)}, u32[]{:S(2)}) %collective-permute-start.7) | collective-permute-done | bytes 276512 | tf_op jit(solution)/shard_map/ppermute | solution.py:226
  70.6 12.2 %all_to_all.20.refs_0_ = f32[8,24,384]{2,1,0:T(8,128)S(1)} all-to-all(f32[8,24,384]{2,1,0:T(8,128)S(1)} %get-tuple-element.22), channel_id=1, replica_groups=mesh['x_hi'=2,'core'=2,'y'=8,'x_lo'=2,'lon'=8] {'lon'}, dimensions={0} | all-to-all | bytes 589824 | tf_op jit(solution)/shard_map/all_to_all | solution.py:353
  83.5 13.2 %all-to-all-start.2 = ((bf16[8,24,384]{2,1,0:T(8,128)(2,1)}), bf16[8,24,384]{2,1,0:T(8,128)(2,1)S(1)}, u32[]{:S(2)}, u32[]{:S(2)}) async-start(bf16[8,24,384]{2,1,0:T(8,128)(2,1)} %get-tuple-element.23), calls=%async_computation.2 | async-start | bytes 294912 | tf_op jit(solution)/shard_map/all_to_all | solution.py:353
  96.8 1.9 %collective-permute-start.8 = (bf16[2,168,384]{2,1,0:T(8,128)(2,1)S(1)}, bf16[2,168,384]{2,1,0:T(8,128)(2,1)S(1)}, u32[]{:S(2)}, u32[]{:S(2)}) collective-permute-start(bf16[2,168,384]{2,1,0:T(8,128)(2,1)S(1)} %shard_map.108), channel_id=1, source_target_pairs={{0,1},{1,2},{2,3},{3,4},{4,5},{5,6},{6,7},{7,0},{8,9},{9,10},{10,1... | collective-permute-start | bytes 774152 | tf_op jit(solution)/shard_map/ppermute | solution.py:373
  98.7 6.2 %all-to-all-done.2 = bf16[8,24,384]{2,1,0:T(8,128)(2,1)S(1)} async-done(((bf16[8,24,384]{2,1,0:T(8,128)(2,1)}), bf16[8,24,384]{2,1,0:T(8,128)(2,1)S(1)}, u32[]{:S(2)}, u32[]{:S(2)}) %all-to-all-start.2) | async-done | bytes 147488 | tf_op jit(solution)/shard_map/all_to_all | solution.py:353
  105.8 3.7 %all-to-all-start.3 = ((bf16[4,192,384]{2,1,0:T(8,128)(2,1)}), bf16[4,192,384]{2,1,0:T(8,128)(2,1)S(1)}, u32[]{:S(2)}, u32[]{:S(2)}) async-start(bf16[4,192,384]{2,1,0:T(8,128)(2,1)} %get-tuple-element.25), calls=%async_computation.3 | async-start | bytes 1179648 | tf_op jit(solution)/shard_map/all_to_all | solution.py:353
  109.5 1.3 copy-done.1
  110.7 4.3 %shard_map.109 = (bf16[2,180,384]{2,1,0:T(8,128)(2,1)S(1)}, bf16[2,180,384]{2,1,0:T(8,128)(2,1)S(1)}) custom-call(s32[16,32]{1,0:T(8,128)S(1)} %bitcast.30, s32[16,32]{1,0:T(8,128)S(1)} %bitcast.32, s32[16,32]{1,0:T(8,128)S(1)} %bitcast.34, f32[16,32]{1,0:T(8,128)S(1)} %bitcast.36, s32[32]{0:T(128)S(1)} %copy-done.6, bf16[1536,384]{1,0:T(8,128)(2,1)S(1)} %bitcast.28, ...), custom_call_target="tpu_custom_call" | custom-call | flops 2500000000 | bytes 5000000 | tf_op jit(solution)/shard_map/pallas_call | solution.py:205
  115.0 1.7 %all-to-all-done.3 = bf16[4,192,384]{2,1,0:T(8,128)(2,1)S(1)} async-done(((bf16[4,192,384]{2,1,0:T(8,128)(2,1)}), bf16[4,192,384]{2,1,0:T(8,128)(2,1)S(1)}, u32[]{:S(2)}, u32[]{:S(2)}) %all-to-all-start.3) | async-done | bytes 589856 | tf_op jit(solution)/shard_map/all_to_all | solution.py:353
  116.8 7.8 %collective-permute-start.9 = (bf16[768,384]{1,0:T(8,128)(2,1)S(1)}, bf16[768,384]{1,0:T(8,128)(2,1)S(1)}, u32[]{:S(2)}, u32[]{:S(2)}) collective-permute-start(bf16[768,384]{1,0:T(8,128)(2,1)S(1)} %get-tuple-element.34.mine), channel_id=1, source_target_pairs={{0,128},{128,0},{1,129},{129,1},{2,130},{130,2},{3,131},{131,3},{4... | collective-permute-start | bytes 1769480 | tf_op jit(solution)/shard_map/ppermute | solution.py:244
  126.4 1.2 shard_map.111
  (33 shorter events, 6.7 us)
Async XLA Ops:
  0.6 28.9 %copy-start.2 = (s32[32,16]{0,1:T(8,128)S(1)}, s32[32,16]{0,1:T(8,128)}, u32[]{:S(2)}) copy-start(s32[32,16]{0,1:T(8,128)} %param.11) | copy-start | bytes 6148
  0.6 28.9 %copy-start.3 = (s32[32,16]{0,1:T(8,128)S(1)}, s32[32,16]{0,1:T(8,128)}, u32[]{:S(2)}) copy-start(s32[32,16]{0,1:T(8,128)} %param.12) | copy-start | bytes 6148
  0.7 28.9 %copy-start.4 = (s32[32,16]{0,1:T(8,128)S(1)}, s32[32,16]{0,1:T(8,128)}, u32[]{:S(2)}) copy-start(s32[32,16]{0,1:T(8,128)} %param.13) | copy-start | bytes 6148
  0.7 28.9 %copy-start.5 = (f32[32,16]{0,1:T(8,128)S(1)}, f32[32,16]{0,1:T(8,128)}, u32[]{:S(2)}) copy-start(f32[32,16]{0,1:T(8,128)} %param.14) | copy-start | bytes 6148
  0.7 28.9 %copy-start = (bf16[4,384,384]{2,1,0:T(8,128)(2,1)S(1)}, bf16[4,384,384]{2,1,0:T(8,128)(2,1)}, u32[]{:S(2)}) copy-start(bf16[4,384,384]{2,1,0:T(8,128)(2,1)} %param.10) | copy-start | bytes 3538948
  0.7 28.9 %copy-start.6 = (s32[32]{0:T(128)S(1)}, s32[32]{0:T(128)}, u32[]{:S(2)}) copy-start(s32[32]{0:T(128)} %tap_count.1) | copy-start | bytes 388
  1.8 27.7 %collective-permute-start = (bf16[2,180,384]{2,1,0:T(8,128)(2,1)S(1)}, bf16[2,180,384]{2,1,0:T(8,128)(2,1)S(1)}, u32[]{:S(2)}, u32[]{:S(2)}) collective-permute-start(bf16[2,180,384]{2,1,0:T(8,128)(2,1)S(1)} %bitcast.20), channel_id=1, source_target_pairs={{0,8},{8,16},{16,24},{24,32},{32,40},{40,48},{48,56},{56,64},{64,7... | collective-permute-start | bytes 829448 | tf_op jit(solution)/shard_map/ppermute | solution.py:222
  5.8 23.7 %collective-permute-start.1 = (bf16[2,180,384]{2,1,0:T(8,128)(2,1)S(1)}, bf16[2,180,384]{2,1,0:T(8,128)(2,1)S(1)}, u32[]{:S(2)}, u32[]{:S(2)}) collective-permute-start(bf16[2,180,384]{2,1,0:T(8,128)(2,1)S(1)} %bitcast.21), channel_id=1, source_target_pairs={{8,0},{16,8},{24,16},{32,24},{40,32},{48,40},{56,48},{64,56},{72,6... | collective-permute-start | bytes 829448 | tf_op jit(solution)/shard_map/ppermute | solution.py:226
  8.1 21.4 %collective-permute-start.2 = (bf16[2,72,384]{2,1,0:T(8,128)(2,1)S(1)}, bf16[2,72,384]{2,1,0:T(8,128)(2,1)S(1)}, u32[]{:S(2)}, u32[]{:S(2)}) collective-permute-start(bf16[2,72,384]{2,1,0:T(8,128)(2,1)S(1)} %pad_maximum_fusion), channel_id=1, source_target_pairs={{0,7},{1,0},{2,1},{3,2},{4,3},{5,4},{6,5},{7,6},{8,15},{9,8},{10,9... | collective-permute-start | bytes 331784 | tf_op jit(solution)/shard_map/ppermute | solution.py:237
  18.8 5.4 %collective-permute-start.3 = (bf16[2,48,384]{2,1,0:T(8,128)(2,1)S(1)}, bf16[2,48,384]{2,1,0:T(8,128)(2,1)S(1)}, u32[]{:S(2)}, u32[]{:S(2)}) collective-permute-start(bf16[2,48,384]{2,1,0:T(8,128)(2,1)S(1)} %slice.9), channel_id=1, source_target_pairs={{0,15},{1,8},{2,9},{3,10},{4,11},{5,12},{6,13},{7,14},{8,23},{9,16... | collective-permute-start | bytes 221192 | tf_op jit(solution)/shard_map/ppermute | solution.py:238
  22.8 6.7 %collective-permute-start.4 = (bf16[2,48,384]{2,1,0:T(8,128)(2,1)S(1)}, bf16[2,48,384]{2,1,0:T(8,128)(2,1)S(1)}, u32[]{:S(2)}, u32[]{:S(2)}) collective-permute-start(bf16[2,48,384]{2,1,0:T(8,128)(2,1)S(1)} %slice.9), channel_id=1, source_target_pairs={{8,7},{9,0},{10,1},{11,2},{12,3},{13,4},{14,5},{15,6},{16,15},{17,... | collective-permute-start | bytes 221192 | tf_op jit(solution)/shard_map/ppermute | solution.py:239
  33.6 6.2 %collective-permute-start.5 = (bf16[768,384]{1,0:T(8,128)(2,1)S(1)}, bf16[768,384]{1,0:T(8,128)(2,1)S(1)}, u32[]{:S(2)}, u32[]{:S(2)}) collective-permute-start(bf16[768,384]{1,0:T(8,128)(2,1)S(1)} %get-tuple-element.20), channel_id=1, source_target_pairs={{0,128},{128,0},{1,129},{129,1},{2,130},{130,2},{3,131},{131,3},{4... | collective-permute-start | bytes 1769480 | tf_op jit(solution)/shard_map/ppermute | solution.py:244
  40.7 29.8 %all-to-all-start = ((bf16[32,24,384]{2,1,0:T(8,128)(2,1)}), bf16[32,24,384]{2,1,0:T(8,128)(2,1)S(1)}, u32[]{:S(2)}, u32[]{:S(2)}) async-start(bf16[32,24,384]{2,1,0:T(8,128)(2,1)} %shard_map.104), calls=%async_computation | async-start | bytes 1179648 | tf_op jit(solution)/shard_map/all_to_all | solution.py:353
  53.8 12.0 %collective-permute-start.6 = (bf16[2,180,384]{2,1,0:T(8,128)(2,1)S(1)}, bf16[2,180,384]{2,1,0:T(8,128)(2,1)S(1)}, u32[]{:S(2)}, u32[]{:S(2)}) collective-permute-start(bf16[2,180,384]{2,1,0:T(8,128)(2,1)S(1)} %get-tuple-element.21.refs_1_), channel_id=1, source_target_pairs={{0,8},{8,16},{16,24},{24,32},{32,40},{40,48},{48,56},{56,64},{64,7... | collective-permute-start | bytes 829448 | tf_op jit(solution)/shard_map/ppermute | solution.py:222
  57.0 13.5 %collective-permute-start.7 = (bf16[2,180,384]{2,1,0:T(8,128)(2,1)S(1)}, bf16[2,180,384]{2,1,0:T(8,128)(2,1)S(1)}, u32[]{:S(2)}, u32[]{:S(2)}) collective-permute-start(bf16[2,180,384]{2,1,0:T(8,128)(2,1)S(1)} %get-tuple-element.21.refs_1_), channel_id=1, source_target_pairs={{8,0},{16,8},{24,16},{32,24},{40,32},{48,40},{56,48},{64,56},{72,6... | collective-permute-start | bytes 829448 | tf_op jit(solution)/shard_map/ppermute | solution.py:226
  83.5 21.4 %all-to-all-start.2 = ((bf16[8,24,384]{2,1,0:T(8,128)(2,1)}), bf16[8,24,384]{2,1,0:T(8,128)(2,1)S(1)}, u32[]{:S(2)}, u32[]{:S(2)}) async-start(bf16[8,24,384]{2,1,0:T(8,128)(2,1)} %get-tuple-element.23), calls=%async_computation.2 | async-start | bytes 294912 | tf_op jit(solution)/shard_map/all_to_all | solution.py:353
  96.8 12.7 %collective-permute-start.8 = (bf16[2,168,384]{2,1,0:T(8,128)(2,1)S(1)}, bf16[2,168,384]{2,1,0:T(8,128)(2,1)S(1)}, u32[]{:S(2)}, u32[]{:S(2)}) collective-permute-start(bf16[2,168,384]{2,1,0:T(8,128)(2,1)S(1)} %shard_map.108), channel_id=1, source_target_pairs={{0,1},{1,2},{2,3},{3,4},{4,5},{5,6},{6,7},{7,0},{8,9},{9,10},{10,1... | collective-permute-start | bytes 774152 | tf_op jit(solution)/shard_map/ppermute | solution.py:373
  105.8 11.0 %all-to-all-start.3 = ((bf16[4,192,384]{2,1,0:T(8,128)(2,1)}), bf16[4,192,384]{2,1,0:T(8,128)(2,1)S(1)}, u32[]{:S(2)}, u32[]{:S(2)}) async-start(bf16[4,192,384]{2,1,0:T(8,128)(2,1)} %get-tuple-element.25), calls=%async_computation.3 | async-start | bytes 1179648 | tf_op jit(solution)/shard_map/all_to_all | solution.py:353
  109.5 1.3 copy-start.1
  116.8 9.6 %collective-permute-start.9 = (bf16[768,384]{1,0:T(8,128)(2,1)S(1)}, bf16[768,384]{1,0:T(8,128)(2,1)S(1)}, u32[]{:S(2)}, u32[]{:S(2)}) collective-permute-start(bf16[768,384]{1,0:T(8,128)(2,1)S(1)} %get-tuple-element.34.mine), channel_id=1, source_target_pairs={{0,128},{128,0},{1,129},{129,1},{2,130},{130,2},{3,131},{131,3},{4... | collective-permute-start | bytes 1769480 | tf_op jit(solution)/shard_map/ppermute | solution.py:244

commit v9 on v6

--- a/solution.py
+++ b/solution.py
@@ -69,7 +69,7 @@
         pos[rows * room + i] = counts[i]
 
 
-def forward_kernel(lat_off, lon_off, basis, tap_val, tap_count, weights, own, north, south, east, ne, se, upstream,
+def forward_kernel(lat_off, lon_off, basis, tap_val, tap_count, weights, own, north, south, strip, upstream,
                    new_state, dmixed, keep, send, pos, val, ext, up, z, dm, *, scale):
     rows, width, channels = own.shape
     kcount = weights.shape[0] // channels
@@ -77,18 +77,18 @@
     tables = (lat_off, lon_off, basis, tap_val, tap_count)
     room = lat_off.shape[0] + 1
     forward_taps(tables, lax.axis_index(LAT) * rows, rows, kcount, pos, val)
-    for side, (mid, rim) in enumerate(((north, ne), (own, east), (south, se))):
+    for side, (mid, at) in enumerate(((north, 0), (own, 2 * RIM), (south, RIM))):
         for r in range(rows):
             base = (side * rows + r) * EXT
             for c in range(chunks):
                 lanes = slice(c * LANES, (c + 1) * LANES)
                 ext[c, base : base + width, :] = mid[r, :, lanes].astype(F32)
-                ext[c, base + width : base + width + RIM, :] = rim[r, :RIM, lanes].astype(F32)
+                ext[c, base + width : base + width + RIM, :] = strip[r, at : at + RIM, lanes].astype(F32)
                 ext[c, base + width + RIM : base + EXT, :] = jnp.zeros((EXT - RIM - width, LANES), F32)
     for i in range(rows):
         kept = width - LONREACH
         up[i, :kept] = upstream[i].astype(F32)[LONREACH:]
-        up[i, kept:width] = east[i].astype(F32)[RIM:]
+        up[i, kept:width] = strip[i].astype(F32)[3 * RIM :]
     for i in range(rows):
         for k in range(kcount):
             for c in range(chunks):
@@ -140,7 +140,7 @@
             jax.ShapeDtypeStruct((wide // 2, channels), F32),
             jax.ShapeDtypeStruct((wide // 2, channels), BF16),
         ],
-        in_specs=[SMEM] * 5 + [VMEM] * 8,
+        in_specs=[SMEM] * 5 + [VMEM] * 6,
         out_specs=[VMEM] * 4,
         scratch_shapes=[
             pltpu.SMEM((lists + 64,), jnp.int32),
@@ -230,13 +230,21 @@
     return [(j, (j + step) % lons) for j in range(lons)]
 
 
-def lon_strips(side, rim):
-    ends, lons = lax.axis_size(LAT) - 1, lax.axis_size("lon")
-    along = lon_shift(-1)
-    level = lax.ppermute(side, "lon", along)
-    upper = lax.ppermute(rim, LAT + ("lon",), [(i * lons + c, (i + 1) * lons + d) for i in range(ends) for c, d in along])
-    lower = lax.ppermute(rim, LAT + ("lon",), [((i + 1) * lons + c, i * lons + d) for i in range(ends) for c, d in along])
-    return level, upper, lower
+def strip_for_west(field, north, south, upstream):
+    def body(field, north, south, upstream, strip):
+        for r in range(field.shape[0]):
+            for n, source in enumerate((north, south, field)):
+                strip[r, n * RIM : (n + 1) * RIM] = source[r, :RIM]
+            strip[r, 3 * RIM :] = upstream[r, :LONREACH]
+
+    rows, _, channels = field.shape
+    return pl.pallas_call(
+        body,
+        out_shape=jax.ShapeDtypeStruct((rows, 3 * RIM + LONREACH, channels), BF16),
+        in_specs=[VMEM] * 4,
+        out_specs=VMEM,
+        compiler_params=pltpu.CompilerParams(vmem_limit_bytes=8 << 20),
+    )(field, north, south, upstream)
 
 
 def core_swap(block):
@@ -367,8 +375,9 @@
     kcount = weights.shape[0]
     wide = weights.reshape(-1, channels)
     tables = (lat_off.T, lon_off.T, basis.T, tap_val.T, tap_count)
-    side = jnp.concatenate([field[:, :RIM], upstream[:, :LONREACH]], axis=1)
-    fields = (field, *lat_blocks(field), *lon_strips(side, field[:, :RIM]))
+    north, south = lat_blocks(field)
+    strip = lax.ppermute(strip_for_west(field, north, south, upstream), "lon", lon_shift(-1))
+    fields = (field, north, south, strip)
     cells = lax.axis_size(DP) * lax.axis_size(LAT) * rows * lax.axis_size("lon") * width
     nx, ny, nz = lax.axis_size(ALONG_X), lax.axis_size("y"), lax.axis_size("lon")
     made, dmixed, keep, send = forward(tables, wide, fields, upstream, 1.0 / math.sqrt(cells))
@@ -382,7 +391,7 @@
     part, strip = sum_and_strip(got, ny, dmixed, north, south, made)
     strip = lax.ppermute(strip, "lon", lon_shift(1))
     got = exchange(part, "y")
-    part, strip = spread(got.reshape(-1, channels), nx, (strip,))
+    part, made = spread(got.reshape(-1, channels), nx, (made,))
     mine = exchange(part, ALONG_X).reshape(-1, channels)
     new_field, field_grad = backward(tables, wide, (dmixed, north, south, strip), made, upstream)
     mine, new_field, field_grad = after(mine, new_field, field_grad)

time: 127 us -> 128 us (level)
  waiting for transfers between devices: 22 us -> 31.4 us
  blocking collectives: 35 us -> 29.5 us
  starting transfers between devices: 51.5 us -> 48 us
    ppermute x2, waiting for transfers between devices: 7.59 us -> 15 us  [lat_blocks(): north = lax.ppermute(block, LAT, [(i, i + 1) for i in range(ends)])]
    all_to_all x2, blocking collectives: 35 us -> 29.5 us  [exchange(): return lax.all_to_all(pieces, axes, 0, 0, tiled=True)]
    ppermute x3 -> x1, starting transfers between devices: 16.8 us -> 12.6 us  [shards(): lax.ppermute(strip_for_west(field, north, south, upstream), 'lon', lon_sh...]
    ppermute x3 -> x1, waiting for transfers between devices: 1.39 us -> 5.07 us  [shards(): lax.ppermute(strip_for_west(field, north, south, upstream), 'lon', lon_sh...]
    ppermute x1, waiting for transfers between devices: 1.91 us -> 0.01 us  [shards(): strip = lax.ppermute(strip, 'lon', lon_shift(1))]
  transfers between devices with their start and end apart: 13 -> 11, of which waited for: 8 -> 8; matrix products, arithmetic and copies ran while one was open for 2% -> 2% of each run, Pallas kernels for 3% -> 4%
where the time goes in v9:
time: 128 us; the launch traced here: 127 us
  starting transfers between devices  48 us (38%)
  waiting for transfers between devices  31.4 us (25%)
  blocking collectives  29.5 us (23%)
  Pallas kernels  12 us (9%)
  local copies, waits for them, and re-layouts  5.22 us (4%)
    all_to_all x2, blocking collectives, exchange(): return lax.all_to_all(pieces, axes, 0, 0, tiled=True)  29.5 us
    ppermute x2, waiting for transfers between devices, lat_blocks(): north = lax.ppermute(block, LAT, [(i, i + 1) for i in range(ends)])  15 us
    ppermute x1, starting transfers between devices, shards(): lax.ppermute(strip_for_west(field, north, south, upstream), 'lon', lon_sh...  12.6 us
    all_to_all x3, starting transfers between devices, exchange(): return lax.all_to_all(pieces, axes, 0, 0, tiled=True)  11.9 us
    ppermute x2, starting transfers between devices, core_swap(): return lax.ppermute(block, 'core', [(0, 1), (1, 0)])  9.12 us
    ppermute x2, starting transfers between devices, lat_blocks(): north = lax.ppermute(block, LAT, [(i, i + 1) for i in range(ends)])  8.59 us
    all_to_all x3, waiting for transfers between devices, exchange(): return lax.all_to_all(pieces, axes, 0, 0, tiled=True)  6.7 us
    unnamed x18, local copies, waits for them, and re-layouts  5.22 us
  transfers between devices with their start and end apart: 11, of which 8 were waited for; matrix products, arithmetic and copies ran while one was open for 2% of the time, Pallas kernels for 4%

profile of v9, /device:TPU:1, one launch (start us, length us, event | category | flops | bytes accessed | tf_op | source)
XLA Modules:
  0.0 126.9 jit_solution(8060236499999804374)
XLA Ops:
  1.8 1.3 %collective-permute-start.1 = (bf16[2,180,384]{2,1,0:T(8,128)(2,1)S(1)}, bf16[2,180,384]{2,1,0:T(8,128)(2,1)S(1)}, u32[]{:S(2)}, u32[]{:S(2)}) collective-permute-start(bf16[2,180,384]{2,1,0:T(8,128)(2,1)S(1)} %bitcast.20), channel_id=1, source_target_pairs={{8,0},{16,8},{24,16},{32,24},{40,32},{48,40},{56,48},{64,56},{72,6... | collective-permute-start | bytes 829448 | tf_op jit(solution)/shard_map/ppermute | solution.py:224
  3.1 4.6 %collective-permute-start = (bf16[2,180,384]{2,1,0:T(8,128)(2,1)S(1)}, bf16[2,180,384]{2,1,0:T(8,128)(2,1)S(1)}, u32[]{:S(2)}, u32[]{:S(2)}) collective-permute-start(bf16[2,180,384]{2,1,0:T(8,128)(2,1)S(1)} %bitcast.21), channel_id=1, source_target_pairs={{0,8},{8,16},{16,24},{24,32},{32,40},{40,48},{48,56},{56,64},{64,7... | collective-permute-start | bytes 829448 | tf_op jit(solution)/shard_map/ppermute | solution.py:223
  9.7 7.5 %collective-permute-done.north.refs_7_ = bf16[2,180,384]{2,1,0:T(8,128)(2,1)S(1)} collective-permute-done((bf16[2,180,384]{2,1,0:T(8,128)(2,1)S(1)}, bf16[2,180,384]{2,1,0:T(8,128)(2,1)S(1)}, u32[]{:S(2)}, u32[]{:S(2)}) %collective-permute-start) | collective-permute-done | bytes 276512 | tf_op jit(solution)/shard_map/ppermute | solution.py:223
  17.2 12.6 %collective-permute-start.2 = (bf16[2,168,384]{2,1,0:T(8,128)(2,1)S(1)}, bf16[2,168,384]{2,1,0:T(8,128)(2,1)S(1)}, u32[]{:S(2)}, u32[]{:S(2)}) collective-permute-start(bf16[2,168,384]{2,1,0:T(8,128)(2,1)S(1)} %shard_map.103), channel_id=1, source_target_pairs={{0,7},{1,0},{2,1},{3,2},{4,3},{5,4},{6,5},{7,6},{8,15},{9,8},{10,9... | collective-permute-start | bytes 774152 | tf_op jit(solution)/shard_map/ppermute | solution.py:379
  29.8 5.1 %collective-permute-done.2.refs_9_ = bf16[2,168,384]{2,1,0:T(8,128)(2,1)S(1)} collective-permute-done((bf16[2,168,384]{2,1,0:T(8,128)(2,1)S(1)}, bf16[2,168,384]{2,1,0:T(8,128)(2,1)S(1)}, u32[]{:S(2)}, u32[]{:S(2)}) %collective-permute-start.2) | collective-permute-done | bytes 258080 | tf_op jit(solution)/shard_map/ppermute | solution.py:379
  34.9 4.0 %shard_map.104 = (bf16[2,180,384]{2,1,0:T(8,128)(2,1)S(1)}, bf16[2,180,384]{2,1,0:T(8,128)(2,1)S(1)}, f32[768,384]{1,0:T(8,128)S(1)}, bf16[768,384]{1,0:T(8,128)(2,1)S(1)}) custom-call(s32[16,32]{1,0:T(8,128)S(1)} %bitcast.29, s32[16,32]{1,0:T(8,128)S(1)} %bitcast.31, s32[16,32]{1,0:T(8,128)S(1)} %bitcast.33, f32[16,32]{1,0:T(8,128)S(1)} %bitcast.35, ...), custom_call_target="tpu_custom_call" | custom-call | flops 2000000000 | bytes 8000000 | tf_op jit(solution)/shard_map/pallas_call | solution.py:135
  39.0 3.2 %collective-permute-start.3 = (bf16[768,384]{1,0:T(8,128)(2,1)S(1)}, bf16[768,384]{1,0:T(8,128)(2,1)S(1)}, u32[]{:S(2)}, u32[]{:S(2)}) collective-permute-start(bf16[768,384]{1,0:T(8,128)(2,1)S(1)} %get-tuple-element.19), channel_id=1, source_target_pairs={{0,128},{128,0},{1,129},{129,1},{2,130},{130,2},{3,131},{131,3},{4... | collective-permute-start | bytes 1769480 | tf_op jit(solution)/shard_map/ppermute | solution.py:251
  42.2 1.6 %collective-permute-done.3.got = bf16[768,384]{1,0:T(8,128)(2,1)S(1)} collective-permute-done((bf16[768,384]{1,0:T(8,128)(2,1)S(1)}, bf16[768,384]{1,0:T(8,128)(2,1)S(1)}, u32[]{:S(2)}, u32[]{:S(2)}) %collective-permute-start.3) | collective-permute-done | bytes 589856 | tf_op jit(solution)/shard_map/ppermute | solution.py:251
  44.0 14.2 %all_to_all.25.refs_0_ = bf16[4,192,384]{2,1,0:T(8,128)(2,1)S(1)} all-to-all(bf16[4,192,384]{2,1,0:T(8,128)(2,1)S(1)} %shard_map.105), channel_id=1, replica_groups=mesh['x_hi'=2,'core'=2,'y'=8,'x_lo'=2,'lon'=8] {'x_hi','x_lo'}, dimensions={0} | all-to-all | bytes 1179648 | tf_op jit(solution)/shard_map/all_to_all | solution.py:369
  58.2 15.3 %all_to_all.26.refs_0_ = bf16[8,24,384]{2,1,0:T(8,128)(2,1)S(1)} all-to-all(bf16[8,24,384]{2,1,0:T(8,128)(2,1)S(1)} %get-tuple-element.21), channel_id=1, replica_groups=mesh['x_hi'=2,'core'=2,'y'=8,'x_lo'=2,'lon'=8] {'y'}, dimensions={0} | all-to-all | bytes 294912 | tf_op jit(solution)/shard_map/all_to_all | solution.py:369
  74.3 4.7 %all-to-all-start.2 = ((f32[8,24,384]{2,1,0:T(8,128)}), f32[8,24,384]{2,1,0:T(8,128)S(1)}, u32[]{:S(2)}, u32[]{:S(2)}) async-start(f32[8,24,384]{2,1,0:T(8,128)} %shard_map.107), calls=%async_computation.2 | async-start | bytes 589824 | tf_op jit(solution)/shard_map/all_to_all | solution.py:369
  79.0 1.3 %collective-permute-start.5 = (bf16[2,180,384]{2,1,0:T(8,128)(2,1)S(1)}, bf16[2,180,384]{2,1,0:T(8,128)(2,1)S(1)}, u32[]{:S(2)}, u32[]{:S(2)}) collective-permute-start(bf16[2,180,384]{2,1,0:T(8,128)(2,1)S(1)} %get-tuple-element.22.dmixed.own), channel_id=1, source_target_pairs={{8,0},{16,8},{24,16},{32,24},{40,32},{48,40},{56,48},{64,56},{72,6... | collective-permute-start | bytes 829448 | tf_op jit(solution)/shard_map/ppermute | solution.py:224
  80.3 4.0 %collective-permute-start.4 = (bf16[2,180,384]{2,1,0:T(8,128)(2,1)S(1)}, bf16[2,180,384]{2,1,0:T(8,128)(2,1)S(1)}, u32[]{:S(2)}, u32[]{:S(2)}) collective-permute-start(bf16[2,180,384]{2,1,0:T(8,128)(2,1)S(1)} %get-tuple-element.22.dmixed.own), channel_id=1, source_target_pairs={{0,8},{8,16},{16,24},{24,32},{32,40},{40,48},{48,56},{56,64},{64,7... | collective-permute-start | bytes 829448 | tf_op jit(solution)/shard_map/ppermute | solution.py:223
  84.3 2.0 %collective-permute-done.5.south = bf16[2,180,384]{2,1,0:T(8,128)(2,1)S(1)} collective-permute-done((bf16[2,180,384]{2,1,0:T(8,128)(2,1)S(1)}, bf16[2,180,384]{2,1,0:T(8,128)(2,1)S(1)}, u32[]{:S(2)}, u32[]{:S(2)}) %collective-permute-start.5) | collective-permute-done | bytes 276512 | tf_op jit(solution)/shard_map/ppermute | solution.py:224
  86.3 7.6 %collective-permute-done.4.north = bf16[2,180,384]{2,1,0:T(8,128)(2,1)S(1)} collective-permute-done((bf16[2,180,384]{2,1,0:T(8,128)(2,1)S(1)}, bf16[2,180,384]{2,1,0:T(8,128)(2,1)S(1)}, u32[]{:S(2)}, u32[]{:S(2)}) %collective-permute-start.4) | collective-permute-done | bytes 276512 | tf_op jit(solution)/shard_map/ppermute | solution.py:223
  94.6 3.4 %all-to-all-start.3 = ((bf16[8,24,384]{2,1,0:T(8,128)(2,1)}), bf16[8,24,384]{2,1,0:T(8,128)(2,1)S(1)}, u32[]{:S(2)}, u32[]{:S(2)}) async-start(bf16[8,24,384]{2,1,0:T(8,128)(2,1)} %get-tuple-element.24), calls=%async_computation.3 | async-start | bytes 294912 | tf_op jit(solution)/shard_map/all_to_all | solution.py:369
  97.9 3.1 %collective-permute-start.6 = (bf16[2,168,384]{2,1,0:T(8,128)(2,1)S(1)}, bf16[2,168,384]{2,1,0:T(8,128)(2,1)S(1)}, u32[]{:S(2)}, u32[]{:S(2)}) collective-permute-start(bf16[2,168,384]{2,1,0:T(8,128)(2,1)S(1)} %get-tuple-element.26), channel_id=1, source_target_pairs={{0,1},{1,2},{2,3},{3,4},{4,5},{5,6},{6,7},{7,0},{8,9},{9,10},{10,1... | collective-permute-start | bytes 774152 | tf_op jit(solution)/shard_map/ppermute | solution.py:392
  101.0 4.9 %all-to-all-done.3 = bf16[8,24,384]{2,1,0:T(8,128)(2,1)S(1)} async-done(((bf16[8,24,384]{2,1,0:T(8,128)(2,1)}), bf16[8,24,384]{2,1,0:T(8,128)(2,1)S(1)}, u32[]{:S(2)}, u32[]{:S(2)}) %all-to-all-start.3) | async-done | bytes 147488 | tf_op jit(solution)/shard_map/all_to_all | solution.py:369
  106.8 3.9 %all-to-all-start.4 = ((bf16[4,192,384]{2,1,0:T(8,128)(2,1)}), bf16[4,192,384]{2,1,0:T(8,128)(2,1)S(1)}, u32[]{:S(2)}, u32[]{:S(2)}) async-start(bf16[4,192,384]{2,1,0:T(8,128)(2,1)} %get-tuple-element.25), calls=%async_computation.4 | async-start | bytes 1179648 | tf_op jit(solution)/shard_map/all_to_all | solution.py:369
  110.7 1.3 %copy-done.1 = bf16[4,384,384]{2,1,0:T(8,128)(2,1)S(1)} copy-done((bf16[4,384,384]{2,1,0:T(8,128)(2,1)S(1)}, bf16[4,384,384]{2,1,0:T(8,128)(2,1)}, u32[]{:S(2)}) %copy-start.1) | copy-done | bytes 1179672
  112.0 4.2 %shard_map.110 = (bf16[2,180,384]{2,1,0:T(8,128)(2,1)S(1)}, bf16[2,180,384]{2,1,0:T(8,128)(2,1)S(1)}) custom-call(s32[16,32]{1,0:T(8,128)S(1)} %bitcast.30, s32[16,32]{1,0:T(8,128)S(1)} %bitcast.32, s32[16,32]{1,0:T(8,128)S(1)} %bitcast.34, f32[16,32]{1,0:T(8,128)S(1)} %bitcast.36, s32[32]{0:T(128)S(1)} %copy-done.6, bf16[1536,384]{1,0:T(8,128)(2,1)S(1)} %bitcast.28, ...), custom_call_target="tpu_custom_call" | custom-call | flops 2500000000 | bytes 5000000 | tf_op jit(solution)/shard_map/pallas_call | solution.py:205
  116.2 1.8 %all-to-all-done.4 = bf16[4,192,384]{2,1,0:T(8,128)(2,1)S(1)} async-done(((bf16[4,192,384]{2,1,0:T(8,128)(2,1)}), bf16[4,192,384]{2,1,0:T(8,128)(2,1)S(1)}, u32[]{:S(2)}, u32[]{:S(2)}) %all-to-all-start.4) | async-done | bytes 589856 | tf_op jit(solution)/shard_map/all_to_all | solution.py:369
  118.0 5.9 %collective-permute-start.7 = (bf16[768,384]{1,0:T(8,128)(2,1)S(1)}, bf16[768,384]{1,0:T(8,128)(2,1)S(1)}, u32[]{:S(2)}, u32[]{:S(2)}) collective-permute-start(bf16[768,384]{1,0:T(8,128)(2,1)S(1)} %get-tuple-element.32.mine), channel_id=1, source_target_pairs={{0,128},{128,0},{1,129},{129,1},{2,130},{130,2},{3,131},{131,3},{4... | collective-permute-start | bytes 1769480 | tf_op jit(solution)/shard_map/ppermute | solution.py:251
  125.7 1.2 shard_map.112
  (28 shorter events, 7.5 us)
Async XLA Ops:
  0.6 34.3 %copy-start.6 = (s32[32]{0:T(128)S(1)}, s32[32]{0:T(128)}, u32[]{:S(2)}) copy-start(s32[32]{0:T(128)} %tap_count.1) | copy-start | bytes 388
  0.6 34.3 %copy-start.5 = (f32[32,16]{0,1:T(8,128)S(1)}, f32[32,16]{0,1:T(8,128)}, u32[]{:S(2)}) copy-start(f32[32,16]{0,1:T(8,128)} %param.14) | copy-start | bytes 6148
  0.7 34.3 %copy-start.4 = (s32[32,16]{0,1:T(8,128)S(1)}, s32[32,16]{0,1:T(8,128)}, u32[]{:S(2)}) copy-start(s32[32,16]{0,1:T(8,128)} %param.13) | copy-start | bytes 6148
  0.7 34.3 %copy-start.3 = (s32[32,16]{0,1:T(8,128)S(1)}, s32[32,16]{0,1:T(8,128)}, u32[]{:S(2)}) copy-start(s32[32,16]{0,1:T(8,128)} %param.12) | copy-start | bytes 6148
  0.7 34.3 %copy-start.2 = (s32[32,16]{0,1:T(8,128)S(1)}, s32[32,16]{0,1:T(8,128)}, u32[]{:S(2)}) copy-start(s32[32,16]{0,1:T(8,128)} %param.11) | copy-start | bytes 6148
  0.7 34.3 %copy-start = (bf16[4,384,384]{2,1,0:T(8,128)(2,1)S(1)}, bf16[4,384,384]{2,1,0:T(8,128)(2,1)}, u32[]{:S(2)}) copy-start(bf16[4,384,384]{2,1,0:T(8,128)(2,1)} %param.10) | copy-start | bytes 3538948
  1.8 7.9 %collective-permute-start.1 = (bf16[2,180,384]{2,1,0:T(8,128)(2,1)S(1)}, bf16[2,180,384]{2,1,0:T(8,128)(2,1)S(1)}, u32[]{:S(2)}, u32[]{:S(2)}) collective-permute-start(bf16[2,180,384]{2,1,0:T(8,128)(2,1)S(1)} %bitcast.20), channel_id=1, source_target_pairs={{8,0},{16,8},{24,16},{32,24},{40,32},{48,40},{56,48},{64,56},{72,6... | collective-permute-start | bytes 829448 | tf_op jit(solution)/shard_map/ppermute | solution.py:224
  3.1 14.1 %collective-permute-start = (bf16[2,180,384]{2,1,0:T(8,128)(2,1)S(1)}, bf16[2,180,384]{2,1,0:T(8,128)(2,1)S(1)}, u32[]{:S(2)}, u32[]{:S(2)}) collective-permute-start(bf16[2,180,384]{2,1,0:T(8,128)(2,1)S(1)} %bitcast.21), channel_id=1, source_target_pairs={{0,8},{8,16},{16,24},{24,32},{32,40},{40,48},{48,56},{56,64},{64,7... | collective-permute-start | bytes 829448 | tf_op jit(solution)/shard_map/ppermute | solution.py:223
  17.2 17.7 %collective-permute-start.2 = (bf16[2,168,384]{2,1,0:T(8,128)(2,1)S(1)}, bf16[2,168,384]{2,1,0:T(8,128)(2,1)S(1)}, u32[]{:S(2)}, u32[]{:S(2)}) collective-permute-start(bf16[2,168,384]{2,1,0:T(8,128)(2,1)S(1)} %shard_map.103), channel_id=1, source_target_pairs={{0,7},{1,0},{2,1},{3,2},{4,3},{5,4},{6,5},{7,6},{8,15},{9,8},{10,9... | collective-permute-start | bytes 774152 | tf_op jit(solution)/shard_map/ppermute | solution.py:379
  39.0 4.9 %collective-permute-start.3 = (bf16[768,384]{1,0:T(8,128)(2,1)S(1)}, bf16[768,384]{1,0:T(8,128)(2,1)S(1)}, u32[]{:S(2)}, u32[]{:S(2)}) collective-permute-start(bf16[768,384]{1,0:T(8,128)(2,1)S(1)} %get-tuple-element.19), channel_id=1, source_target_pairs={{0,128},{128,0},{1,129},{129,1},{2,130},{130,2},{3,131},{131,3},{4... | collective-permute-start | bytes 1769480 | tf_op jit(solution)/shard_map/ppermute | solution.py:251
  74.3 19.6 %all-to-all-start.2 = ((f32[8,24,384]{2,1,0:T(8,128)}), f32[8,24,384]{2,1,0:T(8,128)S(1)}, u32[]{:S(2)}, u32[]{:S(2)}) async-start(f32[8,24,384]{2,1,0:T(8,128)} %shard_map.107), calls=%async_computation.2 | async-start | bytes 589824 | tf_op jit(solution)/shard_map/all_to_all | solution.py:369
  79.0 7.3 %collective-permute-start.5 = (bf16[2,180,384]{2,1,0:T(8,128)(2,1)S(1)}, bf16[2,180,384]{2,1,0:T(8,128)(2,1)S(1)}, u32[]{:S(2)}, u32[]{:S(2)}) collective-permute-start(bf16[2,180,384]{2,1,0:T(8,128)(2,1)S(1)} %get-tuple-element.22.dmixed.own), channel_id=1, source_target_pairs={{8,0},{16,8},{24,16},{32,24},{40,32},{48,40},{56,48},{64,56},{72,6... | collective-permute-start | bytes 829448 | tf_op jit(solution)/shard_map/ppermute | solution.py:224
  80.3 13.6 %collective-permute-start.4 = (bf16[2,180,384]{2,1,0:T(8,128)(2,1)S(1)}, bf16[2,180,384]{2,1,0:T(8,128)(2,1)S(1)}, u32[]{:S(2)}, u32[]{:S(2)}) collective-permute-start(bf16[2,180,384]{2,1,0:T(8,128)(2,1)S(1)} %get-tuple-element.22.dmixed.own), channel_id=1, source_target_pairs={{0,8},{8,16},{16,24},{24,32},{32,40},{40,48},{48,56},{56,64},{64,7... | collective-permute-start | bytes 829448 | tf_op jit(solution)/shard_map/ppermute | solution.py:223
  94.6 11.4 %all-to-all-start.3 = ((bf16[8,24,384]{2,1,0:T(8,128)(2,1)}), bf16[8,24,384]{2,1,0:T(8,128)(2,1)S(1)}, u32[]{:S(2)}, u32[]{:S(2)}) async-start(bf16[8,24,384]{2,1,0:T(8,128)(2,1)} %get-tuple-element.24), calls=%async_computation.3 | async-start | bytes 294912 | tf_op jit(solution)/shard_map/all_to_all | solution.py:369
  97.9 12.8 %collective-permute-start.6 = (bf16[2,168,384]{2,1,0:T(8,128)(2,1)S(1)}, bf16[2,168,384]{2,1,0:T(8,128)(2,1)S(1)}, u32[]{:S(2)}, u32[]{:S(2)}) collective-permute-start(bf16[2,168,384]{2,1,0:T(8,128)(2,1)S(1)} %get-tuple-element.26), channel_id=1, source_target_pairs={{0,1},{1,2},{2,3},{3,4},{4,5},{5,6},{6,7},{7,0},{8,9},{9,10},{10,1... | collective-permute-start | bytes 774152 | tf_op jit(solution)/shard_map/ppermute | solution.py:392
  106.8 11.2 %all-to-all-start.4 = ((bf16[4,192,384]{2,1,0:T(8,128)(2,1)}), bf16[4,192,384]{2,1,0:T(8,128)(2,1)S(1)}, u32[]{:S(2)}, u32[]{:S(2)}) async-start(bf16[4,192,384]{2,1,0:T(8,128)(2,1)} %get-tuple-element.25), calls=%async_computation.4 | async-start | bytes 1179648 | tf_op jit(solution)/shard_map/all_to_all | solution.py:369
  110.7 1.3 %copy-start.1 = (bf16[4,384,384]{2,1,0:T(8,128)(2,1)S(1)}, bf16[4,384,384]{2,1,0:T(8,128)(2,1)}, u32[]{:S(2)}) copy-start(bf16[4,384,384]{2,1,0:T(8,128)(2,1)} %param.10) | copy-start | bytes 3538948
  118.0 7.7 %collective-permute-start.7 = (bf16[768,384]{1,0:T(8,128)(2,1)S(1)}, bf16[768,384]{1,0:T(8,128)(2,1)S(1)}, u32[]{:S(2)}, u32[]{:S(2)}) collective-permute-start(bf16[768,384]{1,0:T(8,128)(2,1)S(1)} %get-tuple-element.32.mine), channel_id=1, source_target_pairs={{0,128},{128,0},{1,129},{129,1},{2,130},{130,2},{3,131},{131,3},{4... | collective-permute-start | bytes 1769480 | tf_op jit(solution)/shard_map/ppermute | solution.py:251

commit v10 on v6

--- a/solution.py
+++ b/solution.py
@@ -382,7 +382,7 @@
     part, strip = sum_and_strip(got, ny, dmixed, north, south, made)
     strip = lax.ppermute(strip, "lon", lon_shift(1))
     got = exchange(part, "y")
-    part, strip = spread(got.reshape(-1, channels), nx, (strip,))
+    part, made = spread(got.reshape(-1, channels), nx, (made,))
     mine = exchange(part, ALONG_X).reshape(-1, channels)
     new_field, field_grad = backward(tables, wide, (dmixed, north, south, strip), made, upstream)
     mine, new_field, field_grad = after(mine, new_field, field_grad)

time: 127 us -> 125 us (0.984)
  waiting for transfers between devices: 22 us -> 19.5 us
    ppermute x1, waiting for transfers between devices: 1.91 us -> 0.01 us  [shards(): strip = lax.ppermute(strip, 'lon', lon_shift(1))]
  transfers between devices with their start and end apart: 13 -> 13, of which waited for: 8 -> 7; matrix products, arithmetic and copies ran while one was open for 2% -> 2% of each run, Pallas kernels for 3% -> 4%
where the time goes in v10:
time: 125 us; the launch traced here: 124 us
  starting transfers between devices  51.8 us (41%)
  blocking collectives  34.9 us (28%)
  waiting for transfers between devices  19.5 us (16%)
  Pallas kernels  12 us (10%)
  local copies, waits for them, and re-layouts  5.23 us (4%)
    all_to_all x2, blocking collectives, exchange(): return lax.all_to_all(pieces, axes, 0, 0, tiled=True)  34.9 us
    ppermute x1, starting transfers between devices, lon_strips(): level = lax.ppermute(side, 'lon', along)  10.9 us
    all_to_all x3, starting transfers between devices, exchange(): return lax.all_to_all(pieces, axes, 0, 0, tiled=True)  10.9 us
    ppermute x2, starting transfers between devices, core_swap(): return lax.ppermute(block, 'core', [(0, 1), (1, 0)])  10 us
    ppermute x2, starting transfers between devices, lat_blocks(): north = lax.ppermute(block, LAT, [(i, i + 1) for i in range(ends)])  8.59 us
    ppermute x2, waiting for transfers between devices, lat_blocks(): north = lax.ppermute(block, LAT, [(i, i + 1) for i in range(ends)])  7.59 us
    all_to_all x3, waiting for transfers between devices, exchange(): return lax.all_to_all(pieces, axes, 0, 0, tiled=True)  6.58 us
    unnamed x18, local copies, waits for them, and re-layouts  5.22 us
  transfers between devices with their start and end apart: 13, of which 7 were waited for; matrix products, arithmetic and copies ran while one was open for 2% of the time, Pallas kernels for 4%

profile of v10, /device:TPU:1, one launch (start us, length us, event | category | flops | bytes accessed | tf_op | source)
XLA Modules:
  0.0 124.4 jit_solution(5423612444588304784)
XLA Ops:
  1.8 1.3 %collective-permute-start.1 = (bf16[2,180,384]{2,1,0:T(8,128)(2,1)S(1)}, bf16[2,180,384]{2,1,0:T(8,128)(2,1)S(1)}, u32[]{:S(2)}, u32[]{:S(2)}) collective-permute-start(bf16[2,180,384]{2,1,0:T(8,128)(2,1)S(1)} %bitcast.20), channel_id=1, source_target_pairs={{8,0},{16,8},{24,16},{32,24},{40,32},{48,40},{56,48},{64,56},{72,6... | collective-permute-start | bytes 829448 | tf_op jit(solution)/shard_map/ppermute | solution.py:224
  3.1 4.6 %collective-permute-start = (bf16[2,180,384]{2,1,0:T(8,128)(2,1)S(1)}, bf16[2,180,384]{2,1,0:T(8,128)(2,1)S(1)}, u32[]{:S(2)}, u32[]{:S(2)}) collective-permute-start(bf16[2,180,384]{2,1,0:T(8,128)(2,1)S(1)} %bitcast.21), channel_id=1, source_target_pairs={{0,8},{8,16},{16,24},{24,32},{32,40},{40,48},{48,56},{56,64},{64,7... | collective-permute-start | bytes 829448 | tf_op jit(solution)/shard_map/ppermute | solution.py:223
  8.7 10.9 %collective-permute-start.2 = (bf16[2,72,384]{2,1,0:T(8,128)(2,1)S(1)}, bf16[2,72,384]{2,1,0:T(8,128)(2,1)S(1)}, u32[]{:S(2)}, u32[]{:S(2)}) collective-permute-start(bf16[2,72,384]{2,1,0:T(8,128)(2,1)S(1)} %pad_maximum_fusion), channel_id=1, source_target_pairs={{0,7},{1,0},{2,1},{3,2},{4,3},{5,4},{6,5},{7,6},{8,15},{9,8},{10,9... | collective-permute-start | bytes 331784 | tf_op jit(solution)/shard_map/ppermute | solution.py:236
  19.6 1.3 %collective-permute-start.4 = (bf16[2,48,384]{2,1,0:T(8,128)(2,1)S(1)}, bf16[2,48,384]{2,1,0:T(8,128)(2,1)S(1)}, u32[]{:S(2)}, u32[]{:S(2)}) collective-permute-start(bf16[2,48,384]{2,1,0:T(8,128)(2,1)S(1)} %slice.9), channel_id=1, source_target_pairs={{8,7},{9,0},{10,1},{11,2},{12,3},{13,4},{14,5},{15,6},{16,15},{17,... | collective-permute-start | bytes 221192 | tf_op jit(solution)/shard_map/ppermute | solution.py:238
  20.9 4.6 %collective-permute-start.3 = (bf16[2,48,384]{2,1,0:T(8,128)(2,1)S(1)}, bf16[2,48,384]{2,1,0:T(8,128)(2,1)S(1)}, u32[]{:S(2)}, u32[]{:S(2)}) collective-permute-start(bf16[2,48,384]{2,1,0:T(8,128)(2,1)S(1)} %slice.9), channel_id=1, source_target_pairs={{0,15},{1,8},{2,9},{3,10},{4,11},{5,12},{6,13},{7,14},{8,23},{9,16... | collective-permute-start | bytes 221192 | tf_op jit(solution)/shard_map/ppermute | solution.py:237
  25.6 1.3 %collective-permute-done.3.refs_10_ = bf16[2,48,384]{2,1,0:T(8,128)(2,1)S(1)} collective-permute-done((bf16[2,48,384]{2,1,0:T(8,128)(2,1)S(1)}, bf16[2,48,384]{2,1,0:T(8,128)(2,1)S(1)}, u32[]{:S(2)}, u32[]{:S(2)}) %collective-permute-start.3) | collective-permute-done | bytes 73760 | tf_op jit(solution)/shard_map/ppermute | solution.py:237
  27.0 3.9 %shard_map.103 = (bf16[2,180,384]{2,1,0:T(8,128)(2,1)S(1)}, bf16[2,180,384]{2,1,0:T(8,128)(2,1)S(1)}, f32[768,384]{1,0:T(8,128)S(1)}, bf16[768,384]{1,0:T(8,128)(2,1)S(1)}) custom-call(s32[16,32]{1,0:T(8,128)S(1)} %bitcast.29, s32[16,32]{1,0:T(8,128)S(1)} %bitcast.31, s32[16,32]{1,0:T(8,128)S(1)} %bitcast.33, f32[16,32]{1,0:T(8,128)S(1)} %bitcast.35, ...), custom_call_target="tpu_custom_call" | custom-call | flops 2000000000 | bytes 8000000 | tf_op jit(solution)/shard_map/pallas_call | solution.py:135
  31.0 4.3 %collective-permute-start.5 = (bf16[768,384]{1,0:T(8,128)(2,1)S(1)}, bf16[768,384]{1,0:T(8,128)(2,1)S(1)}, u32[]{:S(2)}, u32[]{:S(2)}) collective-permute-start(bf16[768,384]{1,0:T(8,128)(2,1)S(1)} %get-tuple-element.19), channel_id=1, source_target_pairs={{0,128},{128,0},{1,129},{129,1},{2,130},{130,2},{3,131},{131,3},{4... | collective-permute-start | bytes 1769480 | tf_op jit(solution)/shard_map/ppermute | solution.py:243
  35.3 1.6 %collective-permute-done.5.got = bf16[768,384]{1,0:T(8,128)(2,1)S(1)} collective-permute-done((bf16[768,384]{1,0:T(8,128)(2,1)S(1)}, bf16[768,384]{1,0:T(8,128)(2,1)S(1)}, u32[]{:S(2)}, u32[]{:S(2)}) %collective-permute-start.5) | collective-permute-done | bytes 589856 | tf_op jit(solution)/shard_map/ppermute | solution.py:243
  37.0 15.1 %all_to_all.25.refs_0_ = bf16[4,192,384]{2,1,0:T(8,128)(2,1)S(1)} all-to-all(bf16[4,192,384]{2,1,0:T(8,128)(2,1)S(1)} %shard_map.104), channel_id=1, replica_groups=mesh['x_hi'=2,'core'=2,'y'=8,'x_lo'=2,'lon'=8] {'x_hi','x_lo'}, dimensions={0} | all-to-all | bytes 1179648 | tf_op jit(solution)/shard_map/all_to_all | solution.py:361
  52.2 19.8 %all_to_all.26.refs_0_ = bf16[8,24,384]{2,1,0:T(8,128)(2,1)S(1)} all-to-all(bf16[8,24,384]{2,1,0:T(8,128)(2,1)S(1)} %get-tuple-element.21), channel_id=1, replica_groups=mesh['x_hi'=2,'core'=2,'y'=8,'x_lo'=2,'lon'=8] {'y'}, dimensions={0} | all-to-all | bytes 294912 | tf_op jit(solution)/shard_map/all_to_all | solution.py:361
  72.8 3.4 %all-to-all-start.2 = ((f32[8,24,384]{2,1,0:T(8,128)}), f32[8,24,384]{2,1,0:T(8,128)S(1)}, u32[]{:S(2)}, u32[]{:S(2)}) async-start(f32[8,24,384]{2,1,0:T(8,128)} %shard_map.106), calls=%async_computation.2 | async-start | bytes 589824 | tf_op jit(solution)/shard_map/all_to_all | solution.py:361
  76.2 1.3 %collective-permute-start.7 = (bf16[2,180,384]{2,1,0:T(8,128)(2,1)S(1)}, bf16[2,180,384]{2,1,0:T(8,128)(2,1)S(1)}, u32[]{:S(2)}, u32[]{:S(2)}) collective-permute-start(bf16[2,180,384]{2,1,0:T(8,128)(2,1)S(1)} %get-tuple-element.22.dmixed.own), channel_id=1, source_target_pairs={{8,0},{16,8},{24,16},{32,24},{40,32},{48,40},{56,48},{64,56},{72,6... | collective-permute-start | bytes 829448 | tf_op jit(solution)/shard_map/ppermute | solution.py:224
  77.5 4.0 %collective-permute-start.6 = (bf16[2,180,384]{2,1,0:T(8,128)(2,1)S(1)}, bf16[2,180,384]{2,1,0:T(8,128)(2,1)S(1)}, u32[]{:S(2)}, u32[]{:S(2)}) collective-permute-start(bf16[2,180,384]{2,1,0:T(8,128)(2,1)S(1)} %get-tuple-element.22.dmixed.own), channel_id=1, source_target_pairs={{0,8},{8,16},{16,24},{24,32},{32,40},{40,48},{48,56},{56,64},{64,7... | collective-permute-start | bytes 829448 | tf_op jit(solution)/shard_map/ppermute | solution.py:223
  81.5 2.3 %collective-permute-done.7.south = bf16[2,180,384]{2,1,0:T(8,128)(2,1)S(1)} collective-permute-done((bf16[2,180,384]{2,1,0:T(8,128)(2,1)S(1)}, bf16[2,180,384]{2,1,0:T(8,128)(2,1)S(1)}, u32[]{:S(2)}, u32[]{:S(2)}) %collective-permute-start.7) | collective-permute-done | bytes 276512 | tf_op jit(solution)/shard_map/ppermute | solution.py:224
  83.8 7.6 %collective-permute-done.6.north = bf16[2,180,384]{2,1,0:T(8,128)(2,1)S(1)} collective-permute-done((bf16[2,180,384]{2,1,0:T(8,128)(2,1)S(1)}, bf16[2,180,384]{2,1,0:T(8,128)(2,1)S(1)}, u32[]{:S(2)}, u32[]{:S(2)}) %collective-permute-start.6) | collective-permute-done | bytes 276512 | tf_op jit(solution)/shard_map/ppermute | solution.py:223
  92.1 3.4 %all-to-all-start.3 = ((bf16[8,24,384]{2,1,0:T(8,128)(2,1)}), bf16[8,24,384]{2,1,0:T(8,128)(2,1)S(1)}, u32[]{:S(2)}, u32[]{:S(2)}) async-start(bf16[8,24,384]{2,1,0:T(8,128)(2,1)} %get-tuple-element.24), calls=%async_computation.3 | async-start | bytes 294912 | tf_op jit(solution)/shard_map/all_to_all | solution.py:361
  95.5 2.9 %collective-permute-start.8 = (bf16[2,168,384]{2,1,0:T(8,128)(2,1)S(1)}, bf16[2,168,384]{2,1,0:T(8,128)(2,1)S(1)}, u32[]{:S(2)}, u32[]{:S(2)}) collective-permute-start(bf16[2,168,384]{2,1,0:T(8,128)(2,1)S(1)} %get-tuple-element.26), channel_id=1, source_target_pairs={{0,1},{1,2},{2,3},{3,4},{4,5},{5,6},{6,7},{7,0},{8,9},{9,10},{10,1... | collective-permute-start | bytes 774152 | tf_op jit(solution)/shard_map/ppermute | solution.py:383
  98.4 4.9 %all-to-all-done.3 = bf16[8,24,384]{2,1,0:T(8,128)(2,1)S(1)} async-done(((bf16[8,24,384]{2,1,0:T(8,128)(2,1)}), bf16[8,24,384]{2,1,0:T(8,128)(2,1)S(1)}, u32[]{:S(2)}, u32[]{:S(2)}) %all-to-all-start.3) | async-done | bytes 147488 | tf_op jit(solution)/shard_map/all_to_all | solution.py:361
  104.2 4.1 %all-to-all-start.4 = ((bf16[4,192,384]{2,1,0:T(8,128)(2,1)}), bf16[4,192,384]{2,1,0:T(8,128)(2,1)S(1)}, u32[]{:S(2)}, u32[]{:S(2)}) async-start(bf16[4,192,384]{2,1,0:T(8,128)(2,1)} %get-tuple-element.25), calls=%async_computation.4 | async-start | bytes 1179648 | tf_op jit(solution)/shard_map/all_to_all | solution.py:361
  108.3 1.3 %copy-done.1 = bf16[4,384,384]{2,1,0:T(8,128)(2,1)S(1)} copy-done((bf16[4,384,384]{2,1,0:T(8,128)(2,1)S(1)}, bf16[4,384,384]{2,1,0:T(8,128)(2,1)}, u32[]{:S(2)}) %copy-start.1) | copy-done | bytes 1179672
  109.6 4.3 %shard_map.109 = (bf16[2,180,384]{2,1,0:T(8,128)(2,1)S(1)}, bf16[2,180,384]{2,1,0:T(8,128)(2,1)S(1)}) custom-call(s32[16,32]{1,0:T(8,128)S(1)} %bitcast.30, s32[16,32]{1,0:T(8,128)S(1)} %bitcast.32, s32[16,32]{1,0:T(8,128)S(1)} %bitcast.34, f32[16,32]{1,0:T(8,128)S(1)} %bitcast.36, s32[32]{0:T(128)S(1)} %copy-done.6, bf16[1536,384]{1,0:T(8,128)(2,1)S(1)} %bitcast.28, ...), custom_call_target="tpu_custom_call" | custom-call | flops 2500000000 | bytes 5000000 | tf_op jit(solution)/shard_map/pallas_call | solution.py:205
  113.9 1.7 %all-to-all-done.4 = bf16[4,192,384]{2,1,0:T(8,128)(2,1)S(1)} async-done(((bf16[4,192,384]{2,1,0:T(8,128)(2,1)}), bf16[4,192,384]{2,1,0:T(8,128)(2,1)S(1)}, u32[]{:S(2)}, u32[]{:S(2)}) %all-to-all-start.4) | async-done | bytes 589856 | tf_op jit(solution)/shard_map/all_to_all | solution.py:361
  115.6 5.7 %collective-permute-start.9 = (bf16[768,384]{1,0:T(8,128)(2,1)S(1)}, bf16[768,384]{1,0:T(8,128)(2,1)S(1)}, u32[]{:S(2)}, u32[]{:S(2)}) collective-permute-start(bf16[768,384]{1,0:T(8,128)(2,1)S(1)} %get-tuple-element.32.mine), channel_id=1, source_target_pairs={{0,128},{128,0},{1,129},{129,1},{2,130},{130,2},{3,131},{131,3},{4... | collective-permute-start | bytes 1769480 | tf_op jit(solution)/shard_map/ppermute | solution.py:243
  (34 shorter events, 7.8 us)
Async XLA Ops:
  0.6 26.3 %copy-start.6 = (s32[32]{0:T(128)S(1)}, s32[32]{0:T(128)}, u32[]{:S(2)}) copy-start(s32[32]{0:T(128)} %tap_count.1) | copy-start | bytes 388
  0.6 26.3 %copy-start.5 = (f32[32,16]{0,1:T(8,128)S(1)}, f32[32,16]{0,1:T(8,128)}, u32[]{:S(2)}) copy-start(f32[32,16]{0,1:T(8,128)} %param.14) | copy-start | bytes 6148
  0.7 26.3 %copy-start.4 = (s32[32,16]{0,1:T(8,128)S(1)}, s32[32,16]{0,1:T(8,128)}, u32[]{:S(2)}) copy-start(s32[32,16]{0,1:T(8,128)} %param.13) | copy-start | bytes 6148
  0.7 26.3 %copy-start.3 = (s32[32,16]{0,1:T(8,128)S(1)}, s32[32,16]{0,1:T(8,128)}, u32[]{:S(2)}) copy-start(s32[32,16]{0,1:T(8,128)} %param.12) | copy-start | bytes 6148
  0.7 26.3 %copy-start.2 = (s32[32,16]{0,1:T(8,128)S(1)}, s32[32,16]{0,1:T(8,128)}, u32[]{:S(2)}) copy-start(s32[32,16]{0,1:T(8,128)} %param.11) | copy-start | bytes 6148
  0.7 26.3 %copy-start = (bf16[4,384,384]{2,1,0:T(8,128)(2,1)S(1)}, bf16[4,384,384]{2,1,0:T(8,128)(2,1)}, u32[]{:S(2)}) copy-start(bf16[4,384,384]{2,1,0:T(8,128)(2,1)} %param.10) | copy-start | bytes 3538948
  1.8 25.2 %collective-permute-start.1 = (bf16[2,180,384]{2,1,0:T(8,128)(2,1)S(1)}, bf16[2,180,384]{2,1,0:T(8,128)(2,1)S(1)}, u32[]{:S(2)}, u32[]{:S(2)}) collective-permute-start(bf16[2,180,384]{2,1,0:T(8,128)(2,1)S(1)} %bitcast.20), channel_id=1, source_target_pairs={{8,0},{16,8},{24,16},{32,24},{40,32},{48,40},{56,48},{64,56},{72,6... | collective-permute-start | bytes 829448 | tf_op jit(solution)/shard_map/ppermute | solution.py:224
  3.1 23.9 %collective-permute-start = (bf16[2,180,384]{2,1,0:T(8,128)(2,1)S(1)}, bf16[2,180,384]{2,1,0:T(8,128)(2,1)S(1)}, u32[]{:S(2)}, u32[]{:S(2)}) collective-permute-start(bf16[2,180,384]{2,1,0:T(8,128)(2,1)S(1)} %bitcast.21), channel_id=1, source_target_pairs={{0,8},{8,16},{16,24},{24,32},{32,40},{40,48},{48,56},{56,64},{64,7... | collective-permute-start | bytes 829448 | tf_op jit(solution)/shard_map/ppermute | solution.py:223
  8.7 18.2 %collective-permute-start.2 = (bf16[2,72,384]{2,1,0:T(8,128)(2,1)S(1)}, bf16[2,72,384]{2,1,0:T(8,128)(2,1)S(1)}, u32[]{:S(2)}, u32[]{:S(2)}) collective-permute-start(bf16[2,72,384]{2,1,0:T(8,128)(2,1)S(1)} %pad_maximum_fusion), channel_id=1, source_target_pairs={{0,7},{1,0},{2,1},{3,2},{4,3},{5,4},{6,5},{7,6},{8,15},{9,8},{10,9... | collective-permute-start | bytes 331784 | tf_op jit(solution)/shard_map/ppermute | solution.py:236
  19.6 6.0 %collective-permute-start.4 = (bf16[2,48,384]{2,1,0:T(8,128)(2,1)S(1)}, bf16[2,48,384]{2,1,0:T(8,128)(2,1)S(1)}, u32[]{:S(2)}, u32[]{:S(2)}) collective-permute-start(bf16[2,48,384]{2,1,0:T(8,128)(2,1)S(1)} %slice.9), channel_id=1, source_target_pairs={{8,7},{9,0},{10,1},{11,2},{12,3},{13,4},{14,5},{15,6},{16,15},{17,... | collective-permute-start | bytes 221192 | tf_op jit(solution)/shard_map/ppermute | solution.py:238
  20.9 6.0 %collective-permute-start.3 = (bf16[2,48,384]{2,1,0:T(8,128)(2,1)S(1)}, bf16[2,48,384]{2,1,0:T(8,128)(2,1)S(1)}, u32[]{:S(2)}, u32[]{:S(2)}) collective-permute-start(bf16[2,48,384]{2,1,0:T(8,128)(2,1)S(1)} %slice.9), channel_id=1, source_target_pairs={{0,15},{1,8},{2,9},{3,10},{4,11},{5,12},{6,13},{7,14},{8,23},{9,16... | collective-permute-start | bytes 221192 | tf_op jit(solution)/shard_map/ppermute | solution.py:237
  31.0 5.9 %collective-permute-start.5 = (bf16[768,384]{1,0:T(8,128)(2,1)S(1)}, bf16[768,384]{1,0:T(8,128)(2,1)S(1)}, u32[]{:S(2)}, u32[]{:S(2)}) collective-permute-start(bf16[768,384]{1,0:T(8,128)(2,1)S(1)} %get-tuple-element.19), channel_id=1, source_target_pairs={{0,128},{128,0},{1,129},{129,1},{2,130},{130,2},{3,131},{131,3},{4... | collective-permute-start | bytes 1769480 | tf_op jit(solution)/shard_map/ppermute | solution.py:243
  72.8 18.6 %all-to-all-start.2 = ((f32[8,24,384]{2,1,0:T(8,128)}), f32[8,24,384]{2,1,0:T(8,128)S(1)}, u32[]{:S(2)}, u32[]{:S(2)}) async-start(f32[8,24,384]{2,1,0:T(8,128)} %shard_map.106), calls=%async_computation.2 | async-start | bytes 589824 | tf_op jit(solution)/shard_map/all_to_all | solution.py:361
  76.2 7.6 %collective-permute-start.7 = (bf16[2,180,384]{2,1,0:T(8,128)(2,1)S(1)}, bf16[2,180,384]{2,1,0:T(8,128)(2,1)S(1)}, u32[]{:S(2)}, u32[]{:S(2)}) collective-permute-start(bf16[2,180,384]{2,1,0:T(8,128)(2,1)S(1)} %get-tuple-element.22.dmixed.own), channel_id=1, source_target_pairs={{8,0},{16,8},{24,16},{32,24},{40,32},{48,40},{56,48},{64,56},{72,6... | collective-permute-start | bytes 829448 | tf_op jit(solution)/shard_map/ppermute | solution.py:224
  77.5 13.9 %collective-permute-start.6 = (bf16[2,180,384]{2,1,0:T(8,128)(2,1)S(1)}, bf16[2,180,384]{2,1,0:T(8,128)(2,1)S(1)}, u32[]{:S(2)}, u32[]{:S(2)}) collective-permute-start(bf16[2,180,384]{2,1,0:T(8,128)(2,1)S(1)} %get-tuple-element.22.dmixed.own), channel_id=1, source_target_pairs={{0,8},{8,16},{16,24},{24,32},{32,40},{40,48},{48,56},{56,64},{64,7... | collective-permute-start | bytes 829448 | tf_op jit(solution)/shard_map/ppermute | solution.py:223
  92.1 11.2 %all-to-all-start.3 = ((bf16[8,24,384]{2,1,0:T(8,128)(2,1)}), bf16[8,24,384]{2,1,0:T(8,128)(2,1)S(1)}, u32[]{:S(2)}, u32[]{:S(2)}) async-start(bf16[8,24,384]{2,1,0:T(8,128)(2,1)} %get-tuple-element.24), calls=%async_computation.3 | async-start | bytes 294912 | tf_op jit(solution)/shard_map/all_to_all | solution.py:361
  95.5 12.8 %collective-permute-start.8 = (bf16[2,168,384]{2,1,0:T(8,128)(2,1)S(1)}, bf16[2,168,384]{2,1,0:T(8,128)(2,1)S(1)}, u32[]{:S(2)}, u32[]{:S(2)}) collective-permute-start(bf16[2,168,384]{2,1,0:T(8,128)(2,1)S(1)} %get-tuple-element.26), channel_id=1, source_target_pairs={{0,1},{1,2},{2,3},{3,4},{4,5},{5,6},{6,7},{7,0},{8,9},{9,10},{10,1... | collective-permute-start | bytes 774152 | tf_op jit(solution)/shard_map/ppermute | solution.py:383
  104.2 11.4 %all-to-all-start.4 = ((bf16[4,192,384]{2,1,0:T(8,128)(2,1)}), bf16[4,192,384]{2,1,0:T(8,128)(2,1)S(1)}, u32[]{:S(2)}, u32[]{:S(2)}) async-start(bf16[4,192,384]{2,1,0:T(8,128)(2,1)} %get-tuple-element.25), calls=%async_computation.4 | async-start | bytes 1179648 | tf_op jit(solution)/shard_map/all_to_all | solution.py:361
  108.3 1.3 %copy-start.1 = (bf16[4,384,384]{2,1,0:T(8,128)(2,1)S(1)}, bf16[4,384,384]{2,1,0:T(8,128)(2,1)}, u32[]{:S(2)}) copy-start(bf16[4,384,384]{2,1,0:T(8,128)(2,1)} %param.10) | copy-start | bytes 3538948
  115.6 7.6 %collective-permute-start.9 = (bf16[768,384]{1,0:T(8,128)(2,1)S(1)}, bf16[768,384]{1,0:T(8,128)(2,1)S(1)}, u32[]{:S(2)}, u32[]{:S(2)}) collective-permute-start(bf16[768,384]{1,0:T(8,128)(2,1)S(1)} %get-tuple-element.32.mine), channel_id=1, source_target_pairs={{0,128},{128,0},{1,129},{129,1},{2,130},{130,2},{3,131},{131,3},{4... | collective-permute-start | bytes 1769480 | tf_op jit(solution)/shard_map/ppermute | solution.py:243
